TPU v7x, 32 devices: a whole 2x2x4 slice. The times are simulated.
32 devices in a mesh: rep: 2 (over y), dev: 16 (over z, x, core).
Axes of the slice: x: 2, y: 2, z: 4, core: 2. Of those that a mesh axis runs over, the one named last changes fastest.
Arguments:
- tokens: bfloat16 [4096, 3584], P(('rep', 'dev')), parts along dimension 0, may hold values from -6 to 6
- norm_gain: float32 [3584], replicated, may hold values from 0.5 to 1.5
- kv_weight: bfloat16 [3584, 576], P('dev'), may hold values from -0.09375 to 0.09375
- key_value_gain: float32 [512], replicated, may hold values from 0.5 to 1.5
- gate_weight: bfloat16 [3584, 4096], P(None, 'dev'), may hold values from -0.09375 to 0.09375
- up_weight: bfloat16 [3584, 4096], P(None, 'dev'), may hold values from -0.09375 to 0.09375
- down_weight: bfloat16 [16384, 896], P('dev'), may hold values from -0.1875 to 0.1875
- expert_index: int32 [4096, 2], P(('rep', 'dev')), parts along dimension 0, may hold values from 0 to 3, all different within a row; in each aligned block of 128 rows (0 to 127, 128 to 255, ...) at most 128 rows name the same one
- route_gate: float32 [4096, 2], P(('rep', 'dev')), parts along dimension 0, may hold values from 0.2 to 1
- owner: int32 [4096, 1], P(('rep', 'dev')), parts along dimension 0, may hold values from 0 to 15; in each aligned block of 128 rows (0 to 127, 128 to 255, ...) at most 16 rows name the same one
Outputs:
- moe_out: bfloat16 [4096, 3584], P(('rep', 'dev')), parts along dimension 0
- latent_cache: bfloat16 [8192, 576], P(('rep', 'dev')), parts along dimension 0
There are 2 independent parts, one for each index of `rep`. A program takes and returns all parts, laid end to end along the dimension named above; an argument that names none is the same for every part. Nothing has to cross between parts.
Inputs may be any that keep to these rules, and one draw needn't show every extreme that they name: `expert_index`: the 2 experts of a token differ. Among the entries of the 128 tokens of one device, no expert is named more than 128 times, and some expert of some device is named exactly 128 times. At most 16 tokens of one device name the same owner, and in some device exactly 16 do.
All inputs are finite; a program needn't handle non-finite values.
Results may differ from a plain program's by a relative error of at most 0.0071.
Values may be sent and summed in bfloat16 or wider, within the bound.
No kernel may reach another device: no remote copies, remote signals or barrier semaphores. Data moves between devices by JAX's collectives and lax.ppermute only.
A program may use at most 128 MiB of HBM per device.

v0:
```python
import jax
import jax.numpy as jnp
from jax import lax
from jax.sharding import PartitionSpec as P

KEY_VALUE_RANK = 512
ROUTES = 2
LOG_GROUP = 2
GROUP = 4


eps = 1e-06
rope_theta = 50000.0


def swapped(value, axis, stride):
    return lax.ppermute(value, axis, [(i, i ^ 1 << stride) for i in range(lax.axis_size(axis))])


def root_mean_scale(values, gain_vector):
    mean_sq = jnp.mean(values * values, axis=-1, keepdims=True)
    return values * lax.rsqrt(mean_sq + eps) * gain_vector


def apply_rotary_keys(key_part, token_positions):
    half_width = key_part.shape[-1] // 2
    frequency = rope_theta ** (
        -jnp.arange(half_width, dtype=jnp.float32) * 2.0 / key_part.shape[-1]
    )
    angles = token_positions.astype(jnp.float32)[:, None] * frequency[None, :]
    cos_part = jnp.cos(angles)
    sin_part = jnp.sin(angles)
    front_half = key_part[:, :half_width]
    back_half = key_part[:, half_width:]
    return jnp.concatenate(
        [
            front_half * cos_part - back_half * sin_part,
            back_half * cos_part + front_half * sin_part,
        ],
        axis=-1,
    )


def block_ranks(labels, label_count):
    onehot = (labels[..., None] == jnp.arange(label_count, dtype=jnp.int32)).astype(jnp.int32)
    before = jnp.cumsum(onehot, axis=1, dtype=jnp.int32) - onehot
    return jnp.sum(before * onehot, axis=-1, dtype=jnp.int32)


def shards(
    tokens,
    norm_gain,
    kv_weight,
    key_value_gain,
    gate_weight,
    up_weight,
    down_weight,
    expert_index,
    route_gate,
    owner,
):
    device_count = lax.axis_size("dev")
    experts_count = device_count // GROUP
    tok_rows = tokens.shape[0]
    features = tokens.shape[1]
    capacity = 2 * tok_rows * ROUTES // experts_count
    push_cap = max(2, 2 * tok_rows // device_count)
    own_index = lax.axis_index("dev")
    normed = root_mean_scale(tokens.astype(jnp.float32), norm_gain).astype(jnp.bfloat16)
    flat_experts = expert_index.reshape(1, tok_rows * ROUTES)
    slot_index = block_ranks(flat_experts, experts_count)[0]
    expert_of = flat_experts[0]
    token_of = jnp.arange(tok_rows * ROUTES, dtype=jnp.int32) // ROUTES
    position = expert_of * capacity + slot_index
    packed = (
        jnp.zeros((experts_count * capacity, features), jnp.bfloat16)
        .at[position]
        .set(normed[token_of])
    )
    copies = jnp.broadcast_to(
        packed.reshape(experts_count, 1, capacity, features),
        (experts_count, GROUP, capacity, features),
    )
    received = lax.all_to_all(
        copies.reshape(device_count * capacity, features),
        "dev",
        split_axis=0,
        concat_axis=0,
        tiled=True,
    )
    gate_part = jnp.dot(received, gate_weight, preferred_element_type=jnp.float32)
    up_part = jnp.dot(received, up_weight, preferred_element_type=jnp.float32)
    hidden = (jax.nn.silu(gate_part) * up_part).astype(jnp.bfloat16)
    for bit_number in range(LOG_GROUP):
        partner = swapped(hidden, "dev", bit_number)
        upper_half = own_index >> bit_number & 1 == 1
        hidden = jnp.where(
            upper_half,
            jnp.concatenate([partner, hidden], axis=1),
            jnp.concatenate([hidden, partner], axis=1),
        )
    outputs = jnp.dot(hidden, down_weight, preferred_element_type=jnp.float32).astype(jnp.bfloat16)
    returned = lax.all_to_all(
        outputs.reshape(device_count, capacity, outputs.shape[1]),
        "dev",
        split_axis=0,
        concat_axis=2,
        tiled=True,
    )
    result = returned.reshape(capacity, experts_count, features)
    picked = result[slot_index, expert_of]
    weighted = route_gate.reshape(tok_rows * ROUTES, 1) * picked.astype(jnp.float32)
    combined = jnp.sum(weighted.reshape(tok_rows, ROUTES, features), axis=1)
    moe_out = combined.astype(jnp.bfloat16)
    unnormed_latent = jnp.dot(
        normed,
        lax.all_gather(kv_weight, "dev", axis=0, tiled=True),
        preferred_element_type=jnp.float32,
    )
    token_positions = jnp.arange(tok_rows, dtype=jnp.int32)
    latent_vector = jnp.concatenate(
        [
            root_mean_scale(unnormed_latent[:, :KEY_VALUE_RANK], key_value_gain),
            apply_rotary_keys(unnormed_latent[:, KEY_VALUE_RANK:], token_positions),
        ],
        axis=-1,
    ).astype(jnp.bfloat16)
    target = owner[:, 0]
    rank_index = block_ranks(target[None, :], device_count)[0]
    send_rows = (
        jnp.zeros((device_count * push_cap, latent_vector.shape[1]), jnp.bfloat16)
        .at[target * push_cap + rank_index]
        .set(latent_vector)
    )
    latent_cache = lax.all_to_all(send_rows, "dev", split_axis=0, concat_axis=0, tiled=True)
    return (moe_out, latent_cache)


def solution(mesh):
    in_specs = (
        P(("rep", "dev"), None),
        P(),
        P("dev", None),
        P(),
        P(None, "dev"),
        P(None, "dev"),
        P("dev", None),
        P(("rep", "dev"), None),
        P(("rep", "dev"), None),
        P(("rep", "dev"), None),
    )
    out_specs = (P(("rep", "dev"), None), P(("rep", "dev"), None))
    return jax.shard_map(shards, mesh=mesh, in_specs=in_specs, out_specs=out_specs, check_vma=False)
```

profile of v0, /device:TPU:15, one launch (start us, length us, event | category | flops | bytes accessed | tf_op | source)
XLA Modules:
  0.0 600.3 jit_solution(8977429240098421660)
XLA Ops:
  7.2 0.0 copy-start
  7.2 0.9 copy.17
  8.1 0.1 eq.62
  8.3 0.1 squeeze_reshape.3
  8.4 1.2 reduce-window.6
  9.6 0.1 slice.27
  9.7 1.4 fusion.9
  11.2 0.1 copy.19
  11.3 0.1 copy.20
  11.4 0.1 broadcast.258
  11.6 1.5 fusion.11
  13.0 10.8 %scatter_custom_fusion = bf16[512,3584]{1,0:T(8,128)(2,1)} fusion(s32[256]{0:T(256)S(1)} %bitcast.48, bf16[128,3584]{1,0:T(8,128)(2,1)S(1)} %fusion.11, s32[1024]{0:T(1024)S(1)} %pad_clamp_fusion, bf16[]{:T(256)} %constant.29.clone.1), kind=kCustom, calls=%fused_computation.22 | custom fusion | bytes 3670018 | tf_op jit(solution)/shard_map/scatter | solution.py:78
  23.9 6.6 %broadcast_in_dim.10 = bf16[4,4,128,3584]{3,2,1,0:T(8,128)(2,1)} broadcast(bf16[4,128,3584]{2,1,0:T(8,128)(2,1)} %bitcast.40), dimensions={0,2,3} | broadcast | bytes 18350080 | tf_op jit(solution)/shard_map/broadcast_in_dim | solution.py:80
  30.5 6.6 %all-to-all-start = ((bf16[16,128,3584]{2,1,0:T(8,128)(2,1)}), bf16[16,128,3584]{2,1,0:T(8,128)(2,1)}, u32[]{:S(2)}, u32[]{:S(2)}) async-start(bf16[16,128,3584]{2,1,0:T(8,128)(2,1)} %bitcast.38), calls=%async_computation | async-start | bytes 29360128 | tf_op jit(solution)/shard_map/all_to_all | solution.py:84
  37.0 0.3 all-gather.2.cloned.1.call-start
  37.3 0.4 all-gather.2.cloned.1.call-update
  37.8 344.1 %all-to-all-done = bf16[16,128,3584]{2,1,0:T(8,128)(2,1)} async-done(((bf16[16,128,3584]{2,1,0:T(8,128)(2,1)}), bf16[16,128,3584]{2,1,0:T(8,128)(2,1)}, u32[]{:S(2)}, u32[]{:S(2)}) %all-to-all-start) | async-done | bytes 14680096 | tf_op jit(solution)/shard_map/all_to_all | solution.py:84
  381.9 11.0 %fusion.35 = f32[2048,256]{0,1:T(8,128)} fusion(bf16[2048,3584]{1,0:T(8,128)(2,1)} %bitcast.9, bf16[3584,256]{1,0:T(8,128)(2,1)} %param.14), kind=kOutput, calls=%fused_computation.71 | convolution fusion | flops 3758096384 | bytes 18612224 | tf_op jit(solution)/shard_map/dot_general | solution.py:91
  392.9 11.5 %fusion.8 = bf16[2048,256]{0,1:T(8,128)(2,1)} fusion(bf16[2048,3584]{1,0:T(8,128)(2,1)} %bitcast.9, bf16[3584,256]{1,0:T(8,128)(2,1)} %param.15, f32[2048,256]{0,1:T(8,128)} %fusion.35), kind=kOutput, calls=%fused_computation.15 | convolution fusion | flops 3761242112 | bytes 19660800 | tf_op jit(solution)/shard_map/dot_general | solution.py:92
  404.4 0.2 collective-permute-start
  404.6 0.0 copy-start.2
  404.6 2.8 collective-permute-done
  407.4 4.8 maximum_select_fusion.4
  412.3 0.0 collective-permute-start.1
  412.3 0.0 copy-done.2
  412.3 0.1 fusion.17
  412.3 0.2 reduce_window_sum.32
  412.5 0.2 select_reduce_fusion
  412.7 0.0 copy-start.1
  412.7 0.0 all-gather.2.cloned.1.call-done
  412.8 4.1 fusion.36
  416.9 0.1 multiply_reduce_fusion.1
  417.0 0.1 fusion.23
  417.2 0.0 copy-done.1
  417.2 0.1 multiply_convert_fusion
  417.3 0.2 copy.22
  417.5 1.8 scatter_custom_fusion.1
  419.3 15.3 %all-to-all-start.2 = ((bf16[16,16,576]{2,1,0:T(8,128)(2,1)}), bf16[16,16,576]{2,1,0:T(8,128)(2,1)S(1)}, u32[]{:S(2)}, u32[]{:S(2)}) async-start(bf16[16,16,576]{2,1,0:T(8,128)(2,1)} %bitcast.17), calls=%async_computation.2 | async-start | bytes 655360 | tf_op jit(solution)/shard_map/all_to_all | solution.py:135
  434.6 27.6 %collective-permute-done.1 = bf16[2048,512]{0,1:T(8,128)(2,1)} collective-permute-done((bf16[2048,512]{0,1:T(8,128)(2,1)}, bf16[2048,512]{0,1:T(8,128)(2,1)}, u32[]{:S(2)}, u32[]{:S(2)}) %collective-permute-start.1) | collective-permute-done | bytes 2097184 | tf_op jit(solution)/shard_map/ppermute | solution.py:17
  462.2 0.0 copy-done
  462.2 10.0 %fusion.7 = bf16[2048,896]{1,0:T(8,128)(2,1)} fusion(bf16[1024,896]{1,0:T(8,128)(2,1)S(1)} %copy-done, bf16[2048,512]{0,1:T(8,128)(2,1)} %maximum_select_fusion.4, bf16[2048,512]{0,1:T(8,128)(2,1)} %collective-permute-done.1, pred[]{:T(512)S(6)} %eq.60), kind=kOutput, calls=%fused_computation.13 | convolution fusion | flops 3778805760 | bytes 9699329 | tf_op jit(solution)/shard_map/dot_general | solution.py:102
  472.2 0.0 all-to-all-done.2
  472.2 0.0 copy-start.3
  472.2 6.2 %all-to-all-start.1 = ((bf16[16,128,896]{2,1,0:T(8,128)(2,1)}), bf16[16,128,896]{2,1,0:T(8,128)(2,1)}, u32[]{:S(2)}, u32[]{:S(2)}) async-start(bf16[16,128,896]{2,1,0:T(8,128)(2,1)} %bitcast.41), calls=%async_computation.1 | async-start | bytes 7340032 | tf_op jit(solution)/shard_map/all_to_all | solution.py:103
  478.4 0.0 copy-done.3
  478.4 0.1 copy.16
  478.5 0.9 copy.23
  479.4 80.2 %all-to-all-done.1 = bf16[16,128,896]{2,1,0:T(8,128)(2,1)} async-done(((bf16[16,128,896]{2,1,0:T(8,128)(2,1)}), bf16[16,128,896]{2,1,0:T(8,128)(2,1)}, u32[]{:S(2)}, u32[]{:S(2)}) %all-to-all-start.1) | async-done | bytes 3670048 | tf_op jit(solution)/shard_map/all_to_all | solution.py:103
  559.6 5.9 copy.21
  565.5 7.3 %reshape.385 = bf16[128,4,3584]{2,1,0:T(4,128)(2,1)} reshape(bf16[1,128,16,896]{3,2,1,0:T(8,128)(2,1)} %copy.21) | data formatting | bytes 7340032 | tf_op jit(solution)/shard_map/reshape | solution.py:110
  572.9 6.7 %gather_fusion = bf16[256,3584]{1,0:T(8,128)(2,1)} fusion(bf16[128,4,3584]{2,1,0:T(4,128)(2,1)} %reshape.385, s32[256]{0:T(256)S(1)} %bitcast.39), kind=kCustom, calls=%fused_computation.1 | custom fusion | bytes 3672064 | tf_op jit(solution)/shard_map/gather | solution.py:111
  579.6 5.4 reshape.386
  585.0 8.2 %multiply_reduce_fusion = bf16[128,3584]{1,0:T(8,128)(2,1)} fusion(f32[128,2,3584]{2,1,0:T(2,128)} %reshape.386, f32[128,2]{1,0:T(8,128)S(1)} %copy.16), kind=kLoop, calls=%fused_computation.12 | loop fusion | flops 1376256 | bytes 4588544 | tf_op jit(solution)/shard_map/reduce_sum | solution.py:113
  (16 shorter events, 0.2 us)
Async XLA Ops:
  7.2 455.1 %copy-start = (bf16[1024,896]{1,0:T(8,128)(2,1)S(1)}, bf16[1024,896]{1,0:T(8,128)(2,1)}, u32[]{:S(2)}) copy-start(bf16[1024,896]{1,0:T(8,128)(2,1)} %param.16) | copy-start | bytes 5505028
  30.5 351.4 %all-to-all-start = ((bf16[16,128,3584]{2,1,0:T(8,128)(2,1)}), bf16[16,128,3584]{2,1,0:T(8,128)(2,1)}, u32[]{:S(2)}, u32[]{:S(2)}) async-start(bf16[16,128,3584]{2,1,0:T(8,128)(2,1)} %bitcast.38), calls=%async_computation | async-start | bytes 29360128 | tf_op jit(solution)/shard_map/all_to_all | solution.py:84
  37.0 375.7 %all-gather.2.cloned.1.call-start = ((), (), s32[]{:S(2)}) async-start(), calls=%async_computation.3 | async-start | bytes 4874240 | tf_op jit(solution)/shard_map/all_gather | solution.py:117
  404.4 3.0 collective-permute-start
  404.6 7.6 %copy-start.2 = (s32[128,1]{0,1:T(1,128)S(1)}, s32[128,1]{0,1:T(1,128)}, u32[]{:S(2)}) copy-start(s32[128,1]{0,1:T(1,128)} %param.19) | copy-start | bytes 1540
  412.3 50.0 %collective-permute-start.1 = (bf16[2048,512]{0,1:T(8,128)(2,1)}, bf16[2048,512]{0,1:T(8,128)(2,1)}, u32[]{:S(2)}, u32[]{:S(2)}) collective-permute-start(bf16[2048,512]{0,1:T(8,128)(2,1)} %maximum_select_fusion.4), channel_id=1, source_target_pairs={{0,2},{1,3},{2,0},{3,1},{4,6},{5,7},{6,4},{7,5},{8,10},{9,11},{10,... | collective-permute-start | bytes 6291464 | tf_op jit(solution)/shard_map/ppermute | solution.py:17
  412.7 4.4 copy-start.1
  419.3 52.9 %all-to-all-start.2 = ((bf16[16,16,576]{2,1,0:T(8,128)(2,1)}), bf16[16,16,576]{2,1,0:T(8,128)(2,1)S(1)}, u32[]{:S(2)}, u32[]{:S(2)}) async-start(bf16[16,16,576]{2,1,0:T(8,128)(2,1)} %bitcast.17), calls=%async_computation.2 | async-start | bytes 655360 | tf_op jit(solution)/shard_map/all_to_all | solution.py:135
  472.2 6.2 %copy-start.3 = (f32[128,2]{0,1:T(2,128)S(1)}, f32[128,2]{0,1:T(2,128)}, u32[]{:S(2)}) copy-start(f32[128,2]{0,1:T(2,128)} %param.18) | copy-start | bytes 3076
  472.2 87.4 %all-to-all-start.1 = ((bf16[16,128,896]{2,1,0:T(8,128)(2,1)}), bf16[16,128,896]{2,1,0:T(8,128)(2,1)}, u32[]{:S(2)}, u32[]{:S(2)}) async-start(bf16[16,128,896]{2,1,0:T(8,128)(2,1)} %bitcast.41), calls=%async_computation.1 | async-start | bytes 7340032 | tf_op jit(solution)/shard_map/all_to_all | solution.py:103
Sparse Core Ops, SparseCore 0:
  40.2 217.5 all-gather.1
where the time goes:
time: 610 us; the launch traced here: 600 us
  waiting for transfers between devices  455 us (75%)
  local copies, waits for them, and re-layouts  47.4 us (8%)
  matrix products  36.6 us (6%)
  starting transfers between devices  28.5 us (5%)
  other arithmetic  18.1 us (3%)
  between operations  14.4 us (2%)
    all_to_all x1, waiting for transfers between devices, shards(): lax.all_to_all(copies.reshape(device_count * capacity, features), 'dev',...  344 us
    all_to_all x1, waiting for transfers between devices, shards(): lax.all_to_all(outputs.reshape(device_count, capacity, outputs.shape[1]),...  80.2 us
    ppermute x2, waiting for transfers between devices, swapped(): lax.ppermute(value, axis, [(i, i ^ 1 << stride) for i in range(lax.axis_s...  30.4 us
    all_to_all x1, starting transfers between devices, shards(): lax.all_to_all(send_rows, 'dev', split_axis=0, concat_axis=0, tiled=True)  15.3 us
  transfers between devices with their start and end apart: 6, of which 4 were waited for; matrix products, arithmetic and copies ran while one was open for 8% of the time, Pallas kernels for 0%

commit v1 on v0

--- a/solution.py
+++ b/solution.py
@@ -1,12 +1,17 @@
+import functools
+
 import jax
 import jax.numpy as jnp
 from jax import lax
+from jax.experimental import pallas as pl
+from jax.experimental.pallas import tpu as pltpu
 from jax.sharding import PartitionSpec as P
 
 KEY_VALUE_RANK = 512
 ROUTES = 2
 LOG_GROUP = 2
 GROUP = 4
+LINE = 4
 
 
 eps = 1e-06
@@ -47,7 +52,28 @@
     return jnp.sum(before * onehot, axis=-1, dtype=jnp.int32)
 
 
-def shards(
+def latent_rows(raw_latent, key_value_gain):
+    token_positions = jnp.arange(raw_latent.shape[0], dtype=jnp.int32)
+    return jnp.concatenate(
+        [
+            root_mean_scale(raw_latent[:, :KEY_VALUE_RANK], key_value_gain),
+            apply_rotary_keys(raw_latent[:, KEY_VALUE_RANK:], token_positions),
+        ],
+        axis=-1,
+    ).astype(jnp.bfloat16)
+
+
+def cache_send_rows(latent_vector, owner, device_count, push_cap):
+    target = owner[:, 0]
+    rank_index = block_ranks(target[None, :], device_count)[0]
+    return (
+        jnp.zeros((device_count * push_cap, latent_vector.shape[1]), jnp.bfloat16)
+        .at[target * push_cap + rank_index]
+        .set(latent_vector)
+    )
+
+
+def packed_shards(
     tokens,
     norm_gain,
     kv_weight,
@@ -112,25 +138,311 @@
     weighted = route_gate.reshape(tok_rows * ROUTES, 1) * picked.astype(jnp.float32)
     combined = jnp.sum(weighted.reshape(tok_rows, ROUTES, features), axis=1)
     moe_out = combined.astype(jnp.bfloat16)
-    unnormed_latent = jnp.dot(
+    raw_latent = jnp.dot(
         normed,
         lax.all_gather(kv_weight, "dev", axis=0, tiled=True),
         preferred_element_type=jnp.float32,
     )
-    token_positions = jnp.arange(tok_rows, dtype=jnp.int32)
-    latent_vector = jnp.concatenate(
-        [
-            root_mean_scale(unnormed_latent[:, :KEY_VALUE_RANK], key_value_gain),
-            apply_rotary_keys(unnormed_latent[:, KEY_VALUE_RANK:], token_positions),
+    send_rows = cache_send_rows(
+        latent_rows(raw_latent, key_value_gain), owner, device_count, push_cap
+    )
+    latent_cache = lax.all_to_all(send_rows, "dev", split_axis=0, concat_axis=0, tiled=True)
+    return (moe_out, latent_cache)
+
+
+def hidden_kernel(
+    place_ref,
+    own_ref, a_ref, b_ref, c_ref, d_ref, e_ref,
+    g0_ref, g1_ref, g2m_ref, g2o_ref, g3m_ref, g3o_ref,
+    u0_ref, u1_ref, u2m_ref, u2o_ref, u3m_ref, u3o_ref,
+    hidden_ref,
+    rows_buf, gate_buf, up_buf, row_sems, gate_sems, up_sems,
+):
+    place, rep, is_end = place_ref[0], place_ref[1], place_ref[2]
+    half = rows_buf.shape[2] // 2
+    own_copy = pltpu.make_async_copy(own_ref, rows_buf.at[0], row_sems.at[0])
+    a_copy = pltpu.make_async_copy(a_ref, rows_buf.at[1], row_sems.at[1])
+    own_copy.start()
+    a_copy.start()
+
+    @pl.when(is_end == 1)
+    def _():
+        pltpu.make_async_copy(c_ref, rows_buf.at[2], row_sems.at[2]).start()
+        pltpu.make_async_copy(e_ref, rows_buf.at[3], row_sems.at[3]).start()
+
+    @pl.when(is_end == 0)
+    def _():
+        pltpu.make_async_copy(d_ref, rows_buf.at[2], row_sems.at[2]).start()
+        pltpu.make_async_copy(b_ref, rows_buf.at[3], row_sems.at[3]).start()
+
+    def fetch(refs, buf, sems):
+        whole0, whole1, mine2, other2, mine3, other3 = refs
+        at_mine, at_other = pl.ds(rep * half, half), pl.ds((1 - rep) * half, half)
+        copies = [
+            [pltpu.make_async_copy(whole0, buf.at[place], sems.at[0])],
+            [pltpu.make_async_copy(whole1, buf.at[place ^ 1], sems.at[1])],
+            [
+                pltpu.make_async_copy(mine2, buf.at[place ^ 2, at_mine], sems.at[2]),
+                pltpu.make_async_copy(other2, buf.at[place ^ 2, at_other], sems.at[3]),
+            ],
+            [
+                pltpu.make_async_copy(mine3, buf.at[place ^ 3, at_mine], sems.at[4]),
+                pltpu.make_async_copy(other3, buf.at[place ^ 3, at_other], sems.at[5]),
+            ],
+        ]
+        return copies
+
+    gates = fetch((g0_ref, g1_ref, g2m_ref, g2o_ref, g3m_ref, g3o_ref), gate_buf, gate_sems)
+    ups = fetch((u0_ref, u1_ref, u2m_ref, u2o_ref, u3m_ref, u3o_ref), up_buf, up_sems)
+    for k in range(GROUP):
+        for copy in gates[k] + ups[k]:
+            copy.start()
+    own_copy.wait()
+    a_copy.wait()
+
+    @pl.when(is_end == 1)
+    def _():
+        pltpu.make_async_copy(c_ref, rows_buf.at[2], row_sems.at[2]).wait()
+        pltpu.make_async_copy(e_ref, rows_buf.at[3], row_sems.at[3]).wait()
+
+    @pl.when(is_end == 0)
+    def _():
+        pltpu.make_async_copy(d_ref, rows_buf.at[2], row_sems.at[2]).wait()
+        pltpu.make_async_copy(b_ref, rows_buf.at[3], row_sems.at[3]).wait()
+
+    units = gate_buf.shape[2]
+    tok_rows, features = rows_buf.shape[1:]
+    for k in range(GROUP):
+        for copy in gates[k] + ups[k]:
+            copy.wait()
+        slot = place ^ k
+        at_units = pl.ds(pl.multiple_of(slot * units, units), units)
+
+        @pl.loop(0, LINE // 2)
+        def _(pair):
+            rows = rows_buf[pl.ds(2 * pair, 2)].reshape(2 * tok_rows, features)
+            gate_part = jnp.dot(rows, gate_buf[slot], preferred_element_type=jnp.float32)
+            up_part = jnp.dot(rows, up_buf[slot], preferred_element_type=jnp.float32)
+            part = (gate_part / (1.0 + jnp.exp(-gate_part)) * up_part).astype(jnp.bfloat16)
+            hidden_ref[pl.ds(2 * pair, 2), :, at_units] = part.reshape(2, tok_rows, units)
+
+
+def hidden_units(place, rows, gates, ups):
+    tok_rows, features = rows[0].shape
+    units = gates[0].shape[1]
+    any_space = pl.BlockSpec(memory_space=pl.ANY)
+    weight_bytes = 2 * GROUP * features * units * 2
+    return pl.pallas_call(
+        hidden_kernel,
+        out_shape=jax.ShapeDtypeStruct((LINE, tok_rows, GROUP * units), jnp.bfloat16),
+        in_specs=[pl.BlockSpec(memory_space=pltpu.SMEM)] + [any_space] * 18,
+        out_specs=pl.BlockSpec(memory_space=pltpu.VMEM),
+        scratch_shapes=[
+            pltpu.VMEM((LINE, tok_rows, features), jnp.bfloat16),
+            pltpu.VMEM((GROUP, features, units), jnp.bfloat16),
+            pltpu.VMEM((GROUP, features, units), jnp.bfloat16),
+            pltpu.SemaphoreType.DMA((LINE,)),
+            pltpu.SemaphoreType.DMA((6,)),
+            pltpu.SemaphoreType.DMA((6,)),
         ],
-        axis=-1,
-    ).astype(jnp.bfloat16)
-    target = owner[:, 0]
-    rank_index = block_ranks(target[None, :], device_count)[0]
-    send_rows = (
-        jnp.zeros((device_count * push_cap, latent_vector.shape[1]), jnp.bfloat16)
-        .at[target * push_cap + rank_index]
-        .set(latent_vector)
+        compiler_params=pltpu.CompilerParams(vmem_limit_bytes=48 * 1024 * 1024),
+        cost_estimate=pl.CostEstimate(
+            flops=4 * LINE * tok_rows * features * GROUP * units,
+            bytes_accessed=weight_bytes + LINE * tok_rows * features * 2,
+            transcendentals=LINE * tok_rows * GROUP * units,
+        ),
+        name="hidden_units",
+    )(place, *rows, *gates, *ups)
+
+
+def down_kernel(parts, place_ref, hidden_ref, scale_ref, *refs):
+    down_refs = refs[:parts]
+    out_refs = refs[parts : parts + LINE]
+    down_buf, sems = refs[parts + LINE :]
+    core, rep = place_ref[0] & 1, place_ref[1]
+    if parts == 2:
+        copies = [
+            pltpu.make_async_copy(down_refs[0], down_buf.at[core], sems.at[0]),
+            pltpu.make_async_copy(down_refs[1], down_buf.at[1 - core], sems.at[1]),
+        ]
+    else:
+        half = down_buf.shape[1] // 2
+        at_mine, at_other = pl.ds(rep * half, half), pl.ds((1 - rep) * half, half)
+        copies = [
+            pltpu.make_async_copy(down_refs[0], down_buf.at[core, at_mine], sems.at[0]),
+            pltpu.make_async_copy(down_refs[1], down_buf.at[core, at_other], sems.at[1]),
+            pltpu.make_async_copy(down_refs[2], down_buf.at[1 - core, at_mine], sems.at[2]),
+            pltpu.make_async_copy(down_refs[3], down_buf.at[1 - core, at_other], sems.at[3]),
+        ]
+    for copy in copies:
+        copy.start()
+    for copy in copies:
+        copy.wait()
+    columns = down_buf.shape[2]
+    for k in reversed(range(LINE)):
+        for column_block in range(2):
+            out = jnp.dot(hidden_ref[k], down_buf[column_block], preferred_element_type=jnp.float32)
+            out = out.astype(jnp.bfloat16).astype(jnp.float32) * scale_ref[k]
+            out_refs[k][:, column_block * columns : (column_block + 1) * columns] = out.astype(
+                jnp.bfloat16
+            )
+
+
+def down_products(place, hidden, scale, downs):
+    tok_rows, depth = hidden.shape[1:]
+    columns = downs[0].shape[1]
+    any_space = pl.BlockSpec(memory_space=pl.ANY)
+    vmem = pl.BlockSpec(memory_space=pltpu.VMEM)
+    return pl.pallas_call(
+        functools.partial(down_kernel, len(downs)),
+        out_shape=[jax.ShapeDtypeStruct((tok_rows, 2 * columns), jnp.bfloat16)] * LINE,
+        in_specs=[pl.BlockSpec(memory_space=pltpu.SMEM), vmem, vmem] + [any_space] * len(downs),
+        out_specs=[vmem] * LINE,
+        scratch_shapes=[
+            pltpu.VMEM((2, depth, columns), jnp.bfloat16),
+            pltpu.SemaphoreType.DMA((len(downs),)),
+        ],
+        compiler_params=pltpu.CompilerParams(vmem_limit_bytes=40 * 1024 * 1024),
+        cost_estimate=pl.CostEstimate(
+            flops=4 * LINE * tok_rows * depth * columns,
+            bytes_accessed=4 * depth * columns + 4 * LINE * tok_rows * columns,
+            transcendentals=0,
+        ),
+        name="down_products",
+    )(place, hidden, scale, *downs)
+
+
+def dense_shards(
+    tokens,
+    norm_gain,
+    kv_weight,
+    key_value_gain,
+    gate_weight,
+    up_weight,
+    down_weight,
+    expert_index,
+    route_gate,
+    owner,
+):
+    device_count = lax.axis_size("dev")
+    tok_rows, features = tokens.shape
+    push_cap = max(2, 2 * tok_rows // device_count)
+    own_index = lax.axis_index("dev")
+    rep = lax.axis_index("rep")
+    plane, place = own_index // GROUP, own_index % GROUP
+    is_end = (plane == 0) | (plane == LINE - 1)
+    place_info = jnp.stack([place, rep, is_end.astype(jnp.int32)]).astype(jnp.int32)
+
+    def along(value, pairs):
+        return lax.ppermute(value, "dev", pairs)
+
+    def across_line(value, k):
+        return along(value, [(i, i ^ GROUP * k) for i in range(device_count)])
+
+    def outer(value):
+        return across_line(value, 1)
+
+    def inner(value):
+        middle = [(i, i ^ GROUP * 3) for i in range(GROUP, 3 * GROUP)]
+        ends = [(i, i) for i in range(device_count) if not GROUP <= i < 3 * GROUP]
+        return along(value, middle + ends)
+
+    def other_core(value):
+        return along(value, [(i, i ^ 1) for i in range(device_count)])
+
+    def other_chip(value):
+        return along(value, [(i, i ^ 2) for i in range(device_count)])
+
+    def other_rep(value):
+        return lax.ppermute(value, "rep", [(0, 1), (1, 0)])
+
+    def whole_expert(weight):
+        half = weight.shape[0] // 2
+        mine = other_chip(lax.dynamic_slice_in_dim(weight, rep * half, half, 0))
+        other = other_rep(mine)
+        return weight, other_core(weight), mine, other, other_core(mine), other_core(other)
+
+    normed = root_mean_scale(tokens.astype(jnp.float32), norm_gain).astype(jnp.bfloat16)
+    a = outer(normed)
+    b = inner(normed)
+    gates = whole_expert(gate_weight)
+    ups = whole_expert(up_weight)
+    downs = whole_expert(down_weight)
+    c = outer(b)
+    d = inner(a)
+    e = outer(d)
+
+    expert_weight = jnp.sum(
+        jnp.where(
+            expert_index[:, :, None] == jnp.arange(LINE, dtype=jnp.int32), route_gate[:, :, None], 0.0
+        ),
+        axis=1,
+    )
+
+    def weight_in(expert):
+        return lax.dynamic_slice_in_dim(expert_weight, expert, 1, 1)
+
+    scale = jnp.stack(
+        [weight_in(plane)] + [across_line(weight_in(plane ^ k), k) for k in range(1, LINE)]
+    )
+
+    kv_pair = other_core(kv_weight)
+    kv_pair = jnp.where(
+        place & 1 == 1,
+        jnp.concatenate([kv_pair, kv_weight]),
+        jnp.concatenate([kv_weight, kv_pair]),
+    )
+    kv_far = other_chip(kv_pair)
+    kv_plane = jnp.where(
+        place & 2 == 2, jnp.concatenate([kv_far, kv_pair]), jnp.concatenate([kv_pair, kv_far])
+    )
+    depth = kv_plane.shape[0]
+
+    def plane_features(rows):
+        return lax.dynamic_slice_in_dim(rows, plane * depth, depth, 1)
+
+    def latent_part(rows):
+        return jnp.dot(rows, kv_plane, preferred_element_type=jnp.float32)
+
+    line_rows = [
+        plane_features(normed),
+        plane_features(a),
+        jnp.where(is_end, plane_features(c), plane_features(d)),
+        jnp.where(is_end, plane_features(e), plane_features(b)),
+    ]
+    latent_parts = latent_part(jnp.concatenate(line_rows)).reshape(LINE, tok_rows, -1)
+    raw_latent = latent_parts[0] + sum(
+        across_line(latent_parts[k].astype(jnp.bfloat16), k).astype(jnp.float32)
+        for k in range(1, LINE)
+    )
+
+    hidden = hidden_units(place_info, (normed, a, b, c, d, e), gates, ups)
+
+    def returned(downs):
+        parts = down_products(place_info, hidden, scale, downs)
+        wide = [part.astype(jnp.float32) for part in parts]
+
+        def narrow(value):
+            return value.astype(jnp.bfloat16)
+
+        from_end = outer(parts[3])
+        back_d = inner(narrow(wide[2] + from_end.astype(jnp.float32)))
+        back_c = outer(parts[2])
+        back_b = inner(narrow(wide[3] + back_c.astype(jnp.float32)))
+        back_a = outer(narrow(wide[1] + jnp.where(is_end, 0.0, back_d.astype(jnp.float32))))
+        return narrow(
+            wide[0] + back_a.astype(jnp.float32) + jnp.where(is_end, 0.0, back_b.astype(jnp.float32))
+        )
+
+    near = returned(downs[:2])
+    far = returned(downs[2:])
+    moe_out = jnp.where(
+        place & 2 == 2,
+        jnp.concatenate([far, near], axis=1),
+        jnp.concatenate([near, far], axis=1),
+    )
+    send_rows = cache_send_rows(
+        latent_rows(raw_latent, key_value_gain), owner, device_count, push_cap
     )
     latent_cache = lax.all_to_all(send_rows, "dev", split_axis=0, concat_axis=0, tiled=True)
     return (moe_out, latent_cache)
@@ -150,4 +462,6 @@
         P(("rep", "dev"), None),
     )
     out_specs = (P(("rep", "dev"), None), P(("rep", "dev"), None))
+    dense = mesh.shape["dev"] == LINE * GROUP and mesh.shape["rep"] == 2
+    shards = dense_shards if dense else packed_shards
     return jax.shard_map(shards, mesh=mesh, in_specs=in_specs, out_specs=out_specs, check_vma=False)

time: 610 us -> 280 us (0.46)
  the two profiles are of different devices: /device:TPU:15 before, /device:TPU:0 now
where the time goes in v1:
time: 280 us; the launch traced here: 278 us
  waiting for transfers between devices  132 us (47%)
  starting transfers between devices  88.7 us (32%)
  Pallas kernels  25.4 us (9%)
  other arithmetic  19.3 us (7%)
  local copies, waits for them, and re-layouts  11.5 us (4%)
    ppermute x35, waiting for transfers between devices, along(): return lax.ppermute(value, 'dev', pairs)  81.9 us
    ppermute x35, starting transfers between devices, along(): return lax.ppermute(value, 'dev', pairs)  81.4 us
    ppermute x3, waiting for transfers between devices, other_rep(): return lax.ppermute(value, 'rep', [(0, 1), (1, 0)])  49.8 us
    pallas_call x1, Pallas kernels, hidden_units(): pl.pallas_call(hidden_kernel, out_shape=jax.ShapeDtypeStruct((LINE, tok_r...  15.6 us
    convert_element_type x8, other arithmetic, narrow(): return value.astype(jnp.bfloat16)  10.9 us
    pallas_call x2, Pallas kernels, down_products(): pl.pallas_call(functools.partial(down_kernel, len(downs)), out_shape=[jax...  9.84 us
  transfers between devices with their start and end apart: 39, of which 11 were waited for; matrix products, arithmetic and copies ran while one was open for 9% of the time, Pallas kernels for 9%

profile of v1, /device:TPU:0, one launch (start us, length us, event | category | flops | bytes accessed | tf_op | source)
XLA Modules:
  0.0 278.3 jit_solution(11398180502317980032)
XLA Ops:
  0.7 1.5 fusion
  2.2 1.5 fusion.2.own_ref
  3.6 3.1 %collective-permute-start = (bf16[128,3584]{1,0:T(8,128)(2,1)S(1)}, bf16[128,3584]{1,0:T(8,128)(2,1)}, u32[]{:S(2)}, u32[]{:S(2)}) collective-permute-start(bf16[128,3584]{1,0:T(8,128)(2,1)S(1)} %fusion.2.own_ref), channel_id=1, source_target_pairs={{0,4},{1,5},{2,6},{3,7},{4,0},{5,1},{6,2},{7,3},{8,12},{9,13},{10,... | collective-permute-start | bytes 2752520 | tf_op jit(solution)/shard_map/ppermute | solution.py:337
  6.8 2.5 collective-permute-start.17
  9.5 1.7 collective-permute-start.15
  11.2 2.3 constant_dynamic-slice_fusion.8
  13.5 2.2 constant_dynamic-slice_fusion.7
  15.7 13.5 %collective-permute-done.17 = f32[128,1]{0,1:T(1,128)S(1)} collective-permute-done((f32[128,1]{0,1:T(1,128)S(1)}, f32[128,1]{0,1:T(1,128)S(1)}, u32[]{:S(2)}, u32[]{:S(2)}) %collective-permute-start.17) | collective-permute-done | bytes 544 | tf_op jit(solution)/shard_map/ppermute | solution.py:337
  29.3 1.6 collective-permute-start.1
  30.8 1.5 collective-permute-start.6
  32.3 0.5 collective-permute-start.11
  33.0 1.6 collective-permute-start.18
  34.5 6.5 %collective-permute-start.2 = (bf16[128,3584]{1,0:T(8,128)(2,1)}, bf16[128,3584]{1,0:T(8,128)(2,1)}, u32[]{:S(2)}, u32[]{:S(2)}) collective-permute-start(bf16[128,3584]{1,0:T(8,128)(2,1)} %collective-permute-done.1.b_ref), channel_id=1, source_target_pairs={{0,4},{1,5},{2,6},{3,7},{4,0},{5,1},{6,2},{7,3},{8,12},{9,13},{10,... | collective-permute-start | bytes 2752520 | tf_op jit(solution)/shard_map/ppermute | solution.py:337
  41.0 13.4 %collective-permute-done.6.g2m_ref = bf16[1792,256]{1,0:T(8,128)(2,1)} collective-permute-done((bf16[1792,256]{1,0:T(8,128)(2,1)}, bf16[1792,256]{1,0:T(8,128)(2,1)}, u32[]{:S(2)}, u32[]{:S(2)}) %collective-permute-start.6) | collective-permute-done | bytes 917536 | tf_op jit(solution)/shard_map/ppermute | solution.py:337
  54.5 19.7 %collective-permute-done.11.u2m_ref = bf16[1792,256]{1,0:T(8,128)(2,1)} collective-permute-done((bf16[1792,256]{1,0:T(8,128)(2,1)}, bf16[1792,256]{1,0:T(8,128)(2,1)}, u32[]{:S(2)}, u32[]{:S(2)}) %collective-permute-start.11) | collective-permute-done | bytes 917536 | tf_op jit(solution)/shard_map/ppermute | solution.py:337
  74.1 8.3 %collective-permute-start.3 = (bf16[128,3584]{1,0:T(8,128)(2,1)}, bf16[128,3584]{1,0:T(8,128)(2,1)}, u32[]{:S(2)}, u32[]{:S(2)}) collective-permute-start(bf16[128,3584]{1,0:T(8,128)(2,1)} %collective-permute-done.a_ref), channel_id=1, source_target_pairs={{4,8},{5,9},{6,10},{7,11},{8,4},{9,5},{10,6},{11,7},{0,0},{1,1},{2... | collective-permute-start | bytes 2752520 | tf_op jit(solution)/shard_map/ppermute | solution.py:337
  82.4 9.0 %collective-permute-done.18.refs_0_ = bf16[512,896]{1,0:T(8,128)(2,1)} collective-permute-done((bf16[512,896]{1,0:T(8,128)(2,1)S(1)}, bf16[512,896]{1,0:T(8,128)(2,1)}, u32[]{:S(2)}, u32[]{:S(2)}) %collective-permute-start.18) | collective-permute-done | bytes 917536 | tf_op jit(solution)/shard_map/ppermute | solution.py:337
  91.4 1.5 collective-permute-start.7
  92.9 0.6 collective-permute-start.12
  94.1 20.9 %collective-permute-done.7.g2o_ref = bf16[1792,256]{1,0:T(8,128)(2,1)} collective-permute-done((bf16[1792,256]{1,0:T(8,128)(2,1)}, bf16[1792,256]{1,0:T(8,128)(2,1)}, u32[]{:S(2)}, u32[]{:S(2)}) %collective-permute-start.7) | collective-permute-done | bytes 917536 | tf_op jit(solution)/shard_map/ppermute | solution.py:357
  115.2 1.6 collective-permute-start.19
  116.8 17.9 %collective-permute-done.12.u2o_ref = bf16[1792,256]{1,0:T(8,128)(2,1)} collective-permute-done((bf16[1792,256]{1,0:T(8,128)(2,1)}, bf16[1792,256]{1,0:T(8,128)(2,1)}, u32[]{:S(2)}, u32[]{:S(2)}) %collective-permute-start.12) | collective-permute-done | bytes 917536 | tf_op jit(solution)/shard_map/ppermute | solution.py:357
  134.7 0.5 collective-permute-start.14
  135.3 0.7 constant_dynamic-slice_fusion.1
  136.2 0.7 copy.37
  136.9 0.9 pad_maximum_fusion.scale_ref
  138.0 1.0 constant_dynamic-slice_fusion
  139.0 1.1 dynamic-slice_select_fusion.1
  140.1 10.9 %collective-permute-done.19.refs_1_ = bf16[512,896]{1,0:T(8,128)(2,1)} collective-permute-done((bf16[512,896]{1,0:T(8,128)(2,1)}, bf16[512,896]{1,0:T(8,128)(2,1)}, u32[]{:S(2)}, u32[]{:S(2)}) %collective-permute-start.19) | collective-permute-done | bytes 917536 | tf_op jit(solution)/shard_map/ppermute | solution.py:357
  151.0 1.5 collective-permute-start.34
  152.5 0.5 collective-permute-start.21
  153.0 15.6 %hidden_units.1.hidden_ref = bf16[4,128,1024]{2,1,0:T(8,128)(2,1)} custom-call(s32[3]{0:T(128)S(1)} %pad_add_fusion.place_ref, bf16[128,3584]{1,0:T(8,128)(2,1)S(1)} %fusion.2.own_ref, bf16[128,3584]{1,0:T(8,128)(2,1)} %collective-permute-done.a_ref, bf16[128,3584]{1,0:T(8,128)(2,1)} %collective-permute-done.1.b_ref, ...), custom_call_target="tpu_custom_call" | custom-call | flops 7516192768 | bytes 18350080 | tf_op jit(solution)/shard_map/hidden_units/pallas_call | solution.py:235
  168.7 1.2 copy-done.1
  169.9 5.3 %down_products.3 = (bf16[128,1792]{1,0:T(8,128)(2,1)S(1)}, bf16[128,1792]{1,0:T(8,128)(2,1)S(1)}, bf16[128,1792]{1,0:T(8,128)(2,1)}, bf16[128,1792]{1,0:T(8,128)(2,1)}) custom-call(s32[3]{0:T(128)S(1)} %pad_add_fusion.place_ref, bf16[4,128,1024]{2,1,0:T(8,128)(2,1)S(1)} %copy-done.1, f32[4,128,1]{2,1,0:T(8,128)S(1)} %pad_maximum_fusion.scale_ref, ...), custom_call_target="tpu_custom_call" | custom-call | flops 1879048192 | bytes 5505024 | tf_op jit(solution)/shard_map/down_products/pallas_call | solution.py:296
  175.2 0.6 collective-permute-start.31
  175.8 1.5 collective-permute-start.28
  177.3 1.1 dynamic-slice_select_fusion
  178.4 0.8 fusion.32
  179.3 1.4 collective-permute-start.37
  180.8 0.7 collective-permute-start.36
  181.5 2.4 collective-permute-start.35
  183.8 4.5 %down_products.2 = (bf16[128,1792]{1,0:T(8,128)(2,1)S(1)}, bf16[128,1792]{1,0:T(8,128)(2,1)S(1)}, bf16[128,1792]{1,0:T(8,128)(2,1)S(1)}, bf16[128,1792]{1,0:T(8,128)(2,1)S(1)}) custom-call(s32[3]{0:T(128)S(1)} %pad_add_fusion.place_ref, bf16[4,128,1024]{2,1,0:T(8,128)(2,1)S(1)} %copy-done.1, f32[4,128,1]{2,1,0:T(8,128)S(1)} %pad_maximum_fusion.scale_ref, ...), custom_call_target="tpu_custom_call" | custom-call | flops 1879048192 | bytes 5505024 | tf_op jit(solution)/shard_map/down_products/pallas_call | solution.py:296
  188.3 13.4 %collective-permute-done.37 = bf16[128,576]{0,1:T(8,128)(2,1)S(1)} collective-permute-done((bf16[128,576]{0,1:T(8,128)(2,1)S(1)}, bf16[128,576]{0,1:T(8,128)(2,1)S(1)}, u32[]{:S(2)}, u32[]{:S(2)}) %collective-permute-start.37) | collective-permute-done | bytes 147488 | tf_op jit(solution)/shard_map/ppermute | solution.py:337
  201.8 1.3 collective-permute-done.36
  203.1 2.4 collective-permute-start.22
  205.5 2.7 collective-permute-done.35
  208.8 1.8 scatter_custom_fusion
  210.7 3.5 %all-to-all-start = ((bf16[16,16,576]{2,1,0:T(8,128)(2,1)}), bf16[16,16,576]{2,1,0:T(8,128)(2,1)S(1)}, u32[]{:S(2)}, u32[]{:S(2)}) async-start(bf16[16,16,576]{2,1,0:T(8,128)(2,1)} %bitcast.10), calls=%async_computation | async-start | bytes 655360 | tf_op jit(solution)/shard_map/all_to_all | solution.py:447
  214.2 2.0 add_convert_fusion.1
  216.2 5.0 %collective-permute-start.32 = (bf16[128,1792]{1,0:T(8,128)(2,1)}, bf16[128,1792]{1,0:T(8,128)(2,1)}, u32[]{:S(2)}, u32[]{:S(2)}) collective-permute-start(bf16[128,1792]{1,0:T(8,128)(2,1)} %add_convert_fusion.1), channel_id=1, source_target_pairs={{4,8},{5,9},{6,10},{7,11},{8,4},{9,5},{10,6},{11,7},{0,0},{1,1},{2... | collective-permute-start | bytes 1376264 | tf_op jit(solution)/shard_map/ppermute | solution.py:337
  221.3 2.0 add_convert_fusion.3
  223.3 5.0 %collective-permute-start.29 = (bf16[128,1792]{1,0:T(8,128)(2,1)}, bf16[128,1792]{1,0:T(8,128)(2,1)}, u32[]{:S(2)}, u32[]{:S(2)}) collective-permute-start(bf16[128,1792]{1,0:T(8,128)(2,1)} %add_convert_fusion.3), channel_id=1, source_target_pairs={{4,8},{5,9},{6,10},{7,11},{8,4},{9,5},{10,6},{11,7},{0,0},{1,1},{2... | collective-permute-start | bytes 1376264 | tf_op jit(solution)/shard_map/ppermute | solution.py:337
  228.4 1.9 add_convert_fusion.5
  230.3 5.0 %collective-permute-start.26 = (bf16[128,1792]{1,0:T(8,128)(2,1)}, bf16[128,1792]{1,0:T(8,128)(2,1)}, u32[]{:S(2)}, u32[]{:S(2)}) collective-permute-start(bf16[128,1792]{1,0:T(8,128)(2,1)} %add_convert_fusion.5), channel_id=1, source_target_pairs={{4,8},{5,9},{6,10},{7,11},{8,4},{9,5},{10,6},{11,7},{0,0},{1,1},{2... | collective-permute-start | bytes 1376264 | tf_op jit(solution)/shard_map/ppermute | solution.py:337
  235.3 1.1 add_convert_fusion.7
  236.5 0.7 collective-permute-start.23
  237.2 0.9 copy.41
  238.1 1.2 add_convert_fusion.2
  239.2 8.9 %collective-permute-start.30 = (bf16[128,1792]{1,0:T(8,128)(2,1)S(1)}, bf16[128,1792]{1,0:T(8,128)(2,1)S(1)}, u32[]{:S(2)}, u32[]{:S(2)}) collective-permute-start(bf16[128,1792]{1,0:T(8,128)(2,1)S(1)} %add_convert_fusion.2), channel_id=1, source_target_pairs={{0,4},{1,5},{2,6},{3,7},{4,0},{5,1},{6,2},{7,3},{8,12},{9,13},{10,... | collective-permute-start | bytes 1376264 | tf_op jit(solution)/shard_map/ppermute | solution.py:337
  248.3 17.6 %collective-permute-start.24 = (bf16[128,1792]{1,0:T(8,128)(2,1)S(1)}, bf16[128,1792]{1,0:T(8,128)(2,1)S(1)}, u32[]{:S(2)}, u32[]{:S(2)}) collective-permute-start(bf16[128,1792]{1,0:T(8,128)(2,1)S(1)} %add_convert_fusion.6), channel_id=1, source_target_pairs={{0,4},{1,5},{2,6},{3,7},{4,0},{5,1},{6,2},{7,3},{8,12},{9,13},{10,... | collective-permute-start | bytes 1376264 | tf_op jit(solution)/shard_map/ppermute | solution.py:337
  265.9 1.2 add_convert_fusion
  267.2 8.7 %collective-permute-done.24 = bf16[128,1792]{1,0:T(8,128)(2,1)S(1)} collective-permute-done((bf16[128,1792]{1,0:T(8,128)(2,1)S(1)}, bf16[128,1792]{1,0:T(8,128)(2,1)S(1)}, u32[]{:S(2)}, u32[]{:S(2)}) %collective-permute-start.24) | collective-permute-done | bytes 458784 | tf_op jit(solution)/shard_map/ppermute | solution.py:337
  275.9 1.2 add_convert_fusion.4
  277.2 1.2 maximum_select_fusion.2
  (78 shorter events, 2.5 us)
Async XLA Ops:
  0.6 6.1 %copy-start.6 = (f32[128,2]{0,1:T(2,128)S(1)}, f32[128,2]{0,1:T(2,128)}, u32[]{:S(2)}) copy-start(f32[128,2]{0,1:T(2,128)} %param.18) | copy-start | bytes 3076
  0.6 6.1 %copy-start.7 = (s32[128,2]{0,1:T(2,128)S(1)}, s32[128,2]{0,1:T(2,128)}, u32[]{:S(2)}) copy-start(s32[128,2]{0,1:T(2,128)} %param.17) | copy-start | bytes 3076
  0.7 10.6 %copy-start.2 = (bf16[224,576]{1,0:T(8,128)(2,1)S(1)}, bf16[224,576]{1,0:T(8,128)(2,1)}, u32[]{:S(2)}) copy-start(bf16[224,576]{1,0:T(8,128)(2,1)} %param.12) | copy-start | bytes 774148
  3.6 29.3 %collective-permute-start = (bf16[128,3584]{1,0:T(8,128)(2,1)S(1)}, bf16[128,3584]{1,0:T(8,128)(2,1)}, u32[]{:S(2)}, u32[]{:S(2)}) collective-permute-start(bf16[128,3584]{1,0:T(8,128)(2,1)S(1)} %fusion.2.own_ref), channel_id=1, source_target_pairs={{0,4},{1,5},{2,6},{3,7},{4,0},{5,1},{6,2},{7,3},{8,12},{9,13},{10,... | collective-permute-start | bytes 2752520 | tf_op jit(solution)/shard_map/ppermute | solution.py:337
  6.8 22.5 %collective-permute-start.17 = (f32[128,1]{0,1:T(1,128)S(1)}, f32[128,1]{0,1:T(1,128)S(1)}, u32[]{:S(2)}, u32[]{:S(2)}) collective-permute-start(f32[128,1]{0,1:T(1,128)S(1)} %get-tuple-element.30), channel_id=1, source_target_pairs={{0,12},{1,13},{2,14},{3,15},{4,8},{5,9},{6,10},{7,11},{8,4},{9,5},... | collective-permute-start | bytes 1544 | tf_op jit(solution)/shard_map/ppermute | solution.py:337
  9.3 21.5 %collective-permute-start.16 = (f32[128,1]{0,1:T(1,128)S(1)}, f32[128,1]{0,1:T(1,128)S(1)}, u32[]{:S(2)}, u32[]{:S(2)}) collective-permute-start(f32[128,1]{0,1:T(1,128)S(1)} %get-tuple-element.31), channel_id=1, source_target_pairs={{0,8},{1,9},{2,10},{3,11},{4,12},{5,13},{6,14},{7,15},{8,0},{9,1},... | collective-permute-start | bytes 1544 | tf_op jit(solution)/shard_map/ppermute | solution.py:337
  9.5 22.8 %collective-permute-start.15 = (f32[128,1]{0,1:T(1,128)S(1)}, f32[128,1]{0,1:T(1,128)S(1)}, u32[]{:S(2)}, u32[]{:S(2)}) collective-permute-start(f32[128,1]{0,1:T(1,128)S(1)} %get-tuple-element.32), channel_id=1, source_target_pairs={{0,4},{1,5},{2,6},{3,7},{4,0},{5,1},{6,2},{7,3},{8,12},{9,13},{10,... | collective-permute-start | bytes 1544 | tf_op jit(solution)/shard_map/ppermute | solution.py:337
  11.2 21.6 %collective-permute-start.33 = (bf16[224,576]{1,0:T(8,128)(2,1)S(1)}, bf16[224,576]{1,0:T(8,128)(2,1)S(1)}, u32[]{:S(2)}, u32[]{:S(2)}) collective-permute-start(bf16[224,576]{1,0:T(8,128)(2,1)S(1)} %copy-done.2), channel_id=1, source_target_pairs={{0,1},{1,0},{2,3},{3,2},{4,5},{5,4},{6,7},{7,6},{8,9},{9,8},{10,11... | collective-permute-start | bytes 774152 | tf_op jit(solution)/shard_map/ppermute | solution.py:337
  11.2 21.6 %copy-start = (bf16[1024,896]{1,0:T(8,128)(2,1)S(1)}, bf16[1024,896]{1,0:T(8,128)(2,1)}, u32[]{:S(2)}) copy-start(bf16[1024,896]{1,0:T(8,128)(2,1)} %refs_0_.1) | copy-start | bytes 5505028
  13.5 80.2 %copy-start.5 = (s32[128,1]{0,1:T(1,128)S(1)}, s32[128,1]{0,1:T(1,128)}, u32[]{:S(2)}) copy-start(s32[128,1]{0,1:T(1,128)} %param.19) | copy-start | bytes 1540
  29.3 5.3 %collective-permute-start.1 = (bf16[128,3584]{1,0:T(8,128)(2,1)S(1)}, bf16[128,3584]{1,0:T(8,128)(2,1)}, u32[]{:S(2)}, u32[]{:S(2)}) collective-permute-start(bf16[128,3584]{1,0:T(8,128)(2,1)S(1)} %fusion.2.own_ref), channel_id=1, source_target_pairs={{4,8},{5,9},{6,10},{7,11},{8,4},{9,5},{10,6},{11,7},{0,0},{1,1},{2... | collective-permute-start | bytes 2752520 | tf_op jit(solution)/shard_map/ppermute | solution.py:337
  30.8 23.6 %collective-permute-start.6 = (bf16[1792,256]{1,0:T(8,128)(2,1)}, bf16[1792,256]{1,0:T(8,128)(2,1)}, u32[]{:S(2)}, u32[]{:S(2)}) collective-permute-start(bf16[1792,256]{1,0:T(8,128)(2,1)} %constant_dynamic-slice_fusion.8), channel_id=1, source_target_pairs={{0,2},{1,3},{2,0},{3,1},{4,6},{5,7},{6,4},{7,5},{8,10},{9,11},{10,... | collective-permute-start | bytes 2752520 | tf_op jit(solution)/shard_map/ppermute | solution.py:337
  32.3 41.8 %collective-permute-start.11 = (bf16[1792,256]{1,0:T(8,128)(2,1)}, bf16[1792,256]{1,0:T(8,128)(2,1)}, u32[]{:S(2)}, u32[]{:S(2)}) collective-permute-start(bf16[1792,256]{1,0:T(8,128)(2,1)} %constant_dynamic-slice_fusion.7), channel_id=1, source_target_pairs={{0,2},{1,3},{2,0},{3,1},{4,6},{5,7},{6,4},{7,5},{8,10},{9,11},{10,... | collective-permute-start | bytes 2752520 | tf_op jit(solution)/shard_map/ppermute | solution.py:337
  32.9 60.6 %collective-permute-start.5 = (bf16[3584,256]{1,0:T(8,128)(2,1)}, bf16[3584,256]{1,0:T(8,128)(2,1)}, u32[]{:S(2)}, u32[]{:S(2)}) collective-permute-start(bf16[3584,256]{1,0:T(8,128)(2,1)} %g0_ref.1), channel_id=1, source_target_pairs={{0,1},{1,0},{2,3},{3,2},{4,5},{5,4},{6,7},{7,6},{8,9},{9,8},{10,11... | collective-permute-start | bytes 5505032 | tf_op jit(solution)/shard_map/ppermute | solution.py:337
  33.0 58.4 %collective-permute-start.18 = (bf16[512,896]{1,0:T(8,128)(2,1)S(1)}, bf16[512,896]{1,0:T(8,128)(2,1)}, u32[]{:S(2)}, u32[]{:S(2)}) collective-permute-start(bf16[512,896]{1,0:T(8,128)(2,1)S(1)} %constant_dynamic-slice_fusion.2), channel_id=1, source_target_pairs={{0,2},{1,3},{2,0},{3,1},{4,6},{5,7},{6,4},{7,5},{8,10},{9,11},{10,... | collective-permute-start | bytes 2752520 | tf_op jit(solution)/shard_map/ppermute | solution.py:337
  34.5 58.4 %collective-permute-start.2 = (bf16[128,3584]{1,0:T(8,128)(2,1)}, bf16[128,3584]{1,0:T(8,128)(2,1)}, u32[]{:S(2)}, u32[]{:S(2)}) collective-permute-start(bf16[128,3584]{1,0:T(8,128)(2,1)} %collective-permute-done.1.b_ref), channel_id=1, source_target_pairs={{0,4},{1,5},{2,6},{3,7},{4,0},{5,1},{6,2},{7,3},{8,12},{9,13},{10,... | collective-permute-start | bytes 2752520 | tf_op jit(solution)/shard_map/ppermute | solution.py:337
  54.4 62.3 %collective-permute-start.10 = (bf16[3584,256]{1,0:T(8,128)(2,1)}, bf16[3584,256]{1,0:T(8,128)(2,1)}, u32[]{:S(2)}, u32[]{:S(2)}) collective-permute-start(bf16[3584,256]{1,0:T(8,128)(2,1)} %u0_ref.1), channel_id=1, source_target_pairs={{0,1},{1,0},{2,3},{3,2},{4,5},{5,4},{6,7},{7,6},{8,9},{9,8},{10,11... | collective-permute-start | bytes 5505032 | tf_op jit(solution)/shard_map/ppermute | solution.py:337
  74.1 18.8 %collective-permute-start.3 = (bf16[128,3584]{1,0:T(8,128)(2,1)}, bf16[128,3584]{1,0:T(8,128)(2,1)}, u32[]{:S(2)}, u32[]{:S(2)}) collective-permute-start(bf16[128,3584]{1,0:T(8,128)(2,1)} %collective-permute-done.a_ref), channel_id=1, source_target_pairs={{4,8},{5,9},{6,10},{7,11},{8,4},{9,5},{10,6},{11,7},{0,0},{1,1},{2... | collective-permute-start | bytes 2752520 | tf_op jit(solution)/shard_map/ppermute | solution.py:337
  91.4 23.6 %collective-permute-start.7 = (bf16[1792,256]{1,0:T(8,128)(2,1)}, bf16[1792,256]{1,0:T(8,128)(2,1)}, u32[]{:S(2)}, u32[]{:S(2)}) collective-permute-start(bf16[1792,256]{1,0:T(8,128)(2,1)} %collective-permute-done.6.g2m_ref), channel_id=1, source_target_pairs={{0,16},{16,0},{1,17},{17,1},{2,18},{18,2},{3,19},{19,3},{4,20},{20... | collective-permute-start | bytes 2752520 | tf_op jit(solution)/shard_map/ppermute | solution.py:357
  92.9 22.3 %collective-permute-start.8 = (bf16[1792,256]{1,0:T(8,128)(2,1)}, bf16[1792,256]{1,0:T(8,128)(2,1)}, u32[]{:S(2)}, u32[]{:S(2)}) collective-permute-start(bf16[1792,256]{1,0:T(8,128)(2,1)} %collective-permute-done.6.g2m_ref), channel_id=1, source_target_pairs={{0,1},{1,0},{2,3},{3,2},{4,5},{5,4},{6,7},{7,6},{8,9},{9,8},{10,11... | collective-permute-start | bytes 2752520 | tf_op jit(solution)/shard_map/ppermute | solution.py:337
  92.9 41.7 %collective-permute-start.12 = (bf16[1792,256]{1,0:T(8,128)(2,1)}, bf16[1792,256]{1,0:T(8,128)(2,1)}, u32[]{:S(2)}, u32[]{:S(2)}) collective-permute-start(bf16[1792,256]{1,0:T(8,128)(2,1)} %collective-permute-done.11.u2m_ref), channel_id=1, source_target_pairs={{0,16},{16,0},{1,17},{17,1},{2,18},{18,2},{3,19},{19,3},{4,20},{20... | collective-permute-start | bytes 2752520 | tf_op jit(solution)/shard_map/ppermute | solution.py:357
  93.5 41.2 %collective-permute-start.13 = (bf16[1792,256]{1,0:T(8,128)(2,1)}, bf16[1792,256]{1,0:T(8,128)(2,1)}, u32[]{:S(2)}, u32[]{:S(2)}) collective-permute-start(bf16[1792,256]{1,0:T(8,128)(2,1)} %collective-permute-done.11.u2m_ref), channel_id=1, source_target_pairs={{0,1},{1,0},{2,3},{3,2},{4,5},{5,4},{6,7},{7,6},{8,9},{9,8},{10,11... | collective-permute-start | bytes 2752520 | tf_op jit(solution)/shard_map/ppermute | solution.py:337
  115.0 53.6 %collective-permute-start.27 = (bf16[1024,896]{1,0:T(8,128)(2,1)S(1)}, bf16[1024,896]{1,0:T(8,128)(2,1)}, u32[]{:S(2)}, u32[]{:S(2)}) collective-permute-start(bf16[1024,896]{1,0:T(8,128)(2,1)S(1)} %copy-done), channel_id=1, source_target_pairs={{0,1},{1,0},{2,3},{3,2},{4,5},{5,4},{6,7},{7,6},{8,9},{9,8},{10,11... | collective-permute-start | bytes 5505032 | tf_op jit(solution)/shard_map/ppermute | solution.py:337
  115.2 35.8 %collective-permute-start.19 = (bf16[512,896]{1,0:T(8,128)(2,1)}, bf16[512,896]{1,0:T(8,128)(2,1)}, u32[]{:S(2)}, u32[]{:S(2)}) collective-permute-start(bf16[512,896]{1,0:T(8,128)(2,1)} %collective-permute-done.18.refs_0_), channel_id=1, source_target_pairs={{0,16},{16,0},{1,17},{17,1},{2,18},{18,2},{3,19},{19,3},{4,20},{20... | collective-permute-start | bytes 2752520 | tf_op jit(solution)/shard_map/ppermute | solution.py:357
  116.8 35.7 %collective-permute-start.4 = (bf16[128,3584]{1,0:T(8,128)(2,1)}, bf16[128,3584]{1,0:T(8,128)(2,1)}, u32[]{:S(2)}, u32[]{:S(2)}) collective-permute-start(bf16[128,3584]{1,0:T(8,128)(2,1)} %collective-permute-done.3.d_ref), channel_id=1, source_target_pairs={{0,4},{1,5},{2,6},{3,7},{4,0},{5,1},{6,2},{7,3},{8,12},{9,13},{10,... | collective-permute-start | bytes 2752520 | tf_op jit(solution)/shard_map/ppermute | solution.py:337
  134.7 17.9 %collective-permute-start.9 = (bf16[1792,256]{1,0:T(8,128)(2,1)}, bf16[1792,256]{1,0:T(8,128)(2,1)}, u32[]{:S(2)}, u32[]{:S(2)}) collective-permute-start(bf16[1792,256]{1,0:T(8,128)(2,1)} %collective-permute-done.7.g2o_ref), channel_id=1, source_target_pairs={{0,1},{1,0},{2,3},{3,2},{4,5},{5,4},{6,7},{7,6},{8,9},{9,8},{10,11... | collective-permute-start | bytes 2752520 | tf_op jit(solution)/shard_map/ppermute | solution.py:337
  134.7 18.4 %collective-permute-start.14 = (bf16[1792,256]{1,0:T(8,128)(2,1)}, bf16[1792,256]{1,0:T(8,128)(2,1)}, u32[]{:S(2)}, u32[]{:S(2)}) collective-permute-start(bf16[1792,256]{1,0:T(8,128)(2,1)} %collective-permute-done.12.u2o_ref), channel_id=1, source_target_pairs={{0,1},{1,0},{2,3},{3,2},{4,5},{5,4},{6,7},{7,6},{8,9},{9,8},{10,11... | collective-permute-start | bytes 2752520 | tf_op jit(solution)/shard_map/ppermute | solution.py:337
  151.0 27.4 %collective-permute-start.34 = (bf16[448,576]{1,0:T(8,128)(2,1)S(1)}, bf16[448,576]{1,0:T(8,128)(2,1)S(1)}, u32[]{:S(2)}, u32[]{:S(2)}) collective-permute-start(bf16[448,576]{1,0:T(8,128)(2,1)S(1)} %maximum_select_fusion.3), channel_id=1, source_target_pairs={{0,2},{1,3},{2,0},{3,1},{4,6},{5,7},{6,4},{7,5},{8,10},{9,11},{10,... | collective-permute-start | bytes 1548296 | tf_op jit(solution)/shard_map/ppermute | solution.py:337
  152.5 28.2 %collective-permute-start.20 = (bf16[512,896]{1,0:T(8,128)(2,1)}, bf16[512,896]{1,0:T(8,128)(2,1)S(1)}, u32[]{:S(2)}, u32[]{:S(2)}) collective-permute-start(bf16[512,896]{1,0:T(8,128)(2,1)} %collective-permute-done.18.refs_0_), channel_id=1, source_target_pairs={{0,1},{1,0},{2,3},{3,2},{4,5},{5,4},{6,7},{7,6},{8,9},{9,8},{10,11... | collective-permute-start | bytes 2752520 | tf_op jit(solution)/shard_map/ppermute | solution.py:337
  152.5 28.9 %collective-permute-start.21 = (bf16[512,896]{1,0:T(8,128)(2,1)}, bf16[512,896]{1,0:T(8,128)(2,1)S(1)}, u32[]{:S(2)}, u32[]{:S(2)}) collective-permute-start(bf16[512,896]{1,0:T(8,128)(2,1)} %collective-permute-done.19.refs_1_), channel_id=1, source_target_pairs={{0,1},{1,0},{2,3},{3,2},{4,5},{5,4},{6,7},{7,6},{8,9},{9,8},{10,11... | collective-permute-start | bytes 2752520 | tf_op jit(solution)/shard_map/ppermute | solution.py:337
  168.6 1.2 copy-start.1
  169.9 8.6 %copy-start.3 = (bf16[128,896]{1,0:T(8,128)(2,1)S(1)}, bf16[128,896]{1,0:T(8,128)(2,1)}, u32[]{:S(2)}) copy-start(bf16[128,896]{1,0:T(8,128)(2,1)} %constant_dynamic-slice_fusion.1) | copy-start | bytes 688132
  175.2 39.0 %collective-permute-start.31 = (bf16[128,1792]{1,0:T(8,128)(2,1)}, bf16[128,1792]{1,0:T(8,128)(2,1)}, u32[]{:S(2)}, u32[]{:S(2)}) collective-permute-start(bf16[128,1792]{1,0:T(8,128)(2,1)} %get-tuple-element.16), channel_id=1, source_target_pairs={{0,4},{1,5},{2,6},{3,7},{4,0},{5,1},{6,2},{7,3},{8,12},{9,13},{10,... | collective-permute-start | bytes 1376264 | tf_op jit(solution)/shard_map/ppermute | solution.py:337
  175.8 45.5 %collective-permute-start.28 = (bf16[128,1792]{1,0:T(8,128)(2,1)}, bf16[128,1792]{1,0:T(8,128)(2,1)}, u32[]{:S(2)}, u32[]{:S(2)}) collective-permute-start(bf16[128,1792]{1,0:T(8,128)(2,1)} %get-tuple-element.17), channel_id=1, source_target_pairs={{0,4},{1,5},{2,6},{3,7},{4,0},{5,1},{6,2},{7,3},{8,12},{9,13},{10,... | collective-permute-start | bytes 1376264 | tf_op jit(solution)/shard_map/ppermute | solution.py:337
  179.3 22.4 %collective-permute-start.37 = (bf16[128,576]{0,1:T(8,128)(2,1)S(1)}, bf16[128,576]{0,1:T(8,128)(2,1)S(1)}, u32[]{:S(2)}, u32[]{:S(2)}) collective-permute-start(bf16[128,576]{0,1:T(8,128)(2,1)S(1)} %get-tuple-element.25), channel_id=1, source_target_pairs={{0,12},{1,13},{2,14},{3,15},{4,8},{5,9},{6,10},{7,11},{8,4},{9,5},... | collective-permute-start | bytes 442376 | tf_op jit(solution)/shard_map/ppermute | solution.py:337
  180.8 22.3 %collective-permute-start.36 = (bf16[128,576]{0,1:T(8,128)(2,1)S(1)}, bf16[128,576]{0,1:T(8,128)(2,1)S(1)}, u32[]{:S(2)}, u32[]{:S(2)}) collective-permute-start(bf16[128,576]{0,1:T(8,128)(2,1)S(1)} %get-tuple-element.26), channel_id=1, source_target_pairs={{0,8},{1,9},{2,10},{3,11},{4,12},{5,13},{6,14},{7,15},{8,0},{9,1},... | collective-permute-start | bytes 442376 | tf_op jit(solution)/shard_map/ppermute | solution.py:337
  181.5 27.0 %copy-start.4 = (f32[512]{0:T(512)S(1)}, f32[512]{0:T(512)}, u32[]{:S(2)}) copy-start(f32[512]{0:T(512)} %param.13) | copy-start | bytes 6148
  181.5 26.7 %collective-permute-start.35 = (bf16[128,576]{0,1:T(8,128)(2,1)S(1)}, bf16[128,576]{0,1:T(8,128)(2,1)S(1)}, u32[]{:S(2)}, u32[]{:S(2)}) collective-permute-start(bf16[128,576]{0,1:T(8,128)(2,1)S(1)} %get-tuple-element.24), channel_id=1, source_target_pairs={{0,4},{1,5},{2,6},{3,7},{4,0},{5,1},{6,2},{7,3},{8,12},{9,13},{10,... | collective-permute-start | bytes 442376 | tf_op jit(solution)/shard_map/ppermute | solution.py:337
  201.8 26.6 %collective-permute-start.25 = (bf16[128,1792]{1,0:T(8,128)(2,1)S(1)}, bf16[128,1792]{1,0:T(8,128)(2,1)}, u32[]{:S(2)}, u32[]{:S(2)}) collective-permute-start(bf16[128,1792]{1,0:T(8,128)(2,1)S(1)} %get-tuple-element.12), channel_id=1, source_target_pairs={{0,4},{1,5},{2,6},{3,7},{4,0},{5,1},{6,2},{7,3},{8,12},{9,13},{10,... | collective-permute-start | bytes 1376264 | tf_op jit(solution)/shard_map/ppermute | solution.py:337
  203.1 32.3 %collective-permute-start.22 = (bf16[128,1792]{1,0:T(8,128)(2,1)S(1)}, bf16[128,1792]{1,0:T(8,128)(2,1)}, u32[]{:S(2)}, u32[]{:S(2)}) collective-permute-start(bf16[128,1792]{1,0:T(8,128)(2,1)S(1)} %get-tuple-element.13), channel_id=1, source_target_pairs={{0,4},{1,5},{2,6},{3,7},{4,0},{5,1},{6,2},{7,3},{8,12},{9,13},{10,... | collective-permute-start | bytes 1376264 | tf_op jit(solution)/shard_map/ppermute | solution.py:337
  210.7 26.5 %all-to-all-start = ((bf16[16,16,576]{2,1,0:T(8,128)(2,1)}), bf16[16,16,576]{2,1,0:T(8,128)(2,1)S(1)}, u32[]{:S(2)}, u32[]{:S(2)}) async-start(bf16[16,16,576]{2,1,0:T(8,128)(2,1)} %bitcast.10), calls=%async_computation | async-start | bytes 655360 | tf_op jit(solution)/shard_map/all_to_all | solution.py:447
  216.2 49.7 %collective-permute-start.32 = (bf16[128,1792]{1,0:T(8,128)(2,1)}, bf16[128,1792]{1,0:T(8,128)(2,1)}, u32[]{:S(2)}, u32[]{:S(2)}) collective-permute-start(bf16[128,1792]{1,0:T(8,128)(2,1)} %add_convert_fusion.1), channel_id=1, source_target_pairs={{4,8},{5,9},{6,10},{7,11},{8,4},{9,5},{10,6},{11,7},{0,0},{1,1},{2... | collective-permute-start | bytes 1376264 | tf_op jit(solution)/shard_map/ppermute | solution.py:337
  223.3 14.8 %collective-permute-start.29 = (bf16[128,1792]{1,0:T(8,128)(2,1)}, bf16[128,1792]{1,0:T(8,128)(2,1)}, u32[]{:S(2)}, u32[]{:S(2)}) collective-permute-start(bf16[128,1792]{1,0:T(8,128)(2,1)} %add_convert_fusion.3), channel_id=1, source_target_pairs={{4,8},{5,9},{6,10},{7,11},{8,4},{9,5},{10,6},{11,7},{0,0},{1,1},{2... | collective-permute-start | bytes 1376264 | tf_op jit(solution)/shard_map/ppermute | solution.py:337
  230.3 36.9 %collective-permute-start.26 = (bf16[128,1792]{1,0:T(8,128)(2,1)}, bf16[128,1792]{1,0:T(8,128)(2,1)}, u32[]{:S(2)}, u32[]{:S(2)}) collective-permute-start(bf16[128,1792]{1,0:T(8,128)(2,1)} %add_convert_fusion.5), channel_id=1, source_target_pairs={{4,8},{5,9},{6,10},{7,11},{8,4},{9,5},{10,6},{11,7},{0,0},{1,1},{2... | collective-permute-start | bytes 1376264 | tf_op jit(solution)/shard_map/ppermute | solution.py:337
  236.5 11.7 %collective-permute-start.23 = (bf16[128,1792]{1,0:T(8,128)(2,1)S(1)}, bf16[128,1792]{1,0:T(8,128)(2,1)S(1)}, u32[]{:S(2)}, u32[]{:S(2)}) collective-permute-start(bf16[128,1792]{1,0:T(8,128)(2,1)S(1)} %add_convert_fusion.7), channel_id=1, source_target_pairs={{4,8},{5,9},{6,10},{7,11},{8,4},{9,5},{10,6},{11,7},{0,0},{1,1},{2... | collective-permute-start | bytes 1376264 | tf_op jit(solution)/shard_map/ppermute | solution.py:337
  239.2 26.7 %collective-permute-start.30 = (bf16[128,1792]{1,0:T(8,128)(2,1)S(1)}, bf16[128,1792]{1,0:T(8,128)(2,1)S(1)}, u32[]{:S(2)}, u32[]{:S(2)}) collective-permute-start(bf16[128,1792]{1,0:T(8,128)(2,1)S(1)} %add_convert_fusion.2), channel_id=1, source_target_pairs={{0,4},{1,5},{2,6},{3,7},{4,0},{5,1},{6,2},{7,3},{8,12},{9,13},{10,... | collective-permute-start | bytes 1376264 | tf_op jit(solution)/shard_map/ppermute | solution.py:337
  248.3 27.6 %collective-permute-start.24 = (bf16[128,1792]{1,0:T(8,128)(2,1)S(1)}, bf16[128,1792]{1,0:T(8,128)(2,1)S(1)}, u32[]{:S(2)}, u32[]{:S(2)}) collective-permute-start(bf16[128,1792]{1,0:T(8,128)(2,1)S(1)} %add_convert_fusion.6), channel_id=1, source_target_pairs={{0,4},{1,5},{2,6},{3,7},{4,0},{5,1},{6,2},{7,3},{8,12},{9,13},{10,... | collective-permute-start | bytes 1376264 | tf_op jit(solution)/shard_map/ppermute | solution.py:337

commit v2 on v0

--- a/solution.py
+++ b/solution.py
@@ -1,12 +1,20 @@
+import functools
+
 import jax
 import jax.numpy as jnp
 from jax import lax
+from jax.experimental import pallas as pl
+from jax.experimental.pallas import tpu as pltpu
 from jax.sharding import PartitionSpec as P
 
 KEY_VALUE_RANK = 512
 ROUTES = 2
 LOG_GROUP = 2
 GROUP = 4
+LINE = 4
+SCALE_COLUMNS = 128
+VMEM_GRANT = 56 * 1024 * 1024
+BRIEF = pl.CostEstimate(flops=1 << 20, bytes_accessed=1 << 20, transcendentals=0)
 
 
 eps = 1e-06
@@ -47,7 +55,28 @@
     return jnp.sum(before * onehot, axis=-1, dtype=jnp.int32)
 
 
-def shards(
+def latent_rows(raw_latent, key_value_gain):
+    token_positions = jnp.arange(raw_latent.shape[0], dtype=jnp.int32)
+    return jnp.concatenate(
+        [
+            root_mean_scale(raw_latent[:, :KEY_VALUE_RANK], key_value_gain),
+            apply_rotary_keys(raw_latent[:, KEY_VALUE_RANK:], token_positions),
+        ],
+        axis=-1,
+    ).astype(jnp.bfloat16)
+
+
+def cache_send_rows(latent_vector, owner, device_count, push_cap):
+    target = owner[:, 0]
+    rank_index = block_ranks(target[None, :], device_count)[0]
+    return (
+        jnp.zeros((device_count * push_cap, latent_vector.shape[1]), jnp.bfloat16)
+        .at[target * push_cap + rank_index]
+        .set(latent_vector)
+    )
+
+
+def packed_shards(
     tokens,
     norm_gain,
     kv_weight,
@@ -112,25 +141,421 @@
     weighted = route_gate.reshape(tok_rows * ROUTES, 1) * picked.astype(jnp.float32)
     combined = jnp.sum(weighted.reshape(tok_rows, ROUTES, features), axis=1)
     moe_out = combined.astype(jnp.bfloat16)
-    unnormed_latent = jnp.dot(
+    raw_latent = jnp.dot(
         normed,
         lax.all_gather(kv_weight, "dev", axis=0, tiled=True),
         preferred_element_type=jnp.float32,
     )
-    token_positions = jnp.arange(tok_rows, dtype=jnp.int32)
-    latent_vector = jnp.concatenate(
-        [
-            root_mean_scale(unnormed_latent[:, :KEY_VALUE_RANK], key_value_gain),
-            apply_rotary_keys(unnormed_latent[:, KEY_VALUE_RANK:], token_positions),
+    send_rows = cache_send_rows(
+        latent_rows(raw_latent, key_value_gain), owner, device_count, push_cap
+    )
+    latent_cache = lax.all_to_all(send_rows, "dev", split_axis=0, concat_axis=0, tiled=True)
+    return (moe_out, latent_cache)
+
+
+def entry_kernel(
+    place_ref, tokens_ref, gain_ref, index_ref, route_ref, weight_ref,
+    rows0_ref, rows1_ref, half_ref, sem,
+):
+    rows = half_ref.shape[0]
+    copy = pltpu.make_async_copy(weight_ref.at[pl.ds(place_ref[1] * rows, rows)], half_ref, sem)
+    copy.start()
+    tok_rows, features = tokens_ref.shape
+    some = rows0_ref.shape[0]
+    row = lax.broadcasted_iota(jnp.int32, (SCALE_COLUMNS, tok_rows), 0)
+    expert, term = row // 3, row % 3
+    left = jnp.zeros((SCALE_COLUMNS, tok_rows), jnp.float32)
+    for route in range(ROUTES):
+        named = index_ref[route : route + 1, :] == expert
+        left = jnp.where(named, route_ref[route : route + 1, :], left)
+    terms = jnp.zeros((SCALE_COLUMNS, tok_rows), jnp.float32)
+    for number in range(3):
+        rounded = left.astype(jnp.bfloat16).astype(jnp.float32)
+        terms = jnp.where(term == number, rounded, terms)
+        left = left - rounded
+    terms = terms.T.astype(jnp.bfloat16)
+    for part, ref in enumerate((rows0_ref, rows1_ref)):
+        mine = slice(part * some, (part + 1) * some)
+        values = tokens_ref[mine].astype(jnp.float32)
+        scale = lax.rsqrt(jnp.mean(values * values, axis=-1, keepdims=True) + eps)
+        lanes = gain_ref.shape[1]
+        for piece in range(gain_ref.shape[0]):
+            at_piece = slice(piece * lanes, (piece + 1) * lanes)
+            values = tokens_ref[mine, at_piece].astype(jnp.float32)
+            ref[:, at_piece] = (values * scale * gain_ref[piece : piece + 1, :]).astype(jnp.bfloat16)
+        ref[:, features:] = terms[mine]
+    copy.wait()
+
+
+def entry(place, tokens, gain, expert_index, route_gate, weight):
+    some, features = tokens.shape[0] // 2, tokens.shape[1]
+    smem, vmem, hbm = (
+        pl.BlockSpec(memory_space=space) for space in (pltpu.SMEM, pltpu.VMEM, pltpu.HBM)
+    )
+    rows = jax.ShapeDtypeStruct((some, features + SCALE_COLUMNS), jnp.bfloat16)
+    return pl.pallas_call(
+        entry_kernel,
+        out_shape=[
+            rows,
+            rows,
+            jax.ShapeDtypeStruct((weight.shape[0] // 2, weight.shape[1]), weight.dtype),
         ],
-        axis=-1,
-    ).astype(jnp.bfloat16)
-    target = owner[:, 0]
-    rank_index = block_ranks(target[None, :], device_count)[0]
-    send_rows = (
-        jnp.zeros((device_count * push_cap, latent_vector.shape[1]), jnp.bfloat16)
-        .at[target * push_cap + rank_index]
-        .set(latent_vector)
+        in_specs=[smem, vmem, vmem, vmem, vmem, hbm],
+        out_specs=[vmem] * 3,
+        scratch_shapes=[pltpu.SemaphoreType.DMA],
+        cost_estimate=BRIEF,
+        name="entry",
+    )(place, tokens, gain.reshape(-1, 128), expert_index.T, route_gate.T, weight)
+
+
+def halves_kernel(place_ref, *refs):
+    count = len(refs) // 2
+    copies = []
+    for index in range(count):
+        weight, half = refs[index], refs[count + index]
+        rows = half.shape[0]
+        source = weight.at[pl.ds(place_ref[1] * rows, rows)]
+        copies.append(pltpu.make_async_copy(source, half, refs[-1].at[index]))
+    for copy in copies:
+        copy.start()
+    for copy in copies:
+        copy.wait()
+
+
+def halves_of(place, *weights):
+    shapes = [
+        jax.ShapeDtypeStruct((weight.shape[0] // 2, weight.shape[1]), weight.dtype)
+        for weight in weights
+    ]
+    return pl.pallas_call(
+        halves_kernel,
+        out_shape=shapes,
+        in_specs=[pl.BlockSpec(memory_space=pltpu.SMEM)]
+        + [pl.BlockSpec(memory_space=pltpu.HBM)] * len(weights),
+        out_specs=[pl.BlockSpec(memory_space=pltpu.VMEM)] * len(weights),
+        scratch_shapes=[pltpu.SemaphoreType.DMA((len(weights),))],
+        cost_estimate=BRIEF,
+        name="weight_halves",
+    )(place, *weights)
+
+
+def begin_block(refs, buf, sems, slot, k, rep):
+    wholes = len(refs) - 4 if len(refs) > 4 else len(refs) % 4
+    for number in range(wholes):
+
+        @pl.when(k == number)
+        def _(number=number):
+            pltpu.make_async_copy(refs[number], buf.at[slot], sems.at[number]).start()
+
+    for index in range(wholes, len(refs), 2):
+        number = wholes + (index - wholes) // 2
+
+        @pl.when(k == number)
+        def _(number=number, index=index):
+            half = refs[index].shape[0]
+            for ref, part in ((refs[index], rep), (refs[index + 1], 1 - rep)):
+                target = buf.at[slot, pl.ds(part * half, half)]
+                pltpu.make_async_copy(ref, target, sems.at[number]).start()
+
+
+def await_block(buf, sems, slot, k):
+    pltpu.make_async_copy(buf.at[slot], buf.at[slot], sems.at[k]).wait()
+
+
+def latent_kernel(place_ref, *refs):
+    row_refs, kv_refs, part_refs = refs[:6], refs[6:10], refs[10:13]
+    rows_buf, kv_buf, row_sems, kv_sems = refs[13:]
+    place, plane = place_ref[0], place_ref[2]
+    depth, piece = rows_buf.shape[1], kv_refs[0].shape[0]
+    some = row_refs[0].shape[0]
+    columns = pl.ds(pl.multiple_of(plane * depth, 128), depth)
+    copies = [
+        pltpu.make_async_copy(
+            ref.at[:, columns], rows_buf.at[pl.ds(index * some, some)], row_sems.at[index]
+        )
+        for index, ref in enumerate(row_refs)
+    ] + [
+        pltpu.make_async_copy(ref, kv_buf.at[pl.ds((place ^ k) * piece, piece)], kv_sems.at[k])
+        for k, ref in enumerate(kv_refs)
+    ]
+    for copy in copies:
+        copy.start()
+    for copy in copies:
+        copy.wait()
+    out = jnp.dot(rows_buf[...], kv_buf[...], preferred_element_type=jnp.float32)
+    for index, ref in enumerate(part_refs):
+        ref[...] = out[2 * index * some : 2 * (index + 1) * some].astype(jnp.bfloat16)
+
+
+def latent_parts(place, rows, kv_parts):
+    some = rows[0].shape[0]
+    piece, width = kv_parts[0].shape
+    vmem, hbm = pl.BlockSpec(memory_space=pltpu.VMEM), pl.BlockSpec(memory_space=pltpu.HBM)
+    return pl.pallas_call(
+        latent_kernel,
+        out_shape=[jax.ShapeDtypeStruct((2 * some, width), jnp.bfloat16)] * (len(rows) // 2),
+        in_specs=[pl.BlockSpec(memory_space=pltpu.SMEM)] + [hbm] * (len(rows) + len(kv_parts)),
+        out_specs=[vmem] * (len(rows) // 2),
+        scratch_shapes=[
+            pltpu.VMEM((len(rows) * some, GROUP * piece), jnp.bfloat16),
+            pltpu.VMEM((GROUP * piece, width), jnp.bfloat16),
+            pltpu.SemaphoreType.DMA((len(rows),)),
+            pltpu.SemaphoreType.DMA((GROUP,)),
+        ],
+        compiler_params=pltpu.CompilerParams(vmem_limit_bytes=VMEM_GRANT),
+        cost_estimate=BRIEF,
+        name="latent_parts",
+    )(place, *rows, *kv_parts)
+
+
+def hidden_kernel(place_ref, *refs):
+    row_refs, gate_refs, up_refs, refs = refs[:7], refs[7:13], refs[13:19], refs[19:]
+    down_refs, kv_refs, refs = refs[:2], refs[2:6], refs[6:]
+    hidden_ref, scale_ref, latent_ref, part_refs, refs = refs[0], refs[1], refs[2], refs[3:7], refs[7:]
+    rows_buf, gate_buf, up_buf, down_buf, kv_buf = refs[:5]
+    row_sems, gate_sems, up_sems, down_sems, kv_sems = refs[5:]
+    place, rep, plane = place_ref[0], place_ref[1], place_ref[2]
+    core = place & 1
+    some = row_refs[0].shape[0]
+    row_copies, first = [], 0
+    for index, ref in enumerate(row_refs):
+        target = rows_buf.at[pl.ds(first, ref.shape[0])]
+        row_copies.append(pltpu.make_async_copy(ref, target, row_sems.at[index]))
+        first += ref.shape[0]
+    piece = kv_refs[0].shape[0]
+    kv_copies = [
+        pltpu.make_async_copy(ref, kv_buf.at[pl.ds((place ^ k) * piece, piece)], kv_sems.at[k])
+        for k, ref in enumerate(kv_refs)
+    ]
+    for copy in row_copies:
+        copy.start()
+    for slot in range(GROUP):
+        begin_block(gate_refs, gate_buf, gate_sems, slot, place ^ slot, rep)
+        begin_block(up_refs, up_buf, up_sems, slot, place ^ slot, rep)
+    for slot in range(2):
+        begin_block(down_refs, down_buf, down_sems, slot, core ^ slot, rep)
+    for copy in kv_copies:
+        copy.start()
+    for copy in row_copies:
+        copy.wait()
+
+    features, units = gate_buf.shape[1:]
+    terms = rows_buf[:, features:].astype(jnp.float32)
+    lane = lax.broadcasted_iota(jnp.int32, terms.shape, 1)
+    own = (lane >= 3 * plane) & (lane < 3 * plane + 3)
+    scale_ref[...] = jnp.sum(jnp.where(own, terms, 0.0), axis=1, keepdims=True)
+
+    for slot in range(GROUP):
+        await_block(gate_buf, gate_sems, slot, place ^ slot)
+        await_block(up_buf, up_sems, slot, place ^ slot)
+        rows = rows_buf[:, :features]
+        gate_part = jnp.dot(rows, gate_buf[slot], preferred_element_type=jnp.float32)
+        up_part = jnp.dot(rows, up_buf[slot], preferred_element_type=jnp.float32)
+        hidden_ref[:, slot * units : (slot + 1) * units] = (
+            gate_part / (1.0 + jnp.exp(-gate_part)) * up_part
+        ).astype(jnp.bfloat16)
+
+    for slot in range(2):
+        await_block(down_buf, down_sems, slot, core ^ slot)
+        weigh_block(hidden_ref, scale_ref, down_buf, slot, part_refs)
+
+    for copy in kv_copies:
+        copy.wait()
+    depth = GROUP * piece
+    columns = pl.ds(pl.multiple_of(plane * depth, 128), depth)
+    latent = jnp.dot(
+        rows_buf[4 * some : 6 * some, columns], kv_buf[...], preferred_element_type=jnp.float32
+    )
+    latent_ref[...] = latent.astype(jnp.bfloat16)
+
+
+def weigh_block(hidden_ref, scale_ref, down_buf, slot, part_refs):
+    out = jnp.dot(hidden_ref[...], down_buf[slot], preferred_element_type=jnp.float32)
+    out = (out.astype(jnp.bfloat16).astype(jnp.float32) * scale_ref[...]).astype(jnp.bfloat16)
+    tok_rows, width = part_refs[0].shape[0], down_buf.shape[2]
+    for index, part_ref in enumerate(part_refs):
+        part_ref[:, slot * width : (slot + 1) * width] = out[
+            index * tok_rows : (index + 1) * tok_rows
+        ]
+
+
+def hidden_units(place, rows, gates, ups, near, kv_parts):
+    some, extended = rows[0].shape
+    features, units = gates[0].shape
+    columns = near[0].shape[1]
+    piece, latent_width = kv_parts[0].shape
+    hbm, vmem = pl.BlockSpec(memory_space=pltpu.HBM), pl.BlockSpec(memory_space=pltpu.VMEM)
+    bf16, dma = jnp.bfloat16, pltpu.SemaphoreType.DMA
+    operands = (*rows, *gates, *ups, *near, *kv_parts)
+    return pl.pallas_call(
+        hidden_kernel,
+        out_shape=[
+            jax.ShapeDtypeStruct((2 * LINE * some, GROUP * units), bf16),
+            jax.ShapeDtypeStruct((2 * LINE * some, 1), jnp.float32),
+            jax.ShapeDtypeStruct((2 * some, latent_width), bf16),
+        ]
+        + [jax.ShapeDtypeStruct((2 * some, 2 * columns), bf16)] * LINE,
+        in_specs=[pl.BlockSpec(memory_space=pltpu.SMEM)] + [hbm] * len(operands),
+        out_specs=[vmem] * (3 + LINE),
+        scratch_shapes=[
+            pltpu.VMEM((2 * LINE * some, extended), bf16),
+            pltpu.VMEM((GROUP, features, units), bf16),
+            pltpu.VMEM((GROUP, features, units), bf16),
+            pltpu.VMEM((2, GROUP * units, columns), bf16),
+            pltpu.VMEM((GROUP * piece, latent_width), bf16),
+            dma((len(rows),)),
+            dma((GROUP,)),
+            dma((GROUP,)),
+            dma((2,)),
+            dma((GROUP,)),
+        ],
+        compiler_params=pltpu.CompilerParams(vmem_limit_bytes=VMEM_GRANT),
+        cost_estimate=BRIEF,
+        name="hidden_units",
+    )(place, *operands)
+
+
+def far_kernel(place_ref, hidden_ref, scale_ref, *refs):
+    down_refs, part_refs, down_buf, sems = refs[:4], refs[4:-2], refs[-2], refs[-1]
+    core, rep = place_ref[0] & 1, place_ref[1]
+    for slot in range(2):
+        begin_block(down_refs, down_buf, sems, slot, core ^ slot, rep)
+    for slot in range(2):
+        await_block(down_buf, sems, slot, core ^ slot)
+        weigh_block(hidden_ref, scale_ref, down_buf, slot, part_refs)
+
+
+def far_products(place, hidden, scale, downs):
+    tok_rows, units, width = hidden.shape[0] // LINE, hidden.shape[1], downs[0].shape[1]
+    hbm, vmem = pl.BlockSpec(memory_space=pltpu.HBM), pl.BlockSpec(memory_space=pltpu.VMEM)
+    return pl.pallas_call(
+        far_kernel,
+        out_shape=[jax.ShapeDtypeStruct((tok_rows, 2 * width), jnp.bfloat16)] * LINE,
+        in_specs=[pl.BlockSpec(memory_space=pltpu.SMEM), vmem, vmem] + [hbm] * len(downs),
+        out_specs=[vmem] * LINE,
+        scratch_shapes=[
+            pltpu.VMEM((2, units, width), jnp.bfloat16),
+            pltpu.SemaphoreType.DMA((2,)),
+        ],
+        compiler_params=pltpu.CompilerParams(vmem_limit_bytes=VMEM_GRANT),
+        cost_estimate=BRIEF,
+        name="far_products",
+    )(place, hidden, scale, *downs)
+
+
+def dense_shards(
+    tokens,
+    norm_gain,
+    kv_weight,
+    key_value_gain,
+    gate_weight,
+    up_weight,
+    down_weight,
+    expert_index,
+    route_gate,
+    owner,
+):
+    device_count = lax.axis_size("dev")
+    push_cap = max(2, 2 * tokens.shape[0] // device_count)
+    own_index = lax.axis_index("dev")
+    plane, place = own_index // GROUP, own_index % GROUP
+    place_info = jnp.stack([place, lax.axis_index("rep"), plane]).astype(jnp.int32)
+    hold = lax.optimization_barrier
+
+    def exchange(value, distance):
+        return lax.ppermute(value, "dev", [(i, i ^ distance) for i in range(device_count)])
+
+    def across_line(value, k):
+        return exchange(value, GROUP * k)
+
+    def other_core(value):
+        return exchange(value, 1)
+
+    def other_chip(value):
+        return exchange(value, 2)
+
+    def other_rep(value):
+        return lax.ppermute(value, "rep", [(0, 1), (1, 0)])
+
+    def narrow(value):
+        return value.astype(jnp.bfloat16)
+
+    def wide(value):
+        return value.astype(jnp.float32)
+
+    gate_core, up_core = other_core(gate_weight), other_core(up_weight)
+    kv_parts = tuple(exchange(kv_weight, distance) for distance in range(1, GROUP))
+    rows0, rows1, gate_half = entry(
+        place_info, tokens, norm_gain, expert_index, route_gate, gate_weight
+    )
+    rows0, gate_half, gate_core, kv_parts = hold((rows0, gate_half, gate_core, kv_parts))
+    kv_parts = (kv_weight, *kv_parts)
+
+    f0, a0 = across_line(rows0, 3), across_line(rows0, 1)
+    gate_x = other_chip(gate_half)
+    down_core = other_core(down_weight)
+    up_half, down_half = halves_of(place_info, up_weight, down_weight)
+    f0, a0, gate_x, up_core, down_core, up_half, down_half, later = hold(
+        (f0, a0, gate_x, up_core, down_core, up_half, down_half, rows1)
+    )
+
+    f1, a1 = across_line(later, 3), across_line(later, 1)
+    gate_y = other_rep(gate_x)
+    up_x = other_chip(up_half)
+    gate_x_core = other_core(gate_x)
+    f0, f1, a1, gate_y, up_x, gate_x_core, down_half = hold(
+        (f0, f1, a1, gate_y, up_x, gate_x_core, down_half)
+    )
+
+    c = across_line(jnp.concatenate([f0, f1]), 1)
+    up_y = other_rep(up_x)
+    down_x = other_chip(down_half)
+    latent0, latent1, latent3 = latent_parts(
+        place_info, (rows0, later, a0, a1, f0, f1), kv_parts
+    )
+    gate_y_core, up_x_core = other_core(gate_y), other_core(up_x)
+    c, up_y, down_x, gate_y_core, up_x_core, latent1, latent3 = hold(
+        (c, up_y, down_x, gate_y_core, up_x_core, latent1, latent3)
+    )
+
+    up_y_core = other_core(up_y)
+    down_y, down_x_core = other_rep(down_x), other_core(down_x)
+    latent1, latent3 = across_line(latent1, 1), across_line(latent3, 3)
+    hidden, scale, latent2, near0, near1, near2, near3 = hidden_units(
+        place_info,
+        (rows0, later, a0, a1, c, f0, f1),
+        (gate_weight, gate_core, gate_x, gate_y, gate_x_core, gate_y_core),
+        (up_weight, up_core, up_x, up_y, up_x_core, up_y_core),
+        (down_weight, down_core),
+        kv_parts,
+    )
+    hidden, near2, latent1, latent3, down_y, down_x_core = hold(
+        (hidden, near2, latent1, latent3, down_y, down_x_core)
+    )
+    near2_there = across_line(near2, 1)
+    down_y_core = other_core(down_y)
+    far0, far1, far2, far3 = far_products(
+        place_info, hidden, scale, (down_x, down_y, down_x_core, down_y_core)
+    )
+    far2_there = across_line(far2, 1)
+    near2_there, far2, latent2 = hold((near2_there, far2, latent2))
+    near_sum = narrow(wide(near3) + wide(near2_there))
+    near_sum, near1 = hold((near_sum, near1))
+    near3_there, near1_there = across_line(near_sum, 3), across_line(near1, 1)
+    latent2 = across_line(latent2, 2)
+    far_sum = narrow(wide(far3) + wide(far2_there))
+    far3_there, far1_there = across_line(far_sum, 3), across_line(far1, 1)
+    raw_latent = wide(latent0) + wide(latent1) + wide(latent2) + wide(latent3)
+    near = narrow(wide(near0) + wide(near1_there) + wide(near3_there))
+    far = narrow(wide(far0) + wide(far1_there) + wide(far3_there))
+    moe_out = jnp.where(
+        place & 2 == 2,
+        jnp.concatenate([far, near], axis=1),
+        jnp.concatenate([near, far], axis=1),
+    )
+
+    send_rows = cache_send_rows(
+        latent_rows(raw_latent, key_value_gain), owner, device_count, push_cap
     )
     latent_cache = lax.all_to_all(send_rows, "dev", split_axis=0, concat_axis=0, tiled=True)
     return (moe_out, latent_cache)
@@ -150,4 +575,6 @@
         P(("rep", "dev"), None),
     )
     out_specs = (P(("rep", "dev"), None), P(("rep", "dev"), None))
+    dense = mesh.shape["dev"] == LINE * GROUP and mesh.shape["rep"] == 2
+    shards = dense_shards if dense else packed_shards
     return jax.shard_map(shards, mesh=mesh, in_specs=in_specs, out_specs=out_specs, check_vma=False)

time: 610 us -> 198 us (0.32)
  the two profiles are of different devices: /device:TPU:15 before, /device:TPU:0 now
where the time goes in v2:
time: 198 us; the launch traced here: 197 us
  waiting for transfers between devices  104 us (53%)
  starting transfers between devices  41.9 us (21%)
  Pallas kernels  37.4 us (19%)
  other arithmetic  7.86 us (4%)
  local copies, waits for them, and re-layouts  5.06 us (3%)
    ppermute x29, waiting for transfers between devices, exchange(): lax.ppermute(value, 'dev', [(i, i ^ distance) for i in range(device_count)])  78.2 us
    ppermute x29, starting transfers between devices, exchange(): lax.ppermute(value, 'dev', [(i, i ^ distance) for i in range(device_count)])  32.6 us
    pallas_call x1, Pallas kernels, hidden_units(): pl.pallas_call(hidden_kernel, out_shape=[jax.ShapeDtypeStruct((2 * LINE *...  19.9 us
    ppermute x3, waiting for transfers between devices, other_rep(): return lax.ppermute(value, 'rep', [(0, 1), (1, 0)])  15.1 us
    all_to_all x1, waiting for transfers between devices, dense_shards(): lax.all_to_all(send_rows, 'dev', split_axis=0, concat_axis=0, tiled=True)  10.5 us
    pallas_call x1, Pallas kernels, far_products(): pl.pallas_call(far_kernel, out_shape=[jax.ShapeDtypeStruct((tok_rows, 2 *...  6.67 us
    all_to_all x1, starting transfers between devices, dense_shards(): lax.all_to_all(send_rows, 'dev', split_axis=0, concat_axis=0, tiled=True)  5.72 us
    unnamed x57, local copies, waits for them, and re-layouts  5.06 us
  transfers between devices with their start and end apart: 33, of which 13 were waited for; matrix products, arithmetic and copies ran while one was open for 4% of the time, Pallas kernels for 19%

profile of v2, /device:TPU:0, one launch (start us, length us, event | category | flops | bytes accessed | tf_op | source)
XLA Modules:
  0.0 197.1 jit_solution(12577263822232689309)
XLA Ops:
  0.6 0.5 collective-permute-start
  1.1 0.1 collective-permute-start.7
  1.2 0.4 collective-permute-start.8
  1.7 0.1 collective-permute-start.1
  1.7 2.9 %collective-permute-start.2 = (bf16[224,576]{1,0:T(8,128)(2,1)}, bf16[224,576]{1,0:T(8,128)(2,1)S(1)}, u32[]{:S(2)}, u32[]{:S(2)}) collective-permute-start(bf16[224,576]{1,0:T(8,128)(2,1)} %refs_21_.1), channel_id=1, source_target_pairs={{0,2},{1,3},{2,0},{3,1},{4,6},{5,7},{6,4},{7,5},{8,10},{9,11},{10,... | collective-permute-start | bytes 774152 | tf_op jit(solution)/shard_map/ppermute | solution.py:466
  4.7 2.7 %collective-permute-done.1.refs_7_.refs_22_ = bf16[224,576]{1,0:T(8,128)(2,1)S(1)} collective-permute-done((bf16[224,576]{1,0:T(8,128)(2,1)}, bf16[224,576]{1,0:T(8,128)(2,1)S(1)}, u32[]{:S(2)}, u32[]{:S(2)}) %collective-permute-start.1) | collective-permute-done | bytes 258080 | tf_op jit(solution)/shard_map/ppermute | solution.py:466
  7.4 2.6 %collective-permute-start.3 = (bf16[224,576]{1,0:T(8,128)(2,1)}, bf16[224,576]{1,0:T(8,128)(2,1)S(1)}, u32[]{:S(2)}, u32[]{:S(2)}) collective-permute-start(bf16[224,576]{1,0:T(8,128)(2,1)} %refs_21_.1), channel_id=1, source_target_pairs={{0,3},{1,2},{2,1},{3,0},{4,7},{5,6},{6,5},{7,4},{8,11},{9,10},{10,... | collective-permute-start | bytes 774152 | tf_op jit(solution)/shard_map/ppermute | solution.py:466
  10.0 0.6 pad_add_fusion.place_ref
  10.6 3.6 %entry.1 = (bf16[64,3712]{1,0:T(8,128)(2,1)}, bf16[64,3712]{1,0:T(8,128)(2,1)}, bf16[1792,256]{1,0:T(8,128)(2,1)}) custom-call(s32[3]{0:T(128)} %pad_add_fusion.place_ref, bf16[128,3584]{1,0:T(8,128)(2,1)} %tokens_ref.1, f32[28,128]{1,0:T(8,128)} %bitcast.16, s32[2,128]{1,0:T(2,128)} %bitcast.19, f32[2,128]{1,0:T(2,128)} %bitcast.20, bf16[3584,256]{1,0:T(8,128)(2,1)} %refs_7_.1), custom_call_target="tpu_custom_call" | custom-call | flops 1048576 | bytes 1048576 | tf_op jit(solution)/shard_map/entry/pallas_call | solution.py:196
  14.3 3.4 %collective-permute-done.3.refs_9_.refs_24_ = bf16[224,576]{1,0:T(8,128)(2,1)S(1)} collective-permute-done((bf16[224,576]{1,0:T(8,128)(2,1)}, bf16[224,576]{1,0:T(8,128)(2,1)S(1)}, u32[]{:S(2)}, u32[]{:S(2)}) %collective-permute-start.3) | collective-permute-done | bytes 258080 | tf_op jit(solution)/shard_map/ppermute | solution.py:466
  17.7 0.7 copy-done.8
  18.4 2.0 %collective-permute-start.6 = (bf16[1792,256]{1,0:T(8,128)(2,1)}, bf16[1792,256]{1,0:T(8,128)(2,1)}, u32[]{:S(2)}, u32[]{:S(2)}) collective-permute-start(bf16[1792,256]{1,0:T(8,128)(2,1)} %get-tuple-element.62), channel_id=1, source_target_pairs={{0,2},{1,3},{2,0},{3,1},{4,6},{5,7},{6,4},{7,5},{8,10},{9,11},{10,... | collective-permute-start | bytes 2752520 | tf_op jit(solution)/shard_map/ppermute | solution.py:466
  20.4 3.6 %collective-permute-start.4 = (bf16[64,3712]{1,0:T(8,128)(2,1)}, bf16[64,3712]{1,0:T(8,128)(2,1)S(1)}, u32[]{:S(2)}, u32[]{:S(2)}) collective-permute-start(bf16[64,3712]{1,0:T(8,128)(2,1)} %get-tuple-element.61.refs_0_), channel_id=1, source_target_pairs={{0,12},{1,13},{2,14},{3,15},{4,8},{5,9},{6,10},{7,11},{8,4},{9,5},... | collective-permute-start | bytes 1425416 | tf_op jit(solution)/shard_map/ppermute | solution.py:466
  24.0 3.4 %weight_halves.1 = (bf16[1792,256]{1,0:T(8,128)(2,1)}, bf16[512,896]{1,0:T(8,128)(2,1)}) custom-call(s32[3]{0:T(128)} %pad_add_fusion.place_ref, bf16[3584,256]{1,0:T(8,128)(2,1)} %refs_13_.1, bf16[1024,896]{1,0:T(8,128)(2,1)} %refs_19_.1), custom_call_target="tpu_custom_call" | custom-call | flops 1048576 | bytes 1048576 | tf_op jit(solution)/shard_map/weight_halves/pallas_call | solution.py:230
  27.4 8.7 %collective-permute-done.4.refs_4_.refs_5_ = bf16[64,3712]{1,0:T(8,128)(2,1)S(1)} collective-permute-done((bf16[64,3712]{1,0:T(8,128)(2,1)}, bf16[64,3712]{1,0:T(8,128)(2,1)S(1)}, u32[]{:S(2)}, u32[]{:S(2)}) %collective-permute-start.4) | collective-permute-done | bytes 475168 | tf_op jit(solution)/shard_map/ppermute | solution.py:466
  36.2 9.2 %collective-permute-done.5.refs_2_ = bf16[64,3712]{1,0:T(8,128)(2,1)S(1)} collective-permute-done((bf16[64,3712]{1,0:T(8,128)(2,1)}, bf16[64,3712]{1,0:T(8,128)(2,1)S(1)}, u32[]{:S(2)}, u32[]{:S(2)}) %collective-permute-start.5) | collective-permute-done | bytes 475168 | tf_op jit(solution)/shard_map/ppermute | solution.py:466
  45.4 1.5 collective-permute-start.11
  46.9 0.5 collective-permute-start.12
  47.4 1.7 collective-permute-start.10
  49.1 0.5 collective-permute-start.9
  49.6 11.4 %collective-permute-done.10.refs_3_ = bf16[64,3712]{1,0:T(8,128)(2,1)S(1)} collective-permute-done((bf16[64,3712]{1,0:T(8,128)(2,1)S(1)}, bf16[64,3712]{1,0:T(8,128)(2,1)S(1)}, u32[]{:S(2)}, u32[]{:S(2)}) %collective-permute-start.10) | collective-permute-done | bytes 475168 | tf_op jit(solution)/shard_map/ppermute | solution.py:466
  60.9 10.2 %collective-permute-done.9.refs_5_.refs_6_ = bf16[64,3712]{1,0:T(8,128)(2,1)S(1)} collective-permute-done((bf16[64,3712]{1,0:T(8,128)(2,1)S(1)}, bf16[64,3712]{1,0:T(8,128)(2,1)S(1)}, u32[]{:S(2)}, u32[]{:S(2)}) %collective-permute-start.9) | collective-permute-done | bytes 475168 | tf_op jit(solution)/shard_map/ppermute | solution.py:466
  71.2 0.1 pad_maximum_fusion
  71.2 1.6 collective-permute-start.14
  72.8 0.5 collective-permute-start.15
  73.3 1.5 collective-permute-start.16
  74.8 0.5 collective-permute-start.18
  75.3 3.8 %latent_parts.1 = (bf16[128,576]{1,0:T(8,128)(2,1)}, bf16[128,576]{1,0:T(8,128)(2,1)}, bf16[128,576]{1,0:T(8,128)(2,1)}) custom-call(s32[3]{0:T(128)} %pad_add_fusion.place_ref, bf16[64,3712]{1,0:T(8,128)(2,1)} %get-tuple-element.61.refs_0_, bf16[64,3712]{1,0:T(8,128)(2,1)} %get-tuple-element.66.refs_1_, bf16[64,3712]{1,0:T(8,128)(2,1)} %copy-done.3, ...), custom_call_target="tpu_custom_call" | custom-call | flops 1048576 | bytes 1048576 | tf_op jit(solution)/shard_map/latent_parts/pallas_call | solution.py:294
  79.2 15.1 %collective-permute-done.15.refs_16_ = bf16[1792,256]{1,0:T(8,128)(2,1)} collective-permute-done((bf16[1792,256]{1,0:T(8,128)(2,1)S(1)}, bf16[1792,256]{1,0:T(8,128)(2,1)}, u32[]{:S(2)}, u32[]{:S(2)}) %collective-permute-start.15) | collective-permute-done | bytes 917536 | tf_op jit(solution)/shard_map/ppermute | solution.py:478
  94.3 0.3 collective-permute-done.16.refs_0_
  94.8 0.9 copy-done.16
  95.6 1.5 collective-permute-start.22
  97.1 0.8 collective-permute-start.20
  97.9 3.3 %collective-permute-start.21 = (bf16[128,576]{1,0:T(8,128)(2,1)}, bf16[128,576]{1,0:T(8,128)(2,1)S(1)}, u32[]{:S(2)}, u32[]{:S(2)}) collective-permute-start(bf16[128,576]{1,0:T(8,128)(2,1)} %get-tuple-element.94), channel_id=1, source_target_pairs={{0,12},{1,13},{2,14},{3,15},{4,8},{5,9},{6,10},{7,11},{8,4},{9,5},... | collective-permute-start | bytes 442376 | tf_op jit(solution)/shard_map/ppermute | solution.py:466
  101.2 1.0 copy-done.17
  102.2 19.9 %hidden_units.1 = (bf16[512,1024]{1,0:T(8,128)(2,1)}, f32[512,1]{1,0:T(8,128)}, bf16[128,576]{1,0:T(8,128)(2,1)}, bf16[128,1792]{1,0:T(8,128)(2,1)}, bf16[128,17...) custom-call(s32[3]{0:T(128)} %pad_add_fusion.place_ref, ...), custom_call_target="tpu_custom_call" | custom-call | flops 1048576 | bytes 1048576 | tf_op jit(solution)/shard_map/hidden_units/pallas_call | solution.py:390
  122.2 0.6 copy-done.23
  122.8 1.0 collective-permute-start.24
  123.8 0.1 fusion.15
  124.0 0.2 reduce_window_sum.11
  124.2 0.2 select_reduce_fusion
  124.4 1.5 collective-permute-done.24.refs_3_
  125.9 0.9 copy-done.13
  126.9 6.7 %far_products.1 = (bf16[128,1792]{1,0:T(8,128)(2,1)}, bf16[128,1792]{1,0:T(8,128)(2,1)}, bf16[128,1792]{1,0:T(8,128)(2,1)}, bf16[128,1792]{1,0:T(8,128)(2,1)}) custom-call(s32[3]{0:T(128)} %pad_add_fusion.place_ref, bf16[512,1024]{1,0:T(8,128)(2,1)} %get-tuple-element.96.hidden_ref, f32[512,1]{1,0:T(8,128)} %get-tuple-element.97.scale_ref, ...), custom_call_target="tpu_custom_call" | custom-call | flops 1048576 | bytes 1048576 | tf_op jit(solution)/shard_map/far_products/pallas_call | solution.py:431
  133.6 0.5 collective-permute-start.26
  134.1 2.6 %collective-permute-done.28 = bf16[128,1792]{1,0:T(8,128)(2,1)} collective-permute-done((bf16[128,1792]{1,0:T(8,128)(2,1)}, bf16[128,1792]{1,0:T(8,128)(2,1)}, u32[]{:S(2)}, u32[]{:S(2)}) %collective-permute-start.28) | collective-permute-done | bytes 458784 | tf_op jit(solution)/shard_map/ppermute | solution.py:466
  136.7 1.1 collective-permute-start.25
  137.8 1.9 add_convert_fusion.1
  139.7 0.9 collective-permute-start.29
  140.6 2.6 %collective-permute-start.30 = (bf16[128,1792]{1,0:T(8,128)(2,1)}, bf16[128,1792]{1,0:T(8,128)(2,1)S(1)}, u32[]{:S(2)}, u32[]{:S(2)}) collective-permute-start(bf16[128,1792]{1,0:T(8,128)(2,1)} %add_convert_fusion.1), channel_id=1, source_target_pairs={{0,12},{1,13},{2,14},{3,15},{4,8},{5,9},{6,10},{7,11},{8,4},{9,5},... | collective-permute-start | bytes 1376264 | tf_op jit(solution)/shard_map/ppermute | solution.py:466
  143.3 5.5 %collective-permute-done.31 = bf16[128,576]{1,0:T(8,128)(2,1)S(1)} collective-permute-done((bf16[128,576]{1,0:T(8,128)(2,1)S(1)}, bf16[128,576]{1,0:T(8,128)(2,1)S(1)}, u32[]{:S(2)}, u32[]{:S(2)}) %collective-permute-start.31) | collective-permute-done | bytes 147488 | tf_op jit(solution)/shard_map/ppermute | solution.py:466
  148.8 0.3 fusion.12
  149.2 0.1 multiply_reduce_fusion
  149.3 0.1 multiply_convert_fusion
  149.4 1.9 scatter_custom_fusion
  151.3 5.7 %all-to-all-start = ((bf16[16,16,576]{2,1,0:T(8,128)(2,1)}), bf16[16,16,576]{2,1,0:T(8,128)(2,1)S(1)}, u32[]{:S(2)}, u32[]{:S(2)}) async-start(bf16[16,16,576]{2,1,0:T(8,128)(2,1)} %bitcast.9), calls=%async_computation | async-start | bytes 655360 | tf_op jit(solution)/shard_map/all_to_all | solution.py:560
  157.1 0.9 add_convert_fusion.3
  157.9 3.7 %collective-permute-start.27 = (bf16[128,1792]{1,0:T(8,128)(2,1)}, bf16[128,1792]{1,0:T(8,128)(2,1)S(1)}, u32[]{:S(2)}, u32[]{:S(2)}) collective-permute-start(bf16[128,1792]{1,0:T(8,128)(2,1)} %add_convert_fusion.3), channel_id=1, source_target_pairs={{0,12},{1,13},{2,14},{3,15},{4,8},{5,9},{6,10},{7,11},{8,4},{9,5},... | collective-permute-start | bytes 1376264 | tf_op jit(solution)/shard_map/ppermute | solution.py:466
  161.6 22.6 %collective-permute-done.29 = bf16[128,1792]{1,0:T(8,128)(2,1)S(1)} collective-permute-done((bf16[128,1792]{1,0:T(8,128)(2,1)}, bf16[128,1792]{1,0:T(8,128)(2,1)S(1)}, u32[]{:S(2)}, u32[]{:S(2)}) %collective-permute-start.29) | collective-permute-done | bytes 458784 | tf_op jit(solution)/shard_map/ppermute | solution.py:466
  184.2 0.2 add_convert_fusion
  184.4 10.5 %all-to-all-done = bf16[16,16,576]{2,1,0:T(8,128)(2,1)S(1)} async-done(((bf16[16,16,576]{2,1,0:T(8,128)(2,1)}), bf16[16,16,576]{2,1,0:T(8,128)(2,1)S(1)}, u32[]{:S(2)}, u32[]{:S(2)}) %all-to-all-start) | async-done | bytes 294944 | tf_op jit(solution)/shard_map/all_to_all | solution.py:560
  194.9 0.9 copy.14
  195.8 0.2 add_convert_fusion.2
  196.0 1.1 maximum_select_fusion
  (83 shorter events, 0.4 us)
Async XLA Ops:
  0.6 17.0 %collective-permute-start = (bf16[3584,256]{1,0:T(8,128)(2,1)}, bf16[3584,256]{1,0:T(8,128)(2,1)S(1)}, u32[]{:S(2)}, u32[]{:S(2)}) collective-permute-start(bf16[3584,256]{1,0:T(8,128)(2,1)} %refs_7_.1), channel_id=1, source_target_pairs={{0,1},{1,0},{2,3},{3,2},{4,5},{5,4},{6,7},{7,6},{8,9},{9,8},{10,11... | collective-permute-start | bytes 5505032 | tf_op jit(solution)/shard_map/ppermute | solution.py:466
  1.1 26.3 %collective-permute-start.7 = (bf16[3584,256]{1,0:T(8,128)(2,1)}, bf16[3584,256]{1,0:T(8,128)(2,1)}, u32[]{:S(2)}, u32[]{:S(2)}) collective-permute-start(bf16[3584,256]{1,0:T(8,128)(2,1)} %refs_13_.1), channel_id=1, source_target_pairs={{0,1},{1,0},{2,3},{3,2},{4,5},{5,4},{6,7},{7,6},{8,9},{9,8},{10,11... | collective-permute-start | bytes 5505032 | tf_op jit(solution)/shard_map/ppermute | solution.py:466
  1.2 26.2 %collective-permute-start.8 = (bf16[1024,896]{1,0:T(8,128)(2,1)}, bf16[1024,896]{1,0:T(8,128)(2,1)}, u32[]{:S(2)}, u32[]{:S(2)}) collective-permute-start(bf16[1024,896]{1,0:T(8,128)(2,1)} %refs_19_.1), channel_id=1, source_target_pairs={{0,1},{1,0},{2,3},{3,2},{4,5},{5,4},{6,7},{7,6},{8,9},{9,8},{10,11... | collective-permute-start | bytes 5505032 | tf_op jit(solution)/shard_map/ppermute | solution.py:466
  1.7 5.7 %collective-permute-start.1 = (bf16[224,576]{1,0:T(8,128)(2,1)}, bf16[224,576]{1,0:T(8,128)(2,1)S(1)}, u32[]{:S(2)}, u32[]{:S(2)}) collective-permute-start(bf16[224,576]{1,0:T(8,128)(2,1)} %refs_21_.1), channel_id=1, source_target_pairs={{0,1},{1,0},{2,3},{3,2},{4,5},{5,4},{6,7},{7,6},{8,9},{9,8},{10,11... | collective-permute-start | bytes 774152 | tf_op jit(solution)/shard_map/ppermute | solution.py:466
  1.7 12.5 %collective-permute-start.2 = (bf16[224,576]{1,0:T(8,128)(2,1)}, bf16[224,576]{1,0:T(8,128)(2,1)S(1)}, u32[]{:S(2)}, u32[]{:S(2)}) collective-permute-start(bf16[224,576]{1,0:T(8,128)(2,1)} %refs_21_.1), channel_id=1, source_target_pairs={{0,2},{1,3},{2,0},{3,1},{4,6},{5,7},{6,4},{7,5},{8,10},{9,11},{10,... | collective-permute-start | bytes 774152 | tf_op jit(solution)/shard_map/ppermute | solution.py:466
  7.4 20.0 %copy-start.6 = (bf16[224,576]{1,0:T(8,128)(2,1)}, bf16[224,576]{1,0:T(8,128)(2,1)S(1)}, u32[]{:S(2)}) copy-start(bf16[224,576]{1,0:T(8,128)(2,1)S(1)} %collective-permute-done.1.refs_7_.refs_22_) | copy-start | bytes 774148
  7.4 10.3 %collective-permute-start.3 = (bf16[224,576]{1,0:T(8,128)(2,1)}, bf16[224,576]{1,0:T(8,128)(2,1)S(1)}, u32[]{:S(2)}, u32[]{:S(2)}) collective-permute-start(bf16[224,576]{1,0:T(8,128)(2,1)} %refs_21_.1), channel_id=1, source_target_pairs={{0,3},{1,2},{2,1},{3,0},{4,7},{5,6},{6,5},{7,4},{8,11},{9,10},{10,... | collective-permute-start | bytes 774152 | tf_op jit(solution)/shard_map/ppermute | solution.py:466
  14.3 4.1 %copy-start.7 = (bf16[224,576]{1,0:T(8,128)(2,1)}, bf16[224,576]{1,0:T(8,128)(2,1)S(1)}, u32[]{:S(2)}) copy-start(bf16[224,576]{1,0:T(8,128)(2,1)S(1)} %collective-permute-done.2.refs_8_.refs_23_) | copy-start | bytes 774148
  17.7 0.7 copy-start.8
  17.7 9.7 %copy-start.5 = (bf16[3584,256]{1,0:T(8,128)(2,1)}, bf16[3584,256]{1,0:T(8,128)(2,1)S(1)}, u32[]{:S(2)}) copy-start(bf16[3584,256]{1,0:T(8,128)(2,1)S(1)} %collective-permute-done.refs_8_) | copy-start | bytes 5505028
  18.4 29.0 %copy-start.2 = (bf16[64,3712]{1,0:T(8,128)(2,1)S(1)}, bf16[64,3712]{1,0:T(8,128)(2,1)}, u32[]{:S(2)}) copy-start(bf16[64,3712]{1,0:T(8,128)(2,1)} %get-tuple-element.66.refs_1_) | copy-start | bytes 1425412
  18.4 27.0 %collective-permute-start.6 = (bf16[1792,256]{1,0:T(8,128)(2,1)}, bf16[1792,256]{1,0:T(8,128)(2,1)}, u32[]{:S(2)}, u32[]{:S(2)}) collective-permute-start(bf16[1792,256]{1,0:T(8,128)(2,1)} %get-tuple-element.62), channel_id=1, source_target_pairs={{0,2},{1,3},{2,0},{3,1},{4,6},{5,7},{6,4},{7,5},{8,10},{9,11},{10,... | collective-permute-start | bytes 2752520 | tf_op jit(solution)/shard_map/ppermute | solution.py:466
  20.4 15.8 %collective-permute-start.4 = (bf16[64,3712]{1,0:T(8,128)(2,1)}, bf16[64,3712]{1,0:T(8,128)(2,1)S(1)}, u32[]{:S(2)}, u32[]{:S(2)}) collective-permute-start(bf16[64,3712]{1,0:T(8,128)(2,1)} %get-tuple-element.61.refs_0_), channel_id=1, source_target_pairs={{0,12},{1,13},{2,14},{3,15},{4,8},{5,9},{6,10},{7,11},{8,4},{9,5},... | collective-permute-start | bytes 1425416 | tf_op jit(solution)/shard_map/ppermute | solution.py:466
  24.0 21.4 %collective-permute-start.5 = (bf16[64,3712]{1,0:T(8,128)(2,1)}, bf16[64,3712]{1,0:T(8,128)(2,1)S(1)}, u32[]{:S(2)}, u32[]{:S(2)}) collective-permute-start(bf16[64,3712]{1,0:T(8,128)(2,1)} %get-tuple-element.61.refs_0_), channel_id=1, source_target_pairs={{0,4},{1,5},{2,6},{3,7},{4,0},{5,1},{6,2},{7,3},{8,12},{9,13},{10,... | collective-permute-start | bytes 1425416 | tf_op jit(solution)/shard_map/ppermute | solution.py:466
  36.2 39.1 %copy-start = (bf16[64,3712]{1,0:T(8,128)(2,1)}, bf16[64,3712]{1,0:T(8,128)(2,1)S(1)}, u32[]{:S(2)}) copy-start(bf16[64,3712]{1,0:T(8,128)(2,1)S(1)} %collective-permute-done.4.refs_4_.refs_5_) | copy-start | bytes 1425412
  45.3 30.0 %copy-start.3 = (bf16[64,3712]{1,0:T(8,128)(2,1)}, bf16[64,3712]{1,0:T(8,128)(2,1)S(1)}, u32[]{:S(2)}) copy-start(bf16[64,3712]{1,0:T(8,128)(2,1)S(1)} %collective-permute-done.5.refs_2_) | copy-start | bytes 1425412
  45.4 25.8 %collective-permute-start.11 = (bf16[1792,256]{1,0:T(8,128)(2,1)}, bf16[1792,256]{1,0:T(8,128)(2,1)S(1)}, u32[]{:S(2)}, u32[]{:S(2)}) collective-permute-start(bf16[1792,256]{1,0:T(8,128)(2,1)} %collective-permute-done.6.refs_9_), channel_id=1, source_target_pairs={{0,16},{16,0},{1,17},{17,1},{2,18},{18,2},{3,19},{19,3},{4,20},{20... | collective-permute-start | bytes 2752520 | tf_op jit(solution)/shard_map/ppermute | solution.py:478
  46.9 24.3 %collective-permute-start.12 = (bf16[1792,256]{1,0:T(8,128)(2,1)}, bf16[1792,256]{1,0:T(8,128)(2,1)S(1)}, u32[]{:S(2)}, u32[]{:S(2)}) collective-permute-start(bf16[1792,256]{1,0:T(8,128)(2,1)} %get-tuple-element.70), channel_id=1, source_target_pairs={{0,2},{1,3},{2,0},{3,1},{4,6},{5,7},{6,4},{7,5},{8,10},{9,11},{10,... | collective-permute-start | bytes 2752520 | tf_op jit(solution)/shard_map/ppermute | solution.py:466
  47.4 23.7 %collective-permute-start.13 = (bf16[1792,256]{1,0:T(8,128)(2,1)}, bf16[1792,256]{1,0:T(8,128)(2,1)}, u32[]{:S(2)}, u32[]{:S(2)}) collective-permute-start(bf16[1792,256]{1,0:T(8,128)(2,1)} %collective-permute-done.6.refs_9_), channel_id=1, source_target_pairs={{0,1},{1,0},{2,3},{3,2},{4,5},{5,4},{6,7},{7,6},{8,9},{9,8},{10,11... | collective-permute-start | bytes 2752520 | tf_op jit(solution)/shard_map/ppermute | solution.py:466
  47.4 13.5 %collective-permute-start.10 = (bf16[64,3712]{1,0:T(8,128)(2,1)S(1)}, bf16[64,3712]{1,0:T(8,128)(2,1)S(1)}, u32[]{:S(2)}, u32[]{:S(2)}) collective-permute-start(bf16[64,3712]{1,0:T(8,128)(2,1)S(1)} %copy-done.2), channel_id=1, source_target_pairs={{0,4},{1,5},{2,6},{3,7},{4,0},{5,1},{6,2},{7,3},{8,12},{9,13},{10,... | collective-permute-start | bytes 1425416 | tf_op jit(solution)/shard_map/ppermute | solution.py:466
  49.1 22.0 %collective-permute-start.9 = (bf16[64,3712]{1,0:T(8,128)(2,1)S(1)}, bf16[64,3712]{1,0:T(8,128)(2,1)S(1)}, u32[]{:S(2)}, u32[]{:S(2)}) collective-permute-start(bf16[64,3712]{1,0:T(8,128)(2,1)S(1)} %copy-done.2), channel_id=1, source_target_pairs={{0,12},{1,13},{2,14},{3,15},{4,8},{5,9},{6,10},{7,11},{8,4},{9,5},... | collective-permute-start | bytes 1425416 | tf_op jit(solution)/shard_map/ppermute | solution.py:466
  60.9 14.4 %copy-start.4 = (bf16[64,3712]{1,0:T(8,128)(2,1)}, bf16[64,3712]{1,0:T(8,128)(2,1)S(1)}, u32[]{:S(2)}) copy-start(bf16[64,3712]{1,0:T(8,128)(2,1)S(1)} %collective-permute-done.10.refs_3_) | copy-start | bytes 1425412
  71.1 4.2 %copy-start.1 = (bf16[64,3712]{1,0:T(8,128)(2,1)}, bf16[64,3712]{1,0:T(8,128)(2,1)S(1)}, u32[]{:S(2)}) copy-start(bf16[64,3712]{1,0:T(8,128)(2,1)S(1)} %collective-permute-done.9.refs_5_.refs_6_) | copy-start | bytes 1425412
  71.1 8.0 %copy-start.14 = (bf16[1792,256]{1,0:T(8,128)(2,1)}, bf16[1792,256]{1,0:T(8,128)(2,1)S(1)}, u32[]{:S(2)}) copy-start(bf16[1792,256]{1,0:T(8,128)(2,1)S(1)} %collective-permute-done.11.refs_10_) | copy-start | bytes 2752516
  71.1 8.0 %copy-start.15 = (bf16[1792,256]{1,0:T(8,128)(2,1)}, bf16[1792,256]{1,0:T(8,128)(2,1)S(1)}, u32[]{:S(2)}) copy-start(bf16[1792,256]{1,0:T(8,128)(2,1)S(1)} %collective-permute-done.12.refs_15_) | copy-start | bytes 2752516
  71.2 23.4 %collective-permute-start.14 = (bf16[128,3712]{1,0:T(8,128)(2,1)S(1)}, bf16[128,3712]{1,0:T(8,128)(2,1)S(1)}, u32[]{:S(2)}, u32[]{:S(2)}) collective-permute-start(bf16[128,3712]{1,0:T(8,128)(2,1)S(1)} %pad_maximum_fusion), channel_id=1, source_target_pairs={{0,4},{1,5},{2,6},{3,7},{4,0},{5,1},{6,2},{7,3},{8,12},{9,13},{10,... | collective-permute-start | bytes 2850824 | tf_op jit(solution)/shard_map/ppermute | solution.py:466
  72.8 21.5 %collective-permute-start.15 = (bf16[1792,256]{1,0:T(8,128)(2,1)S(1)}, bf16[1792,256]{1,0:T(8,128)(2,1)}, u32[]{:S(2)}, u32[]{:S(2)}) collective-permute-start(bf16[1792,256]{1,0:T(8,128)(2,1)S(1)} %collective-permute-done.12.refs_15_), channel_id=1, source_target_pairs={{0,16},{16,0},{1,17},{17,1},{2,18},{18,2},{3,19},{19,3},{4,20},{20... | collective-permute-start | bytes 2752520 | tf_op jit(solution)/shard_map/ppermute | solution.py:478
  73.3 21.3 %collective-permute-start.16 = (bf16[512,896]{1,0:T(8,128)(2,1)}, bf16[512,896]{1,0:T(8,128)(2,1)S(1)}, u32[]{:S(2)}, u32[]{:S(2)}) collective-permute-start(bf16[512,896]{1,0:T(8,128)(2,1)} %get-tuple-element.76), channel_id=1, source_target_pairs={{0,2},{1,3},{2,0},{3,1},{4,6},{5,7},{6,4},{7,5},{8,10},{9,11},{10,... | collective-permute-start | bytes 2752520 | tf_op jit(solution)/shard_map/ppermute | solution.py:466
  74.8 19.8 %collective-permute-start.17 = (bf16[1792,256]{1,0:T(8,128)(2,1)S(1)}, bf16[1792,256]{1,0:T(8,128)(2,1)S(1)}, u32[]{:S(2)}, u32[]{:S(2)}) collective-permute-start(bf16[1792,256]{1,0:T(8,128)(2,1)S(1)} %collective-permute-done.11.refs_10_), channel_id=1, source_target_pairs={{0,1},{1,0},{2,3},{3,2},{4,5},{5,4},{6,7},{7,6},{8,9},{9,8},{10,11... | collective-permute-start | bytes 2752520 | tf_op jit(solution)/shard_map/ppermute | solution.py:466
  74.8 19.8 %collective-permute-start.18 = (bf16[1792,256]{1,0:T(8,128)(2,1)S(1)}, bf16[1792,256]{1,0:T(8,128)(2,1)}, u32[]{:S(2)}, u32[]{:S(2)}) collective-permute-start(bf16[1792,256]{1,0:T(8,128)(2,1)S(1)} %collective-permute-done.12.refs_15_), channel_id=1, source_target_pairs={{0,1},{1,0},{2,3},{3,2},{4,5},{5,4},{6,7},{7,6},{8,9},{9,8},{10,11... | collective-permute-start | bytes 2752520 | tf_op jit(solution)/shard_map/ppermute | solution.py:466
  94.6 27.5 %copy-start.10 = (bf16[512,896]{1,0:T(8,128)(2,1)}, bf16[512,896]{1,0:T(8,128)(2,1)S(1)}, u32[]{:S(2)}) copy-start(bf16[512,896]{1,0:T(8,128)(2,1)S(1)} %collective-permute-done.16.refs_0_) | copy-start | bytes 2752516
  94.6 1.0 copy-start.16
  94.7 6.6 %copy-start.9 = (bf16[128,3712]{1,0:T(8,128)(2,1)}, bf16[128,3712]{1,0:T(8,128)(2,1)S(1)}, u32[]{:S(2)}) copy-start(bf16[128,3712]{1,0:T(8,128)(2,1)S(1)} %collective-permute-done.14.refs_4_) | copy-start | bytes 2850820
  94.7 29.1 %copy-start.26 = (s32[128,1]{0,1:T(1,128)S(1)}, s32[128,1]{0,1:T(1,128)}, u32[]{:S(2)}) copy-start(s32[128,1]{0,1:T(1,128)} %param.19) | copy-start | bytes 1540
  94.7 6.5 %collective-permute-start.19 = (bf16[1792,256]{1,0:T(8,128)(2,1)}, bf16[1792,256]{1,0:T(8,128)(2,1)S(1)}, u32[]{:S(2)}, u32[]{:S(2)}) collective-permute-start(bf16[1792,256]{1,0:T(8,128)(2,1)} %collective-permute-done.15.refs_16_), channel_id=1, source_target_pairs={{0,1},{1,0},{2,3},{3,2},{4,5},{5,4},{6,7},{7,6},{8,9},{9,8},{10,11... | collective-permute-start | bytes 2752520 | tf_op jit(solution)/shard_map/ppermute | solution.py:466
  95.6 26.6 %collective-permute-start.22 = (bf16[512,896]{1,0:T(8,128)(2,1)S(1)}, bf16[512,896]{1,0:T(8,128)(2,1)S(1)}, u32[]{:S(2)}, u32[]{:S(2)}) collective-permute-start(bf16[512,896]{1,0:T(8,128)(2,1)S(1)} %collective-permute-done.16.refs_0_), channel_id=1, source_target_pairs={{0,16},{16,0},{1,17},{17,1},{2,18},{18,2},{3,19},{19,3},{4,20},{20... | collective-permute-start | bytes 2752520 | tf_op jit(solution)/shard_map/ppermute | solution.py:478
  97.1 25.1 %collective-permute-start.23 = (bf16[512,896]{1,0:T(8,128)(2,1)S(1)}, bf16[512,896]{1,0:T(8,128)(2,1)S(1)}, u32[]{:S(2)}, u32[]{:S(2)}) collective-permute-start(bf16[512,896]{1,0:T(8,128)(2,1)S(1)} %collective-permute-done.16.refs_0_), channel_id=1, source_target_pairs={{0,1},{1,0},{2,3},{3,2},{4,5},{5,4},{6,7},{7,6},{8,9},{9,8},{10,11... | collective-permute-start | bytes 2752520 | tf_op jit(solution)/shard_map/ppermute | solution.py:466
  97.1 25.0 %collective-permute-start.20 = (bf16[128,576]{1,0:T(8,128)(2,1)}, bf16[128,576]{1,0:T(8,128)(2,1)S(1)}, u32[]{:S(2)}, u32[]{:S(2)}) collective-permute-start(bf16[128,576]{1,0:T(8,128)(2,1)} %get-tuple-element.93), channel_id=1, source_target_pairs={{0,4},{1,5},{2,6},{3,7},{4,0},{5,1},{6,2},{7,3},{8,12},{9,13},{10,... | collective-permute-start | bytes 442376 | tf_op jit(solution)/shard_map/ppermute | solution.py:466
  97.9 24.2 %collective-permute-start.21 = (bf16[128,576]{1,0:T(8,128)(2,1)}, bf16[128,576]{1,0:T(8,128)(2,1)S(1)}, u32[]{:S(2)}, u32[]{:S(2)}) collective-permute-start(bf16[128,576]{1,0:T(8,128)(2,1)} %get-tuple-element.94), channel_id=1, source_target_pairs={{0,12},{1,13},{2,14},{3,15},{4,8},{5,9},{6,10},{7,11},{8,4},{9,5},... | collective-permute-start | bytes 442376 | tf_op jit(solution)/shard_map/ppermute | solution.py:466
  101.2 1.0 copy-start.17
  122.2 0.7 copy-start.23
  122.2 3.7 %copy-start.11 = (bf16[512,896]{1,0:T(8,128)(2,1)}, bf16[512,896]{1,0:T(8,128)(2,1)S(1)}, u32[]{:S(2)}) copy-start(bf16[512,896]{1,0:T(8,128)(2,1)S(1)} %collective-permute-done.22.refs_1_) | copy-start | bytes 2752516
  122.2 3.7 %copy-start.12 = (bf16[512,896]{1,0:T(8,128)(2,1)}, bf16[512,896]{1,0:T(8,128)(2,1)S(1)}, u32[]{:S(2)}) copy-start(bf16[512,896]{1,0:T(8,128)(2,1)S(1)} %collective-permute-done.23.refs_2_) | copy-start | bytes 2752516
  122.8 3.1 %collective-permute-start.24 = (bf16[512,896]{1,0:T(8,128)(2,1)S(1)}, bf16[512,896]{1,0:T(8,128)(2,1)S(1)}, u32[]{:S(2)}, u32[]{:S(2)}) collective-permute-start(bf16[512,896]{1,0:T(8,128)(2,1)S(1)} %collective-permute-done.22.refs_1_), channel_id=1, source_target_pairs={{0,1},{1,0},{2,3},{3,2},{4,5},{5,4},{6,7},{7,6},{8,9},{9,8},{10,11... | collective-permute-start | bytes 2752520 | tf_op jit(solution)/shard_map/ppermute | solution.py:466
  123.9 12.8 %collective-permute-start.28 = (bf16[128,1792]{1,0:T(8,128)(2,1)}, bf16[128,1792]{1,0:T(8,128)(2,1)}, u32[]{:S(2)}, u32[]{:S(2)}) collective-permute-start(bf16[128,1792]{1,0:T(8,128)(2,1)} %get-tuple-element.106), channel_id=1, source_target_pairs={{0,4},{1,5},{2,6},{3,7},{4,0},{5,1},{6,2},{7,3},{8,12},{9,13},{10,... | collective-permute-start | bytes 1376264 | tf_op jit(solution)/shard_map/ppermute | solution.py:466
  125.9 1.0 copy-start.13
  126.9 9.8 %copy-start.27 = (bf16[128,576]{1,0:T(8,128)(2,1)S(1)}, bf16[128,576]{1,0:T(8,128)(2,1)}, u32[]{:S(2)}) copy-start(bf16[128,576]{1,0:T(8,128)(2,1)} %get-tuple-element.114) | copy-start | bytes 442372
  126.9 10.9 %copy-start.20 = (bf16[128,1792]{1,0:T(8,128)(2,1)S(1)}, bf16[128,1792]{1,0:T(8,128)(2,1)}, u32[]{:S(2)}) copy-start(bf16[128,1792]{1,0:T(8,128)(2,1)} %get-tuple-element.105) | copy-start | bytes 1376260
  126.9 21.9 %copy-start.22 = (bf16[128,576]{1,0:T(8,128)(2,1)S(1)}, bf16[128,576]{1,0:T(8,128)(2,1)}, u32[]{:S(2)}) copy-start(bf16[128,576]{1,0:T(8,128)(2,1)} %get-tuple-element.112) | copy-start | bytes 442372
  126.9 21.9 %copy-start.24 = (bf16[128,576]{1,0:T(8,128)(2,1)S(1)}, bf16[128,576]{1,0:T(8,128)(2,1)}, u32[]{:S(2)}) copy-start(bf16[128,576]{1,0:T(8,128)(2,1)} %copy-done.23) | copy-start | bytes 442372
  133.5 15.7 %copy-start.25 = (f32[512]{0:T(512)S(1)}, f32[512]{0:T(512)}, u32[]{:S(2)}) copy-start(f32[512]{0:T(512)} %param.13) | copy-start | bytes 6148
  133.6 23.5 %collective-permute-start.26 = (bf16[128,1792]{1,0:T(8,128)(2,1)}, bf16[128,1792]{1,0:T(8,128)(2,1)S(1)}, u32[]{:S(2)}, u32[]{:S(2)}) collective-permute-start(bf16[128,1792]{1,0:T(8,128)(2,1)} %get-tuple-element.103), channel_id=1, source_target_pairs={{0,4},{1,5},{2,6},{3,7},{4,0},{5,1},{6,2},{7,3},{8,12},{9,13},{10,... | collective-permute-start | bytes 1376264 | tf_op jit(solution)/shard_map/ppermute | solution.py:466
  136.7 12.0 %collective-permute-start.31 = (bf16[128,576]{1,0:T(8,128)(2,1)S(1)}, bf16[128,576]{1,0:T(8,128)(2,1)S(1)}, u32[]{:S(2)}, u32[]{:S(2)}) collective-permute-start(bf16[128,576]{1,0:T(8,128)(2,1)S(1)} %copy-done.27), channel_id=1, source_target_pairs={{0,8},{1,9},{2,10},{3,11},{4,12},{5,13},{6,14},{7,15},{8,0},{9,1},... | collective-permute-start | bytes 442376 | tf_op jit(solution)/shard_map/ppermute | solution.py:466
  136.7 59.1 %collective-permute-start.25 = (bf16[128,1792]{1,0:T(8,128)(2,1)}, bf16[128,1792]{1,0:T(8,128)(2,1)S(1)}, u32[]{:S(2)}, u32[]{:S(2)}) collective-permute-start(bf16[128,1792]{1,0:T(8,128)(2,1)} %get-tuple-element.101), channel_id=1, source_target_pairs={{0,4},{1,5},{2,6},{3,7},{4,0},{5,1},{6,2},{7,3},{8,12},{9,13},{10,... | collective-permute-start | bytes 1376264 | tf_op jit(solution)/shard_map/ppermute | solution.py:466
  139.7 17.3 %copy-start.21 = (bf16[128,1792]{1,0:T(8,128)(2,1)S(1)}, bf16[128,1792]{1,0:T(8,128)(2,1)}, u32[]{:S(2)}) copy-start(bf16[128,1792]{1,0:T(8,128)(2,1)} %get-tuple-element.102) | copy-start | bytes 1376260
  139.7 44.6 %collective-permute-start.29 = (bf16[128,1792]{1,0:T(8,128)(2,1)}, bf16[128,1792]{1,0:T(8,128)(2,1)S(1)}, u32[]{:S(2)}, u32[]{:S(2)}) collective-permute-start(bf16[128,1792]{1,0:T(8,128)(2,1)} %get-tuple-element.110), channel_id=1, source_target_pairs={{0,4},{1,5},{2,6},{3,7},{4,0},{5,1},{6,2},{7,3},{8,12},{9,13},{10,... | collective-permute-start | bytes 1376264 | tf_op jit(solution)/shard_map/ppermute | solution.py:466
  140.6 43.6 %collective-permute-start.30 = (bf16[128,1792]{1,0:T(8,128)(2,1)}, bf16[128,1792]{1,0:T(8,128)(2,1)S(1)}, u32[]{:S(2)}, u32[]{:S(2)}) collective-permute-start(bf16[128,1792]{1,0:T(8,128)(2,1)} %add_convert_fusion.1), channel_id=1, source_target_pairs={{0,12},{1,13},{2,14},{3,15},{4,8},{5,9},{6,10},{7,11},{8,4},{9,5},... | collective-permute-start | bytes 1376264 | tf_op jit(solution)/shard_map/ppermute | solution.py:466
  148.8 35.4 %copy-start.18 = (bf16[128,1792]{1,0:T(8,128)(2,1)S(1)}, bf16[128,1792]{1,0:T(8,128)(2,1)}, u32[]{:S(2)}) copy-start(bf16[128,1792]{1,0:T(8,128)(2,1)} %get-tuple-element.104) | copy-start | bytes 1376260
  151.3 43.6 %all-to-all-start = ((bf16[16,16,576]{2,1,0:T(8,128)(2,1)}), bf16[16,16,576]{2,1,0:T(8,128)(2,1)S(1)}, u32[]{:S(2)}, u32[]{:S(2)}) async-start(bf16[16,16,576]{2,1,0:T(8,128)(2,1)} %bitcast.9), calls=%async_computation | async-start | bytes 655360 | tf_op jit(solution)/shard_map/all_to_all | solution.py:560
  157.0 38.8 %copy-start.19 = (bf16[128,1792]{1,0:T(8,128)(2,1)S(1)}, bf16[128,1792]{1,0:T(8,128)(2,1)}, u32[]{:S(2)}) copy-start(bf16[128,1792]{1,0:T(8,128)(2,1)} %get-tuple-element.100) | copy-start | bytes 1376260
  157.9 37.9 %collective-permute-start.27 = (bf16[128,1792]{1,0:T(8,128)(2,1)}, bf16[128,1792]{1,0:T(8,128)(2,1)S(1)}, u32[]{:S(2)}, u32[]{:S(2)}) collective-permute-start(bf16[128,1792]{1,0:T(8,128)(2,1)} %add_convert_fusion.3), channel_id=1, source_target_pairs={{0,12},{1,13},{2,14},{3,15},{4,8},{5,9},{6,10},{7,11},{8,4},{9,5},... | collective-permute-start | bytes 1376264 | tf_op jit(solution)/shard_map/ppermute | solution.py:466

commit v3 on v2

--- a/solution.py
+++ b/solution.py
@@ -13,7 +13,7 @@
 GROUP = 4
 LINE = 4
 SCALE_COLUMNS = 128
-VMEM_GRANT = 56 * 1024 * 1024
+MIB = 1024 * 1024
 BRIEF = pl.CostEstimate(flops=1 << 20, bytes_accessed=1 << 20, transcendentals=0)
 
 
@@ -66,14 +66,13 @@
     ).astype(jnp.bfloat16)
 
 
-def cache_send_rows(latent_vector, owner, device_count, push_cap):
+def cache_slots(owner, device_count, push_cap):
     target = owner[:, 0]
-    rank_index = block_ranks(target[None, :], device_count)[0]
-    return (
-        jnp.zeros((device_count * push_cap, latent_vector.shape[1]), jnp.bfloat16)
-        .at[target * push_cap + rank_index]
-        .set(latent_vector)
-    )
+    return target * push_cap + block_ranks(target[None, :], device_count)[0]
+
+
+def cache_send_rows(latent_vector, slots, rows):
+    return jnp.zeros((rows, latent_vector.shape[1]), jnp.bfloat16).at[slots].set(latent_vector)
 
 
 def packed_shards(
@@ -147,7 +146,9 @@
         preferred_element_type=jnp.float32,
     )
     send_rows = cache_send_rows(
-        latent_rows(raw_latent, key_value_gain), owner, device_count, push_cap
+        latent_rows(raw_latent, key_value_gain),
+        cache_slots(owner, device_count, push_cap),
+        device_count * push_cap,
     )
     latent_cache = lax.all_to_all(send_rows, "dev", split_axis=0, concat_axis=0, tiled=True)
     return (moe_out, latent_cache)
@@ -192,13 +193,13 @@
     smem, vmem, hbm = (
         pl.BlockSpec(memory_space=space) for space in (pltpu.SMEM, pltpu.VMEM, pltpu.HBM)
     )
-    rows = jax.ShapeDtypeStruct((some, features + SCALE_COLUMNS), jnp.bfloat16)
+    rows = pltpu.VMEM((some, features + SCALE_COLUMNS), jnp.bfloat16)
     return pl.pallas_call(
         entry_kernel,
         out_shape=[
             rows,
             rows,
-            jax.ShapeDtypeStruct((weight.shape[0] // 2, weight.shape[1]), weight.dtype),
+            pltpu.VMEM((weight.shape[0] // 2, weight.shape[1]), weight.dtype),
         ],
         in_specs=[smem, vmem, vmem, vmem, vmem, hbm],
         out_specs=[vmem] * 3,
@@ -224,7 +225,7 @@
 
 def halves_of(place, *weights):
     shapes = [
-        jax.ShapeDtypeStruct((weight.shape[0] // 2, weight.shape[1]), weight.dtype)
+        pltpu.VMEM((weight.shape[0] // 2, weight.shape[1]), weight.dtype)
         for weight in weights
     ]
     return pl.pallas_call(
@@ -262,9 +263,9 @@
     pltpu.make_async_copy(buf.at[slot], buf.at[slot], sems.at[k]).wait()
 
 
-def latent_kernel(place_ref, *refs):
-    row_refs, kv_refs, part_refs = refs[:6], refs[6:10], refs[10:13]
-    rows_buf, kv_buf, row_sems, kv_sems = refs[13:]
+def latent_kernel(count, place_ref, *refs):
+    row_refs, kv_refs, part_refs = refs[:count], refs[count : count + 4], refs[count + 4 : -4]
+    rows_buf, kv_buf, row_sems, kv_sems = refs[-4:]
     place, plane = place_ref[0], place_ref[2]
     depth, piece = rows_buf.shape[1], kv_refs[0].shape[0]
     some = row_refs[0].shape[0]
@@ -283,26 +284,28 @@
     for copy in copies:
         copy.wait()
     out = jnp.dot(rows_buf[...], kv_buf[...], preferred_element_type=jnp.float32)
+    tok_rows = part_refs[0].shape[0]
     for index, ref in enumerate(part_refs):
-        ref[...] = out[2 * index * some : 2 * (index + 1) * some].astype(jnp.bfloat16)
-
-
-def latent_parts(place, rows, kv_parts):
-    some = rows[0].shape[0]
+        ref[...] = out[index * tok_rows : (index + 1) * tok_rows].astype(jnp.bfloat16)
+
+
+def latent_parts(place, rows, kv_parts, tok_rows):
+    height = sum(each.shape[0] for each in rows)
     piece, width = kv_parts[0].shape
-    vmem, hbm = pl.BlockSpec(memory_space=pltpu.VMEM), pl.BlockSpec(memory_space=pltpu.HBM)
+    vmem, anywhere = pl.BlockSpec(memory_space=pltpu.VMEM), pl.BlockSpec(memory_space=pl.ANY)
     return pl.pallas_call(
-        latent_kernel,
-        out_shape=[jax.ShapeDtypeStruct((2 * some, width), jnp.bfloat16)] * (len(rows) // 2),
-        in_specs=[pl.BlockSpec(memory_space=pltpu.SMEM)] + [hbm] * (len(rows) + len(kv_parts)),
-        out_specs=[vmem] * (len(rows) // 2),
+        functools.partial(latent_kernel, len(rows)),
+        out_shape=[pltpu.VMEM((tok_rows, width), jnp.bfloat16)] * (height // tok_rows),
+        in_specs=[pl.BlockSpec(memory_space=pltpu.SMEM)]
+        + [anywhere] * (len(rows) + len(kv_parts)),
+        out_specs=[vmem] * (height // tok_rows),
         scratch_shapes=[
-            pltpu.VMEM((len(rows) * some, GROUP * piece), jnp.bfloat16),
+            pltpu.VMEM((height, GROUP * piece), jnp.bfloat16),
             pltpu.VMEM((GROUP * piece, width), jnp.bfloat16),
             pltpu.SemaphoreType.DMA((len(rows),)),
             pltpu.SemaphoreType.DMA((GROUP,)),
         ],
-        compiler_params=pltpu.CompilerParams(vmem_limit_bytes=VMEM_GRANT),
+        compiler_params=pltpu.CompilerParams(vmem_limit_bytes=8 * MIB),
         cost_estimate=BRIEF,
         name="latent_parts",
     )(place, *rows, *kv_parts)
@@ -310,10 +313,9 @@
 
 def hidden_kernel(place_ref, *refs):
     row_refs, gate_refs, up_refs, refs = refs[:7], refs[7:13], refs[13:19], refs[19:]
-    down_refs, kv_refs, refs = refs[:2], refs[2:6], refs[6:]
-    hidden_ref, scale_ref, latent_ref, part_refs, refs = refs[0], refs[1], refs[2], refs[3:7], refs[7:]
-    rows_buf, gate_buf, up_buf, down_buf, kv_buf = refs[:5]
-    row_sems, gate_sems, up_sems, down_sems, kv_sems = refs[5:]
+    down_refs, (hidden_ref, scale_ref, part_ref), refs = refs[:2], refs[2:5], refs[5:]
+    rows_buf, gate_buf, up_buf, down_buf = refs[:4]
+    row_sems, gate_sems, up_sems, down_sems = refs[4:]
     place, rep, plane = place_ref[0], place_ref[1], place_ref[2]
     core = place & 1
     some = row_refs[0].shape[0]
@@ -322,22 +324,17 @@
         target = rows_buf.at[pl.ds(first, ref.shape[0])]
         row_copies.append(pltpu.make_async_copy(ref, target, row_sems.at[index]))
         first += ref.shape[0]
-    piece = kv_refs[0].shape[0]
-    kv_copies = [
-        pltpu.make_async_copy(ref, kv_buf.at[pl.ds((place ^ k) * piece, piece)], kv_sems.at[k])
-        for k, ref in enumerate(kv_refs)
-    ]
+
+    def begin_slot(slot):
+        begin_block(gate_refs, gate_buf, gate_sems, slot, place ^ slot, rep)
+        begin_block(up_refs, up_buf, up_sems, slot, place ^ slot, rep)
+
     for copy in row_copies:
         copy.start()
-    for slot in range(GROUP):
-        begin_block(gate_refs, gate_buf, gate_sems, slot, place ^ slot, rep)
-        begin_block(up_refs, up_buf, up_sems, slot, place ^ slot, rep)
-    for slot in range(2):
-        begin_block(down_refs, down_buf, down_sems, slot, core ^ slot, rep)
-    for copy in kv_copies:
-        copy.start()
+    begin_slot(0)
     for copy in row_copies:
         copy.wait()
+    begin_slot(1)
 
     features, units = gate_buf.shape[1:]
     terms = rows_buf[:, features:].astype(jnp.float32)
@@ -348,6 +345,10 @@
     for slot in range(GROUP):
         await_block(gate_buf, gate_sems, slot, place ^ slot)
         await_block(up_buf, up_sems, slot, place ^ slot)
+        if slot + 2 < GROUP:
+            begin_slot(slot + 2)
+        else:
+            begin_block(down_refs, down_buf, down_sems, slot - 2, core ^ (slot - 2), rep)
         rows = rows_buf[:, :features]
         gate_part = jnp.dot(rows, gate_buf[slot], preferred_element_type=jnp.float32)
         up_part = jnp.dot(rows, up_buf[slot], preferred_element_type=jnp.float32)
@@ -357,90 +358,134 @@
 
     for slot in range(2):
         await_block(down_buf, down_sems, slot, core ^ slot)
-        weigh_block(hidden_ref, scale_ref, down_buf, slot, part_refs)
-
-    for copy in kv_copies:
-        copy.wait()
-    depth = GROUP * piece
-    columns = pl.ds(pl.multiple_of(plane * depth, 128), depth)
-    latent = jnp.dot(
-        rows_buf[4 * some : 6 * some, columns], kv_buf[...], preferred_element_type=jnp.float32
-    )
-    latent_ref[...] = latent.astype(jnp.bfloat16)
-
-
-def weigh_block(hidden_ref, scale_ref, down_buf, slot, part_refs):
-    out = jnp.dot(hidden_ref[...], down_buf[slot], preferred_element_type=jnp.float32)
-    out = (out.astype(jnp.bfloat16).astype(jnp.float32) * scale_ref[...]).astype(jnp.bfloat16)
-    tok_rows, width = part_refs[0].shape[0], down_buf.shape[2]
-    for index, part_ref in enumerate(part_refs):
-        part_ref[:, slot * width : (slot + 1) * width] = out[
-            index * tok_rows : (index + 1) * tok_rows
-        ]
-
-
-def hidden_units(place, rows, gates, ups, near, kv_parts):
+        width = down_buf.shape[2]
+        part_ref[:, slot * width : (slot + 1) * width] = weighed(
+            hidden_ref[4 * some : 6 * some], scale_ref[4 * some : 6 * some], down_buf[slot]
+        )
+
+
+def weighed(hidden, scale, down):
+    out = jnp.dot(hidden, down, preferred_element_type=jnp.float32)
+    return (out.astype(jnp.bfloat16).astype(jnp.float32) * scale).astype(jnp.bfloat16)
+
+
+def hidden_units(place, rows, gates, ups, near):
     some, extended = rows[0].shape
     features, units = gates[0].shape
     columns = near[0].shape[1]
-    piece, latent_width = kv_parts[0].shape
     hbm, vmem = pl.BlockSpec(memory_space=pltpu.HBM), pl.BlockSpec(memory_space=pltpu.VMEM)
     bf16, dma = jnp.bfloat16, pltpu.SemaphoreType.DMA
-    operands = (*rows, *gates, *ups, *near, *kv_parts)
+    operands = (*rows, *gates, *ups, *near)
+    late = [rows[4], ups[3], ups[4], ups[5], gates[5]]
+    specs = [
+        pl.BlockSpec(memory_space=pl.ANY if any(each is one for one in late) else pltpu.HBM)
+        for each in operands
+    ]
     return pl.pallas_call(
         hidden_kernel,
         out_shape=[
-            jax.ShapeDtypeStruct((2 * LINE * some, GROUP * units), bf16),
-            jax.ShapeDtypeStruct((2 * LINE * some, 1), jnp.float32),
-            jax.ShapeDtypeStruct((2 * some, latent_width), bf16),
+            pltpu.VMEM((2 * LINE * some, GROUP * units), bf16),
+            pltpu.VMEM((2 * LINE * some, 1), jnp.float32),
         ]
-        + [jax.ShapeDtypeStruct((2 * some, 2 * columns), bf16)] * LINE,
-        in_specs=[pl.BlockSpec(memory_space=pltpu.SMEM)] + [hbm] * len(operands),
-        out_specs=[vmem] * (3 + LINE),
+        + [pltpu.VMEM((2 * some, 2 * columns), bf16)],
+        in_specs=[pl.BlockSpec(memory_space=pltpu.SMEM)] + specs,
+        out_specs=[vmem] * 3,
         scratch_shapes=[
             pltpu.VMEM((2 * LINE * some, extended), bf16),
             pltpu.VMEM((GROUP, features, units), bf16),
             pltpu.VMEM((GROUP, features, units), bf16),
             pltpu.VMEM((2, GROUP * units, columns), bf16),
-            pltpu.VMEM((GROUP * piece, latent_width), bf16),
             dma((len(rows),)),
             dma((GROUP,)),
             dma((GROUP,)),
             dma((2,)),
-            dma((GROUP,)),
         ],
-        compiler_params=pltpu.CompilerParams(vmem_limit_bytes=VMEM_GRANT),
+        compiler_params=pltpu.CompilerParams(vmem_limit_bytes=52 * MIB),
         cost_estimate=BRIEF,
         name="hidden_units",
     )(place, *operands)
 
 
-def far_kernel(place_ref, hidden_ref, scale_ref, *refs):
-    down_refs, part_refs, down_buf, sems = refs[:4], refs[4:-2], refs[-2], refs[-1]
-    core, rep = place_ref[0] & 1, place_ref[1]
-    for slot in range(2):
-        begin_block(down_refs, down_buf, sems, slot, core ^ slot, rep)
-    for slot in range(2):
-        await_block(down_buf, sems, slot, core ^ slot)
-        weigh_block(hidden_ref, scale_ref, down_buf, slot, part_refs)
-
-
-def far_products(place, hidden, scale, downs):
+def rest_kernel(place_ref, hidden_ref, scale_ref, *refs):
+    down_refs, (part0_ref, part1_ref, part3_ref, far_ref), (down_buf, sems) = refs[:6], refs[6:10], refs[10:]
+    place, rep = place_ref[0], place_ref[1]
+
+    def begin_slot(slot):
+        begin_block(down_refs, down_buf, sems, slot, place ^ slot, rep)
+
+    begin_slot(0)
+    begin_slot(1)
+    tok_rows, width = part0_ref.shape[0], down_buf.shape[2]
+    for slot in range(GROUP):
+        await_block(down_buf, sems, slot, place ^ slot)
+        if slot + 2 < GROUP:
+            begin_slot(slot + 2)
+        out = weighed(hidden_ref[...], scale_ref[...], down_buf[slot])
+        columns = slice(slot * width, (slot + 1) * width)
+        for k, ref in ((0, part0_ref), (1, part1_ref), (3, part3_ref)):
+            ref[:, columns] = out[k * tok_rows : (k + 1) * tok_rows]
+
+        @pl.when((place ^ slot) >= 2)
+        def _(slot=slot, out=out):
+            columns = slice((slot % 2) * width, (slot % 2 + 1) * width)
+            far_ref[:, columns] = out[2 * tok_rows : 3 * tok_rows]
+
+
+def rest_products(place, hidden, scale, downs):
     tok_rows, units, width = hidden.shape[0] // LINE, hidden.shape[1], downs[0].shape[1]
     hbm, vmem = pl.BlockSpec(memory_space=pltpu.HBM), pl.BlockSpec(memory_space=pltpu.VMEM)
     return pl.pallas_call(
-        far_kernel,
-        out_shape=[jax.ShapeDtypeStruct((tok_rows, 2 * width), jnp.bfloat16)] * LINE,
-        in_specs=[pl.BlockSpec(memory_space=pltpu.SMEM), vmem, vmem] + [hbm] * len(downs),
-        out_specs=[vmem] * LINE,
+        rest_kernel,
+        out_shape=[pltpu.VMEM((tok_rows, GROUP * width), jnp.bfloat16)] * 3
+        + [pltpu.VMEM((tok_rows, 2 * width), jnp.bfloat16)],
+        in_specs=[pl.BlockSpec(memory_space=pltpu.SMEM), vmem, vmem]
+        + [hbm] * (len(downs) - 1)
+        + [pl.BlockSpec(memory_space=pl.ANY)],
+        out_specs=[vmem] * 4,
         scratch_shapes=[
-            pltpu.VMEM((2, units, width), jnp.bfloat16),
-            pltpu.SemaphoreType.DMA((2,)),
+            pltpu.VMEM((GROUP, units, width), jnp.bfloat16),
+            pltpu.SemaphoreType.DMA((GROUP,)),
         ],
-        compiler_params=pltpu.CompilerParams(vmem_limit_bytes=VMEM_GRANT),
+        compiler_params=pltpu.CompilerParams(vmem_limit_bytes=40 * MIB),
         cost_estimate=BRIEF,
-        name="far_products",
+        name="rest_products",
     )(place, hidden, scale, *downs)
+
+
+def order_kernel(place_ref, blocks_ref, ordered_ref, sems):
+    plane, chip, core = place_ref[0], place_ref[1], place_ref[2]
+    count = sems.shape[0]
+    rows = ordered_ref.shape[0] // count
+    copies = []
+    for source in range(count):
+        far = ((source & 1) ^ core) * (count // 2) + ((source >> 1 & 1) ^ chip) * (count // 4)
+        block = far + ((source >> 2) ^ plane)
+        copies.append(
+            pltpu.make_async_copy(
+                blocks_ref.at[pl.ds(block * rows, rows)],
+                ordered_ref.at[pl.ds(source * rows, rows)],
+                sems.at[source],
+            )
+        )
+    for copy in copies:
+        copy.start()
+    for copy in copies:
+        copy.wait()
+
+
+def in_source_order(place, blocks, rows):
+    return pl.pallas_call(
+        order_kernel,
+        out_shape=jax.ShapeDtypeStruct(blocks.shape, blocks.dtype),
+        in_specs=[
+            pl.BlockSpec(memory_space=pltpu.SMEM),
+            pl.BlockSpec(memory_space=pl.ANY),
+        ],
+        out_specs=pl.BlockSpec(memory_space=pltpu.VMEM),
+        scratch_shapes=[pltpu.SemaphoreType.DMA((blocks.shape[0] // rows,))],
+        cost_estimate=BRIEF,
+        name="in_source_order",
+    )(place, blocks)
 
 
 def dense_shards(
@@ -483,21 +528,26 @@
     def wide(value):
         return value.astype(jnp.float32)
 
+    some = tokens.shape[0] // 2
+    slots = cache_slots(owner, device_count, push_cap)
+
     gate_core, up_core = other_core(gate_weight), other_core(up_weight)
-    kv_parts = tuple(exchange(kv_weight, distance) for distance in range(1, GROUP))
+    kv_core, kv_x = other_core(kv_weight), other_chip(kv_weight)
     rows0, rows1, gate_half = entry(
         place_info, tokens, norm_gain, expert_index, route_gate, gate_weight
     )
-    rows0, gate_half, gate_core, kv_parts = hold((rows0, gate_half, gate_core, kv_parts))
-    kv_parts = (kv_weight, *kv_parts)
+    rows0, rows1, gate_half, gate_core, up_core, kv_core, kv_x, up_own, down_own = hold(
+        (rows0, rows1, gate_half, gate_core, up_core, kv_core, kv_x, up_weight, down_weight)
+    )
 
     f0, a0 = across_line(rows0, 3), across_line(rows0, 1)
     gate_x = other_chip(gate_half)
-    down_core = other_core(down_weight)
-    up_half, down_half = halves_of(place_info, up_weight, down_weight)
-    f0, a0, gate_x, up_core, down_core, up_half, down_half, later = hold(
-        (f0, a0, gate_x, up_core, down_core, up_half, down_half, rows1)
-    )
+    down_core, kv_x_core = other_core(down_own), other_core(kv_x)
+    up_half, down_half = halves_of(place_info, up_own, down_own)
+    f0, a0, gate_x, down_core, kv_x_core, up_half, down_half, later, slots = hold(
+        (f0, a0, gate_x, down_core, kv_x_core, up_half, down_half, rows1, slots)
+    )
+    kv_parts = (kv_weight, kv_core, kv_x, kv_x_core)
 
     f1, a1 = across_line(later, 3), across_line(later, 1)
     gate_y = other_rep(gate_x)
@@ -511,7 +561,7 @@
     up_y = other_rep(up_x)
     down_x = other_chip(down_half)
     latent0, latent1, latent3 = latent_parts(
-        place_info, (rows0, later, a0, a1, f0, f1), kv_parts
+        place_info, (rows0, later, a0, a1, f0, f1), kv_parts, 2 * some
     )
     gate_y_core, up_x_core = other_core(gate_y), other_core(up_x)
     c, up_y, down_x, gate_y_core, up_x_core, latent1, latent3 = hold(
@@ -520,44 +570,67 @@
 
     up_y_core = other_core(up_y)
     down_y, down_x_core = other_rep(down_x), other_core(down_x)
-    latent1, latent3 = across_line(latent1, 1), across_line(latent3, 3)
-    hidden, scale, latent2, near0, near1, near2, near3 = hidden_units(
+    (latent2,) = latent_parts(place_info, (c,), kv_parts, 2 * some)
+    latents = [across_line(value, k) for k, value in ((1, latent1), (2, latent2), (3, latent3))]
+    hidden, scale, near2 = hidden_units(
         place_info,
         (rows0, later, a0, a1, c, f0, f1),
         (gate_weight, gate_core, gate_x, gate_y, gate_x_core, gate_y_core),
         (up_weight, up_core, up_x, up_y, up_x_core, up_y_core),
         (down_weight, down_core),
-        kv_parts,
-    )
-    hidden, near2, latent1, latent3, down_y, down_x_core = hold(
-        (hidden, near2, latent1, latent3, down_y, down_x_core)
+    )
+    hidden, near2, latents, down_y, down_x_core = hold(
+        (hidden, near2, latents, down_y, down_x_core)
     )
     near2_there = across_line(near2, 1)
     down_y_core = other_core(down_y)
-    far0, far1, far2, far3 = far_products(
-        place_info, hidden, scale, (down_x, down_y, down_x_core, down_y_core)
+    part0, part1, part3, far2 = rest_products(
+        place_info,
+        hidden,
+        scale,
+        (down_weight, down_core, down_x, down_y, down_x_core, down_y_core),
     )
     far2_there = across_line(far2, 1)
-    near2_there, far2, latent2 = hold((near2_there, far2, latent2))
-    near_sum = narrow(wide(near3) + wide(near2_there))
-    near_sum, near1 = hold((near_sum, near1))
-    near3_there, near1_there = across_line(near_sum, 3), across_line(near1, 1)
-    latent2 = across_line(latent2, 2)
-    far_sum = narrow(wide(far3) + wide(far2_there))
-    far3_there, far1_there = across_line(far_sum, 3), across_line(far1, 1)
-    raw_latent = wide(latent0) + wide(latent1) + wide(latent2) + wide(latent3)
-    near = narrow(wide(near0) + wide(near1_there) + wide(near3_there))
-    far = narrow(wide(far0) + wide(far1_there) + wide(far3_there))
-    moe_out = jnp.where(
+
+    raw_latent = wide(latent0) + sum(wide(value) for value in latents)
+    send_rows = cache_send_rows(
+        latent_rows(raw_latent, key_value_gain), slots, device_count * push_cap
+    )
+    by_plane = send_rows.reshape(LINE, GROUP, push_cap, send_rows.shape[1])
+
+    def for_plane(number):
+        return lax.dynamic_index_in_dim(by_plane, number, 0, keepdims=False)
+
+    there = [for_plane(plane)] + [across_line(for_plane(plane ^ k), k) for k in range(1, LINE)]
+
+    part2_there = jnp.where(
         place & 2 == 2,
-        jnp.concatenate([far, near], axis=1),
-        jnp.concatenate([near, far], axis=1),
-    )
-
-    send_rows = cache_send_rows(
-        latent_rows(raw_latent, key_value_gain), owner, device_count, push_cap
-    )
-    latent_cache = lax.all_to_all(send_rows, "dev", split_axis=0, concat_axis=0, tiled=True)
+        jnp.concatenate([far2_there, near2_there], axis=1),
+        jnp.concatenate([near2_there, far2_there], axis=1),
+    )
+    part2_there, there = hold((part2_there, there))
+    part_sum = narrow(wide(part3) + wide(part2_there))
+    part_sum, part1 = hold((part_sum, part1))
+    there3, there1 = across_line(part_sum, 3), across_line(part1, 1)
+
+    chip, core = place >> 1, place & 1
+    by_chip = jnp.stack(there).reshape(LINE, 2, 2, push_cap, send_rows.shape[1])
+
+    def for_chip(number):
+        return lax.dynamic_index_in_dim(by_chip, number, 1, keepdims=False)
+
+    by_core = jnp.stack([for_chip(chip), other_chip(for_chip(1 - chip))])
+
+    def for_core(number):
+        return lax.dynamic_index_in_dim(by_core, number, 2, keepdims=False)
+
+    by_source = jnp.stack([for_core(core), other_core(for_core(1 - core))])
+    latent_cache = in_source_order(
+        jnp.stack([plane, chip, core]).astype(jnp.int32),
+        by_source.reshape(device_count * push_cap, -1),
+        push_cap,
+    )
+    moe_out = narrow(wide(part0) + wide(there1) + wide(there3))
     return (moe_out, latent_cache)
 
 

time: 198 us -> 188 us (0.949)
  starting transfers between devices: 41.9 us -> 31.5 us
  Pallas kernels: 37.4 us -> 34.8 us
  other arithmetic: 7.86 us -> 10.4 us
    ppermute x29 -> x32, waiting for transfers between devices: 78.2 us -> 89.1 us  [exchange(): lax.ppermute(value, 'dev', [(i, i ^ distance) for i in range(device_count)])]
    all_to_all x1 -> x0, waiting for transfers between devices: 10.5 us -> none  [dense_shards(): lax.all_to_all(send_rows, 'dev', split_axis=0, concat_axis=0, tiled=True)]
    all_to_all x1 -> x0, starting transfers between devices: 5.72 us -> none  [dense_shards(): lax.all_to_all(send_rows, 'dev', split_axis=0, concat_axis=0, tiled=True)]
    ppermute x29 -> x32, starting transfers between devices: 32.6 us -> 27.9 us  [exchange(): lax.ppermute(value, 'dev', [(i, i ^ distance) for i in range(device_count)])]
    another operation x2 -> x6, other arithmetic: 0.41 us -> 2.81 us  [the longest x1 0.95 us: dense_shards(): by_chip = jnp.stack(there).reshape(LINE, 2, 2, push_cap, send_rows.shape[1])]
    pallas_call x4 -> x6, Pallas kernels: 34 us -> 31.7 us  [the longest x1 14 us: hidden_units(): pl.pallas_call(hidden_kernel, out_shape=[pltpu.VMEM((2 * LINE * some, GRO...]
    unnamed x57 -> x49, local copies, waits for them, and re-layouts: 5.06 us -> 4.72 us
  transfers between devices with their start and end apart: 33 -> 35, of which waited for: 13 -> 14; matrix products, arithmetic and copies ran while one was open for 4% -> 5% of each run, Pallas kernels for 19% -> 19%
where the time goes in v3:
time: 188 us; the launch traced here: 187 us
  waiting for transfers between devices  105 us (56%)
  Pallas kernels  34.8 us (19%)
  starting transfers between devices  31.5 us (17%)
  other arithmetic  10.4 us (6%)
  local copies, waits for them, and re-layouts  4.8 us (3%)
    ppermute x32, waiting for transfers between devices, exchange(): lax.ppermute(value, 'dev', [(i, i ^ distance) for i in range(device_count)])  89.1 us
    ppermute x32, starting transfers between devices, exchange(): lax.ppermute(value, 'dev', [(i, i ^ distance) for i in range(device_count)])  27.9 us
    ppermute x3, waiting for transfers between devices, other_rep(): return lax.ppermute(value, 'rep', [(0, 1), (1, 0)])  15.4 us
    pallas_call x1, Pallas kernels, hidden_units(): pl.pallas_call(hidden_kernel, out_shape=[pltpu.VMEM((2 * LINE * some, GRO...  14 us
    pallas_call x1, Pallas kernels, rest_products(): pl.pallas_call(rest_kernel, out_shape=[pltpu.VMEM((tok_rows, GROUP * widt...  6.44 us
    pallas_call x2, Pallas kernels, latent_parts(): pl.pallas_call(functools.partial(latent_kernel, len(rows)), out_shape=[pl...  5.49 us
    unnamed x49, local copies, waits for them, and re-layouts  4.72 us
  transfers between devices with their start and end apart: 35, of which 14 were waited for; matrix products, arithmetic and copies ran while one was open for 5% of the time, Pallas kernels for 19%

profile of v3, /device:TPU:0, one launch (start us, length us, event | category | flops | bytes accessed | tf_op | source)
XLA Modules:
  0.0 187.2 jit_solution(17445816818334112351)
XLA Ops:
  0.6 0.5 collective-permute-start
  1.2 0.4 collective-permute-start.2
  1.7 2.6 %collective-permute-start.3 = (bf16[224,576]{1,0:T(8,128)(2,1)}, bf16[224,576]{1,0:T(8,128)(2,1)}, u32[]{:S(2)}, u32[]{:S(2)}) collective-permute-start(bf16[224,576]{1,0:T(8,128)(2,1)} %refs_1_.2), channel_id=1, source_target_pairs={{0,2},{1,3},{2,0},{3,1},{4,6},{5,7},{6,4},{7,5},{8,10},{9,11},{10,... | collective-permute-start | bytes 774152 | tf_op jit(solution)/shard_map/ppermute | solution.py:511
  4.2 0.6 pad_add_fusion.place_ref
  4.9 3.3 %entry.1 = (bf16[64,3712]{1,0:T(8,128)(2,1)S(1)}, bf16[64,3712]{1,0:T(8,128)(2,1)S(1)}, bf16[1792,256]{1,0:T(8,128)(2,1)}) custom-call(s32[3]{0:T(128)} %pad_add_fusion.place_ref, bf16[128,3584]{1,0:T(8,128)(2,1)} %tokens_ref.1, f32[28,128]{1,0:T(8,128)} %bitcast.42, s32[2,128]{1,0:T(2,128)} %bitcast.45, f32[2,128]{1,0:T(2,128)} %bitcast.46, ...), custom_call_target="tpu_custom_call" | custom-call | flops 1048576 | bytes 1048576 | tf_op jit(solution)/shard_map/entry/pallas_call | solution.py:197
  8.2 3.8 %collective-permute-done.3.refs_8_.refs_3_ = bf16[224,576]{1,0:T(8,128)(2,1)} collective-permute-done((bf16[224,576]{1,0:T(8,128)(2,1)}, bf16[224,576]{1,0:T(8,128)(2,1)}, u32[]{:S(2)}, u32[]{:S(2)}) %collective-permute-start.3) | collective-permute-done | bytes 258080 | tf_op jit(solution)/shard_map/ppermute | solution.py:511
  12.0 1.8 collective-permute-start.6
  13.8 3.6 %collective-permute-start.4 = (bf16[64,3712]{1,0:T(8,128)(2,1)S(1)}, bf16[64,3712]{1,0:T(8,128)(2,1)S(1)}, u32[]{:S(2)}, u32[]{:S(2)}) collective-permute-start(bf16[64,3712]{1,0:T(8,128)(2,1)S(1)} %get-tuple-element.66.refs_0_), channel_id=1, source_target_pairs={{0,12},{1,13},{2,14},{3,15},{4,8},{5,9},{6,10},{7,11},{8,4},{9,5},... | collective-permute-start | bytes 1425416 | tf_op jit(solution)/shard_map/ppermute | solution.py:511
  17.5 0.2 reduce_window_sum.11
  17.8 0.2 select_reduce_fusion
  17.9 3.1 %weight_halves.1 = (bf16[1792,256]{1,0:T(8,128)(2,1)}, bf16[512,896]{1,0:T(8,128)(2,1)S(1)}) custom-call(s32[3]{0:T(128)} %pad_add_fusion.place_ref, bf16[3584,256]{1,0:T(8,128)(2,1)} %refs_13_.1, bf16[1024,896]{1,0:T(8,128)(2,1)} %refs_0_.2), custom_call_target="tpu_custom_call" | custom-call | flops 1048576 | bytes 1048576 | tf_op jit(solution)/shard_map/weight_halves/pallas_call | solution.py:231
  21.1 0.9 copy-done.13
  22.0 7.4 %collective-permute-done.4.refs_4_.refs_5_ = bf16[64,3712]{1,0:T(8,128)(2,1)S(1)} collective-permute-done((bf16[64,3712]{1,0:T(8,128)(2,1)S(1)}, bf16[64,3712]{1,0:T(8,128)(2,1)S(1)}, u32[]{:S(2)}, u32[]{:S(2)}) %collective-permute-start.4) | collective-permute-done | bytes 475168 | tf_op jit(solution)/shard_map/ppermute | solution.py:511
  29.4 9.6 %collective-permute-done.5.refs_2_ = bf16[64,3712]{1,0:T(8,128)(2,1)} collective-permute-done((bf16[64,3712]{1,0:T(8,128)(2,1)S(1)}, bf16[64,3712]{1,0:T(8,128)(2,1)}, u32[]{:S(2)}, u32[]{:S(2)}) %collective-permute-start.5) | collective-permute-done | bytes 475168 | tf_op jit(solution)/shard_map/ppermute | solution.py:511
  39.0 1.5 collective-permute-start.11
  40.5 0.5 collective-permute-start.12
  41.1 1.7 collective-permute-start.10
  42.8 0.4 collective-permute-start.9
  43.1 11.6 %collective-permute-done.10.refs_3_ = bf16[64,3712]{1,0:T(8,128)(2,1)S(1)} collective-permute-done((bf16[64,3712]{1,0:T(8,128)(2,1)S(1)}, bf16[64,3712]{1,0:T(8,128)(2,1)S(1)}, u32[]{:S(2)}, u32[]{:S(2)}) %collective-permute-start.10) | collective-permute-done | bytes 475168 | tf_op jit(solution)/shard_map/ppermute | solution.py:511
  54.7 10.0 %collective-permute-done.9.refs_5_.refs_6_ = bf16[64,3712]{1,0:T(8,128)(2,1)S(1)} collective-permute-done((bf16[64,3712]{1,0:T(8,128)(2,1)S(1)}, bf16[64,3712]{1,0:T(8,128)(2,1)S(1)}, u32[]{:S(2)}, u32[]{:S(2)}) %collective-permute-start.9) | collective-permute-done | bytes 475168 | tf_op jit(solution)/shard_map/ppermute | solution.py:511
  64.8 1.7 collective-permute-start.14
  66.5 0.5 collective-permute-start.15
  67.0 1.5 collective-permute-start.16
  68.5 0.5 collective-permute-start.18
  69.0 3.3 %latent_parts.2 = (bf16[128,576]{1,0:T(8,128)(2,1)S(1)}, bf16[128,576]{1,0:T(8,128)(2,1)}, bf16[128,576]{1,0:T(8,128)(2,1)}) custom-call(s32[3]{0:T(128)S(1)} %copy-done.10, bf16[64,3712]{1,0:T(8,128)(2,1)S(1)} %get-tuple-element.66.refs_0_, bf16[64,3712]{1,0:T(8,128)(2,1)S(1)} %get-tuple-element.74.refs_1_, ...), custom_call_target="tpu_custom_call" | custom-call | flops 1048576 | bytes 1048576 | tf_op jit(solution)/shard_map/latent_parts/pallas_call | solution.py:296
  72.4 15.4 %collective-permute-done.15.refs_16_ = bf16[1792,256]{1,0:T(8,128)(2,1)S(1)} collective-permute-done((bf16[1792,256]{1,0:T(8,128)(2,1)S(1)}, bf16[1792,256]{1,0:T(8,128)(2,1)S(1)}, u32[]{:S(2)}, u32[]{:S(2)}) %collective-permute-start.15) | collective-permute-done | bytes 917536 | tf_op jit(solution)/shard_map/ppermute | solution.py:523
  87.8 0.3 collective-permute-done.16.refs_2_
  88.3 1.6 collective-permute-start.23
  89.9 0.2 collective-permute-start.24
  90.1 2.1 %latent_parts.3 = bf16[128,576]{1,0:T(8,128)(2,1)S(1)} custom-call(s32[3]{0:T(128)S(1)} %copy-done.10, bf16[128,3712]{1,0:T(8,128)(2,1)S(1)} %collective-permute-done.14.refs_4_.refs_0_, bf16[224,576]{1,0:T(8,128)(2,1)S(1)} %copy-done.7, bf16[224,576]{1,0:T(8,128)(2,1)S(1)} %collective-permute-done.2.refs_7_.refs_2_, ...), custom_call_target="tpu_custom_call" | custom-call | flops 1048576 | bytes 1048576 | tf_op jit(solution)/shard_map/latent_parts/pallas_call | solution.py:296
  92.2 2.7 %collective-permute-start.21 = (bf16[128,576]{1,0:T(8,128)(2,1)S(1)}, bf16[128,576]{1,0:T(8,128)(2,1)S(1)}, u32[]{:S(2)}, u32[]{:S(2)}) collective-permute-start(bf16[128,576]{1,0:T(8,128)(2,1)S(1)} %latent_parts.3), channel_id=1, source_target_pairs={{0,8},{1,9},{2,10},{3,11},{4,12},{5,13},{6,14},{7,15},{8,0},{9,1},... | collective-permute-start | bytes 442376 | tf_op jit(solution)/shard_map/ppermute | solution.py:511
  94.9 0.4 collective-permute-start.20
  95.3 0.9 copy-done.20
  96.2 1.4 collective-permute-start.22
  97.6 14.0 %hidden_units.1 = (bf16[512,1024]{1,0:T(8,128)(2,1)S(1)}, f32[512,1]{1,0:T(8,128)S(1)}, bf16[128,1792]{1,0:T(8,128)(2,1)}) custom-call(s32[3]{0:T(128)S(1)} %copy-done.10, bf16[64,3712]{1,0:T(8,128)(2,1)} %copy-done.4, bf16[64,3712]{1,0:T(8,128)(2,1)} %copy-done.5, bf16[64,3712]{1,0:T(8,128)(2,1)} %collective-permute-done.5.refs_2_, ...), custom_call_target="tpu_custom_call" | custom-call | flops 1048576 | bytes 1048576 | tf_op jit(solution)/shard_map/hidden_units/pallas_call | solution.py:384
  111.8 0.3 collective-permute-start.27
  112.1 0.1 add_add_fusion
  112.2 0.1 multiply_reduce_fusion
  112.3 0.3 fusion.16
  112.7 1.6 collective-permute-done.25.refs_5_
  114.2 6.4 %rest_products.1 = (bf16[128,3584]{1,0:T(8,128)(2,1)S(1)}, bf16[128,3584]{1,0:T(8,128)(2,1)S(1)}, bf16[128,3584]{1,0:T(8,128)(2,1)S(1)}, bf16[128,1792]{1,0:T(8,128)(2,1)S(1)}) custom-call(s32[3]{0:T(128)S(1)} %copy-done.10, bf16[512,1024]{1,0:T(8,128)(2,1)S(1)} %get-tuple-element.103.hidden_ref, f32[512,1]{1,0:T(8,128)S(1)} %get-tuple-element.104.scale_ref, ...), custom_call_target="tpu_custom_call" | custom-call | flops 1048576 | bytes 1048576 | tf_op jit(solution)/shard_map/rest_products/pallas_call | solution.py:437
  120.7 0.9 copy-done.11
  121.6 0.3 collective-permute-start.26
  121.9 0.1 multiply_convert_fusion
  122.0 1.3 scatter_custom_fusion
  123.4 1.8 collective-permute-start.28
  125.2 2.1 %collective-permute-start.29 = (bf16[4,16,576]{2,1,0:T(8,128)(2,1)S(1)}, bf16[4,16,576]{2,1,0:T(8,128)(2,1)S(1)}, u32[]{:S(2)}, u32[]{:S(2)}) collective-permute-start(bf16[4,16,576]{2,1,0:T(8,128)(2,1)S(1)} %get-tuple-element.135), channel_id=1, source_target_pairs={{0,8},{1,9},{2,10},{3,11},{4,12},{5,13},{6,14},{7,15},{8,0},{9,1},... | collective-permute-start | bytes 221192 | tf_op jit(solution)/shard_map/ppermute | solution.py:511
  127.3 0.5 collective-permute-start.30
  127.8 8.6 %collective-permute-done.26 = bf16[128,1792]{1,0:T(8,128)(2,1)S(1)} collective-permute-done((bf16[128,1792]{1,0:T(8,128)(2,1)S(1)}, bf16[128,1792]{1,0:T(8,128)(2,1)S(1)}, u32[]{:S(2)}, u32[]{:S(2)}) %collective-permute-start.26) | collective-permute-done | bytes 458784 | tf_op jit(solution)/shard_map/ppermute | solution.py:511
  136.4 1.4 maximum_select_fusion
  137.8 0.3 collective-permute-done.28
  138.1 3.3 %collective-permute-done.30 = bf16[4,16,576]{2,1,0:T(8,128)(2,1)S(1)} collective-permute-done((bf16[4,16,576]{2,1,0:T(8,128)(2,1)S(1)}, bf16[4,16,576]{2,1,0:T(8,128)(2,1)S(1)}, u32[]{:S(2)}, u32[]{:S(2)}) %collective-permute-start.30) | collective-permute-done | bytes 73760 | tf_op jit(solution)/shard_map/ppermute | solution.py:511
  141.5 1.1 add_convert_fusion.1
  142.6 0.6 collective-permute-start.32
  143.2 0.9 pad_maximum_fusion.1
  144.2 2.0 %collective-permute-start.33 = (bf16[4,2,16,576]{3,2,0,1:T(8,128)(2,1)S(1)}, bf16[4,2,16,576]{3,2,0,1:T(8,128)(2,1)S(1)}, u32[]{:S(2)}, u32[]{:S(2)}) collective-permute-start(bf16[4,2,16,576]{3,2,0,1:T(8,128)(2,1)S(1)} %get-tuple-element.132), channel_id=1, source_target_pairs={{0,2},{1,3},{2,0},{3,1},{4,6},{5,7},{6,4},{7,5},{8,10},{9,11},{10,... | collective-permute-start | bytes 442376 | tf_op jit(solution)/shard_map/ppermute | solution.py:511
  146.3 4.4 %collective-permute-done.33 = bf16[4,2,16,576]{3,2,0,1:T(8,128)(2,1)S(1)} collective-permute-done((bf16[4,2,16,576]{3,2,0,1:T(8,128)(2,1)S(1)}, bf16[4,2,16,576]{3,2,0,1:T(8,128)(2,1)S(1)}, u32[]{:S(2)}, u32[]{:S(2)}) %collective-permute-start.33) | collective-permute-done | bytes 147488 | tf_op jit(solution)/shard_map/ppermute | solution.py:511
  150.8 0.6 pad_add_fusion.1.place_ref
  151.4 0.8 collective-permute-done.34
  152.2 0.8 pad_maximum_fusion.2
  152.9 2.5 %in_source_order.1 = bf16[256,576]{1,0:T(8,128)(2,1)} custom-call(s32[3]{0:T(128)} %pad_add_fusion.1.place_ref, bf16[256,576]{1,0:T(8,128)(2,1)} %bitcast.35), custom_call_target="tpu_custom_call" | custom-call | flops 1048576 | bytes 1048576 | tf_op jit(solution)/shard_map/in_source_order/pallas_call | solution.py:477
  155.4 1.8 copy.14
  157.2 27.5 %collective-permute-done.31 = bf16[128,3584]{1,0:T(8,128)(2,1)S(1)} collective-permute-done((bf16[128,3584]{1,0:T(8,128)(2,1)S(1)}, bf16[128,3584]{1,0:T(8,128)(2,1)S(1)}, u32[]{:S(2)}, u32[]{:S(2)}) %collective-permute-start.31) | collective-permute-done | bytes 917536 | tf_op jit(solution)/shard_map/ppermute | solution.py:511
  184.8 2.4 %add_convert_fusion = bf16[128,3584]{1,0:T(8,128)(2,1)} fusion(bf16[128,3584]{1,0:T(8,128)(2,1)} %collective-permute-done.32, bf16[128,3584]{1,0:T(8,128)(2,1)S(1)} %collective-permute-done.31, bf16[128,3584]{1,0:T(8,128)(2,1)S(1)} %get-tuple-element.107), kind=kLoop, calls=%fused_computation.1 | loop fusion | flops 2752512 | bytes 3670016 | tf_op jit(solution)/shard_map/convert_element_type | solution.py:526
  (86 shorter events, 0.8 us)
Async XLA Ops:
  0.6 16.8 %copy-start.23 = (s32[128,1]{0,1:T(1,128)S(1)}, s32[128,1]{0,1:T(1,128)}, u32[]{:S(2)}) copy-start(s32[128,1]{0,1:T(1,128)} %param.19) | copy-start | bytes 1540
  0.6 11.3 %collective-permute-start = (bf16[3584,256]{1,0:T(8,128)(2,1)}, bf16[3584,256]{1,0:T(8,128)(2,1)}, u32[]{:S(2)}, u32[]{:S(2)}) collective-permute-start(bf16[3584,256]{1,0:T(8,128)(2,1)} %refs_7_.1), channel_id=1, source_target_pairs={{0,1},{1,0},{2,3},{3,2},{4,5},{5,4},{6,7},{7,6},{8,9},{9,8},{10,11... | collective-permute-start | bytes 5505032 | tf_op jit(solution)/shard_map/ppermute | solution.py:511
  1.2 10.8 %collective-permute-start.1 = (bf16[3584,256]{1,0:T(8,128)(2,1)}, bf16[3584,256]{1,0:T(8,128)(2,1)}, u32[]{:S(2)}, u32[]{:S(2)}) collective-permute-start(bf16[3584,256]{1,0:T(8,128)(2,1)} %refs_13_.1), channel_id=1, source_target_pairs={{0,1},{1,0},{2,3},{3,2},{4,5},{5,4},{6,7},{7,6},{8,9},{9,8},{10,11... | collective-permute-start | bytes 5505032 | tf_op jit(solution)/shard_map/ppermute | solution.py:511
  1.2 7.0 %collective-permute-start.2 = (bf16[224,576]{1,0:T(8,128)(2,1)}, bf16[224,576]{1,0:T(8,128)(2,1)S(1)}, u32[]{:S(2)}, u32[]{:S(2)}) collective-permute-start(bf16[224,576]{1,0:T(8,128)(2,1)} %refs_1_.2), channel_id=1, source_target_pairs={{0,1},{1,0},{2,3},{3,2},{4,5},{5,4},{6,7},{7,6},{8,9},{9,8},{10,11... | collective-permute-start | bytes 774152 | tf_op jit(solution)/shard_map/ppermute | solution.py:511
  1.7 10.3 %collective-permute-start.3 = (bf16[224,576]{1,0:T(8,128)(2,1)}, bf16[224,576]{1,0:T(8,128)(2,1)}, u32[]{:S(2)}, u32[]{:S(2)}) collective-permute-start(bf16[224,576]{1,0:T(8,128)(2,1)} %refs_1_.2), channel_id=1, source_target_pairs={{0,2},{1,3},{2,0},{3,1},{4,6},{5,7},{6,4},{7,5},{8,10},{9,11},{10,... | collective-permute-start | bytes 774152 | tf_op jit(solution)/shard_map/ppermute | solution.py:511
  8.2 60.8 %copy-start.4 = (bf16[64,3712]{1,0:T(8,128)(2,1)}, bf16[64,3712]{1,0:T(8,128)(2,1)S(1)}, u32[]{:S(2)}) copy-start(bf16[64,3712]{1,0:T(8,128)(2,1)S(1)} %get-tuple-element.66.refs_0_) | copy-start | bytes 1425412
  8.2 60.8 %copy-start.5 = (bf16[64,3712]{1,0:T(8,128)(2,1)}, bf16[64,3712]{1,0:T(8,128)(2,1)S(1)}, u32[]{:S(2)}) copy-start(bf16[64,3712]{1,0:T(8,128)(2,1)S(1)} %get-tuple-element.74.refs_1_) | copy-start | bytes 1425412
  12.0 27.0 %collective-permute-start.7 = (bf16[1024,896]{1,0:T(8,128)(2,1)}, bf16[1024,896]{1,0:T(8,128)(2,1)}, u32[]{:S(2)}, u32[]{:S(2)}) collective-permute-start(bf16[1024,896]{1,0:T(8,128)(2,1)} %refs_0_.2), channel_id=1, source_target_pairs={{0,1},{1,0},{2,3},{3,2},{4,5},{5,4},{6,7},{7,6},{8,9},{9,8},{10,11... | collective-permute-start | bytes 5505032 | tf_op jit(solution)/shard_map/ppermute | solution.py:511
  12.0 27.0 %collective-permute-start.6 = (bf16[1792,256]{1,0:T(8,128)(2,1)}, bf16[1792,256]{1,0:T(8,128)(2,1)}, u32[]{:S(2)}, u32[]{:S(2)}) collective-permute-start(bf16[1792,256]{1,0:T(8,128)(2,1)} %get-tuple-element.67), channel_id=1, source_target_pairs={{0,2},{1,3},{2,0},{3,1},{4,6},{5,7},{6,4},{7,5},{8,10},{9,11},{10,... | collective-permute-start | bytes 2752520 | tf_op jit(solution)/shard_map/ppermute | solution.py:511
  13.8 15.6 %collective-permute-start.4 = (bf16[64,3712]{1,0:T(8,128)(2,1)S(1)}, bf16[64,3712]{1,0:T(8,128)(2,1)S(1)}, u32[]{:S(2)}, u32[]{:S(2)}) collective-permute-start(bf16[64,3712]{1,0:T(8,128)(2,1)S(1)} %get-tuple-element.66.refs_0_), channel_id=1, source_target_pairs={{0,12},{1,13},{2,14},{3,15},{4,8},{5,9},{6,10},{7,11},{8,4},{9,5},... | collective-permute-start | bytes 1425416 | tf_op jit(solution)/shard_map/ppermute | solution.py:511
  17.4 21.6 %collective-permute-start.5 = (bf16[64,3712]{1,0:T(8,128)(2,1)S(1)}, bf16[64,3712]{1,0:T(8,128)(2,1)}, u32[]{:S(2)}, u32[]{:S(2)}) collective-permute-start(bf16[64,3712]{1,0:T(8,128)(2,1)S(1)} %get-tuple-element.66.refs_0_), channel_id=1, source_target_pairs={{0,4},{1,5},{2,6},{3,7},{4,0},{5,1},{6,2},{7,3},{8,12},{9,13},{10,... | collective-permute-start | bytes 1425416 | tf_op jit(solution)/shard_map/ppermute | solution.py:511
  17.7 4.3 %collective-permute-start.8 = (bf16[224,576]{1,0:T(8,128)(2,1)}, bf16[224,576]{1,0:T(8,128)(2,1)}, u32[]{:S(2)}, u32[]{:S(2)}) collective-permute-start(bf16[224,576]{1,0:T(8,128)(2,1)} %collective-permute-done.3.refs_8_.refs_3_), channel_id=1, source_target_pairs={{0,1},{1,0},{2,3},{3,2},{4,5},{5,4},{6,7},{7,6},{8,9},{9,8},{10,11... | collective-permute-start | bytes 774152 | tf_op jit(solution)/shard_map/ppermute | solution.py:511
  21.0 0.9 copy-start.13
  22.0 47.0 %copy-start.7 = (bf16[224,576]{1,0:T(8,128)(2,1)S(1)}, bf16[224,576]{1,0:T(8,128)(2,1)}, u32[]{:S(2)}) copy-start(bf16[224,576]{1,0:T(8,128)(2,1)} %refs_1_.2) | copy-start | bytes 774148
  22.0 47.0 %copy-start.10 = (s32[3]{0:T(128)S(1)}, s32[3]{0:T(128)}, u32[]{:S(2)}) copy-start(s32[3]{0:T(128)} %pad_add_fusion.place_ref) | copy-start | bytes 40
  22.0 45.0 %copy-start.14 = (bf16[512,896]{1,0:T(8,128)(2,1)S(1)}, bf16[512,896]{1,0:T(8,128)(2,1)}, u32[]{:S(2)}) copy-start(bf16[512,896]{1,0:T(8,128)(2,1)} %copy-done.13) | copy-start | bytes 2752516
  29.4 42.9 %copy-start.1 = (bf16[64,3712]{1,0:T(8,128)(2,1)}, bf16[64,3712]{1,0:T(8,128)(2,1)S(1)}, u32[]{:S(2)}) copy-start(bf16[64,3712]{1,0:T(8,128)(2,1)S(1)} %collective-permute-done.4.refs_4_.refs_5_) | copy-start | bytes 1425412
  39.0 25.7 %collective-permute-start.11 = (bf16[1792,256]{1,0:T(8,128)(2,1)}, bf16[1792,256]{1,0:T(8,128)(2,1)S(1)}, u32[]{:S(2)}, u32[]{:S(2)}) collective-permute-start(bf16[1792,256]{1,0:T(8,128)(2,1)} %collective-permute-done.6.refs_9_), channel_id=1, source_target_pairs={{0,16},{16,0},{1,17},{17,1},{2,18},{18,2},{3,19},{19,3},{4,20},{20... | collective-permute-start | bytes 2752520 | tf_op jit(solution)/shard_map/ppermute | solution.py:523
  40.5 24.2 %collective-permute-start.12 = (bf16[1792,256]{1,0:T(8,128)(2,1)}, bf16[1792,256]{1,0:T(8,128)(2,1)S(1)}, u32[]{:S(2)}, u32[]{:S(2)}) collective-permute-start(bf16[1792,256]{1,0:T(8,128)(2,1)} %get-tuple-element.78), channel_id=1, source_target_pairs={{0,2},{1,3},{2,0},{3,1},{4,6},{5,7},{6,4},{7,5},{8,10},{9,11},{10,... | collective-permute-start | bytes 2752520 | tf_op jit(solution)/shard_map/ppermute | solution.py:511
  41.1 23.6 %collective-permute-start.13 = (bf16[1792,256]{1,0:T(8,128)(2,1)}, bf16[1792,256]{1,0:T(8,128)(2,1)}, u32[]{:S(2)}, u32[]{:S(2)}) collective-permute-start(bf16[1792,256]{1,0:T(8,128)(2,1)} %collective-permute-done.6.refs_9_), channel_id=1, source_target_pairs={{0,1},{1,0},{2,3},{3,2},{4,5},{5,4},{6,7},{7,6},{8,9},{9,8},{10,11... | collective-permute-start | bytes 2752520 | tf_op jit(solution)/shard_map/ppermute | solution.py:511
  41.1 13.6 %collective-permute-start.10 = (bf16[64,3712]{1,0:T(8,128)(2,1)S(1)}, bf16[64,3712]{1,0:T(8,128)(2,1)S(1)}, u32[]{:S(2)}, u32[]{:S(2)}) collective-permute-start(bf16[64,3712]{1,0:T(8,128)(2,1)S(1)} %get-tuple-element.74.refs_1_), channel_id=1, source_target_pairs={{0,4},{1,5},{2,6},{3,7},{4,0},{5,1},{6,2},{7,3},{8,12},{9,13},{10,... | collective-permute-start | bytes 1425416 | tf_op jit(solution)/shard_map/ppermute | solution.py:511
  42.8 21.9 %collective-permute-start.9 = (bf16[64,3712]{1,0:T(8,128)(2,1)S(1)}, bf16[64,3712]{1,0:T(8,128)(2,1)S(1)}, u32[]{:S(2)}, u32[]{:S(2)}) collective-permute-start(bf16[64,3712]{1,0:T(8,128)(2,1)S(1)} %get-tuple-element.74.refs_1_), channel_id=1, source_target_pairs={{0,12},{1,13},{2,14},{3,15},{4,8},{5,9},{6,10},{7,11},{8,4},{9,5},... | collective-permute-start | bytes 1425416 | tf_op jit(solution)/shard_map/ppermute | solution.py:511
  54.7 17.7 %copy-start.6 = (bf16[64,3712]{1,0:T(8,128)(2,1)}, bf16[64,3712]{1,0:T(8,128)(2,1)S(1)}, u32[]{:S(2)}) copy-start(bf16[64,3712]{1,0:T(8,128)(2,1)S(1)} %collective-permute-done.10.refs_3_) | copy-start | bytes 1425412
  64.7 7.7 %copy-start.2 = (bf16[64,3712]{1,0:T(8,128)(2,1)}, bf16[64,3712]{1,0:T(8,128)(2,1)S(1)}, u32[]{:S(2)}) copy-start(bf16[64,3712]{1,0:T(8,128)(2,1)S(1)} %collective-permute-done.9.refs_5_.refs_6_) | copy-start | bytes 1425412
  64.7 7.7 %copy-start.15 = (bf16[1792,256]{1,0:T(8,128)(2,1)}, bf16[1792,256]{1,0:T(8,128)(2,1)S(1)}, u32[]{:S(2)}) copy-start(bf16[1792,256]{1,0:T(8,128)(2,1)S(1)} %collective-permute-done.11.refs_10_) | copy-start | bytes 2752516
  64.7 7.7 %copy-start.16 = (bf16[1792,256]{1,0:T(8,128)(2,1)}, bf16[1792,256]{1,0:T(8,128)(2,1)S(1)}, u32[]{:S(2)}) copy-start(bf16[1792,256]{1,0:T(8,128)(2,1)S(1)} %collective-permute-done.12.refs_15_) | copy-start | bytes 2752516
  64.8 23.4 %collective-permute-start.14 = (bf16[128,3712]{1,0:T(8,128)(2,1)S(1)}, bf16[128,3712]{1,0:T(8,128)(2,1)S(1)}, u32[]{:S(2)}, u32[]{:S(2)}) collective-permute-start(bf16[128,3712]{1,0:T(8,128)(2,1)S(1)} %pad_maximum_fusion), channel_id=1, source_target_pairs={{0,4},{1,5},{2,6},{3,7},{4,0},{5,1},{6,2},{7,3},{8,12},{9,13},{10,... | collective-permute-start | bytes 2850824 | tf_op jit(solution)/shard_map/ppermute | solution.py:511
  66.5 21.4 %collective-permute-start.15 = (bf16[1792,256]{1,0:T(8,128)(2,1)S(1)}, bf16[1792,256]{1,0:T(8,128)(2,1)S(1)}, u32[]{:S(2)}, u32[]{:S(2)}) collective-permute-start(bf16[1792,256]{1,0:T(8,128)(2,1)S(1)} %collective-permute-done.12.refs_15_), channel_id=1, source_target_pairs={{0,16},{16,0},{1,17},{17,1},{2,18},{18,2},{3,19},{19,3},{4,20},{20... | collective-permute-start | bytes 2752520 | tf_op jit(solution)/shard_map/ppermute | solution.py:523
  67.0 21.2 %collective-permute-start.16 = (bf16[512,896]{1,0:T(8,128)(2,1)S(1)}, bf16[512,896]{1,0:T(8,128)(2,1)}, u32[]{:S(2)}, u32[]{:S(2)}) collective-permute-start(bf16[512,896]{1,0:T(8,128)(2,1)S(1)} %copy-done.14), channel_id=1, source_target_pairs={{0,2},{1,3},{2,0},{3,1},{4,6},{5,7},{6,4},{7,5},{8,10},{9,11},{10,... | collective-permute-start | bytes 2752520 | tf_op jit(solution)/shard_map/ppermute | solution.py:511
  68.5 19.7 %collective-permute-start.17 = (bf16[1792,256]{1,0:T(8,128)(2,1)S(1)}, bf16[1792,256]{1,0:T(8,128)(2,1)S(1)}, u32[]{:S(2)}, u32[]{:S(2)}) collective-permute-start(bf16[1792,256]{1,0:T(8,128)(2,1)S(1)} %collective-permute-done.11.refs_10_), channel_id=1, source_target_pairs={{0,1},{1,0},{2,3},{3,2},{4,5},{5,4},{6,7},{7,6},{8,9},{9,8},{10,11... | collective-permute-start | bytes 2752520 | tf_op jit(solution)/shard_map/ppermute | solution.py:511
  68.5 19.7 %collective-permute-start.18 = (bf16[1792,256]{1,0:T(8,128)(2,1)S(1)}, bf16[1792,256]{1,0:T(8,128)(2,1)S(1)}, u32[]{:S(2)}, u32[]{:S(2)}) collective-permute-start(bf16[1792,256]{1,0:T(8,128)(2,1)S(1)} %collective-permute-done.12.refs_15_), channel_id=1, source_target_pairs={{0,1},{1,0},{2,3},{3,2},{4,5},{5,4},{6,7},{7,6},{8,9},{9,8},{10,11... | collective-permute-start | bytes 2752520 | tf_op jit(solution)/shard_map/ppermute | solution.py:511
  72.4 22.5 %copy-start.8 = (bf16[128,576]{1,0:T(8,128)(2,1)}, bf16[128,576]{1,0:T(8,128)(2,1)S(1)}, u32[]{:S(2)}) copy-start(bf16[128,576]{1,0:T(8,128)(2,1)S(1)} %get-tuple-element.112) | copy-start | bytes 442372
  87.8 7.4 %copy-start.17 = (bf16[1792,256]{1,0:T(8,128)(2,1)}, bf16[1792,256]{1,0:T(8,128)(2,1)S(1)}, u32[]{:S(2)}) copy-start(bf16[1792,256]{1,0:T(8,128)(2,1)S(1)} %collective-permute-done.15.refs_16_) | copy-start | bytes 2752516
  88.2 7.1 %copy-start.18 = (bf16[1792,256]{1,0:T(8,128)(2,1)}, bf16[1792,256]{1,0:T(8,128)(2,1)S(1)}, u32[]{:S(2)}) copy-start(bf16[1792,256]{1,0:T(8,128)(2,1)S(1)} %collective-permute-done.17.refs_12_) | copy-start | bytes 2752516
  88.2 7.1 %copy-start.19 = (bf16[1792,256]{1,0:T(8,128)(2,1)}, bf16[1792,256]{1,0:T(8,128)(2,1)S(1)}, u32[]{:S(2)}) copy-start(bf16[1792,256]{1,0:T(8,128)(2,1)S(1)} %collective-permute-done.18.refs_17_) | copy-start | bytes 2752516
  88.2 9.4 %copy-start.3 = (bf16[128,3712]{1,0:T(8,128)(2,1)}, bf16[128,3712]{1,0:T(8,128)(2,1)S(1)}, u32[]{:S(2)}) copy-start(bf16[128,3712]{1,0:T(8,128)(2,1)S(1)} %collective-permute-done.14.refs_4_.refs_0_) | copy-start | bytes 2850820
  88.2 7.0 %collective-permute-start.19 = (bf16[1792,256]{1,0:T(8,128)(2,1)S(1)}, bf16[1792,256]{1,0:T(8,128)(2,1)S(1)}, u32[]{:S(2)}, u32[]{:S(2)}) collective-permute-start(bf16[1792,256]{1,0:T(8,128)(2,1)S(1)} %collective-permute-done.15.refs_16_), channel_id=1, source_target_pairs={{0,1},{1,0},{2,3},{3,2},{4,5},{5,4},{6,7},{7,6},{8,9},{9,8},{10,11... | collective-permute-start | bytes 2752520 | tf_op jit(solution)/shard_map/ppermute | solution.py:511
  88.3 23.4 %collective-permute-start.23 = (bf16[512,896]{1,0:T(8,128)(2,1)}, bf16[512,896]{1,0:T(8,128)(2,1)S(1)}, u32[]{:S(2)}, u32[]{:S(2)}) collective-permute-start(bf16[512,896]{1,0:T(8,128)(2,1)} %collective-permute-done.16.refs_2_), channel_id=1, source_target_pairs={{0,16},{16,0},{1,17},{17,1},{2,18},{18,2},{3,19},{19,3},{4,20},{20... | collective-permute-start | bytes 2752520 | tf_op jit(solution)/shard_map/ppermute | solution.py:523
  89.9 21.8 %collective-permute-start.24 = (bf16[512,896]{1,0:T(8,128)(2,1)}, bf16[512,896]{1,0:T(8,128)(2,1)}, u32[]{:S(2)}, u32[]{:S(2)}) collective-permute-start(bf16[512,896]{1,0:T(8,128)(2,1)} %collective-permute-done.16.refs_2_), channel_id=1, source_target_pairs={{0,1},{1,0},{2,3},{3,2},{4,5},{5,4},{6,7},{7,6},{8,9},{9,8},{10,11... | collective-permute-start | bytes 2752520 | tf_op jit(solution)/shard_map/ppermute | solution.py:511
  92.2 19.4 %collective-permute-start.21 = (bf16[128,576]{1,0:T(8,128)(2,1)S(1)}, bf16[128,576]{1,0:T(8,128)(2,1)S(1)}, u32[]{:S(2)}, u32[]{:S(2)}) collective-permute-start(bf16[128,576]{1,0:T(8,128)(2,1)S(1)} %latent_parts.3), channel_id=1, source_target_pairs={{0,8},{1,9},{2,10},{3,11},{4,12},{5,13},{6,14},{7,15},{8,0},{9,1},... | collective-permute-start | bytes 442376 | tf_op jit(solution)/shard_map/ppermute | solution.py:511
  94.9 16.8 %collective-permute-start.20 = (bf16[128,576]{1,0:T(8,128)(2,1)}, bf16[128,576]{1,0:T(8,128)(2,1)S(1)}, u32[]{:S(2)}, u32[]{:S(2)}) collective-permute-start(bf16[128,576]{1,0:T(8,128)(2,1)} %get-tuple-element.100), channel_id=1, source_target_pairs={{0,4},{1,5},{2,6},{3,7},{4,0},{5,1},{6,2},{7,3},{8,12},{9,13},{10,... | collective-permute-start | bytes 442376 | tf_op jit(solution)/shard_map/ppermute | solution.py:511
  95.3 0.9 copy-start.20
  96.2 15.5 %collective-permute-start.22 = (bf16[128,576]{1,0:T(8,128)(2,1)}, bf16[128,576]{1,0:T(8,128)(2,1)S(1)}, u32[]{:S(2)}, u32[]{:S(2)}) collective-permute-start(bf16[128,576]{1,0:T(8,128)(2,1)} %get-tuple-element.101), channel_id=1, source_target_pairs={{0,12},{1,13},{2,14},{3,15},{4,8},{5,9},{6,10},{7,11},{8,4},{9,5},... | collective-permute-start | bytes 442376 | tf_op jit(solution)/shard_map/ppermute | solution.py:511
  97.6 14.5 %copy-start.9 = (bf16[128,576]{1,0:T(8,128)(2,1)S(1)}, bf16[128,576]{1,0:T(8,128)(2,1)}, u32[]{:S(2)}) copy-start(bf16[128,576]{1,0:T(8,128)(2,1)} %copy-done.8) | copy-start | bytes 442372
  97.6 16.6 %copy-start = (bf16[1024,896]{1,0:T(8,128)(2,1)S(1)}, bf16[1024,896]{1,0:T(8,128)(2,1)}, u32[]{:S(2)}) copy-start(bf16[1024,896]{1,0:T(8,128)(2,1)} %refs_0_.2) | copy-start | bytes 5505028
  111.7 2.5 %collective-permute-start.25 = (bf16[512,896]{1,0:T(8,128)(2,1)S(1)}, bf16[512,896]{1,0:T(8,128)(2,1)S(1)}, u32[]{:S(2)}, u32[]{:S(2)}) collective-permute-start(bf16[512,896]{1,0:T(8,128)(2,1)S(1)} %collective-permute-done.23.refs_3_), channel_id=1, source_target_pairs={{0,1},{1,0},{2,3},{3,2},{4,5},{5,4},{6,7},{7,6},{8,9},{9,8},{10,11... | collective-permute-start | bytes 2752520 | tf_op jit(solution)/shard_map/ppermute | solution.py:511
  111.8 16.0 %collective-permute-start.27 = (bf16[128,1792]{1,0:T(8,128)(2,1)}, bf16[128,1792]{1,0:T(8,128)(2,1)}, u32[]{:S(2)}, u32[]{:S(2)}) collective-permute-start(bf16[128,1792]{1,0:T(8,128)(2,1)} %get-tuple-element.110), channel_id=1, source_target_pairs={{0,4},{1,5},{2,6},{3,7},{4,0},{5,1},{6,2},{7,3},{8,12},{9,13},{10,... | collective-permute-start | bytes 1376264 | tf_op jit(solution)/shard_map/ppermute | solution.py:511
  114.2 7.7 %copy-start.22 = (f32[512]{0:T(512)S(1)}, f32[512]{0:T(512)}, u32[]{:S(2)}) copy-start(f32[512]{0:T(512)} %param.13) | copy-start | bytes 6148
  120.7 1.0 copy-start.11
  121.6 14.7 %collective-permute-start.26 = (bf16[128,1792]{1,0:T(8,128)(2,1)S(1)}, bf16[128,1792]{1,0:T(8,128)(2,1)S(1)}, u32[]{:S(2)}, u32[]{:S(2)}) collective-permute-start(bf16[128,1792]{1,0:T(8,128)(2,1)S(1)} %get-tuple-element.109), channel_id=1, source_target_pairs={{0,4},{1,5},{2,6},{3,7},{4,0},{5,1},{6,2},{7,3},{8,12},{9,13},{10,... | collective-permute-start | bytes 1376264 | tf_op jit(solution)/shard_map/ppermute | solution.py:511
  123.4 14.8 %collective-permute-start.28 = (bf16[4,16,576]{2,1,0:T(8,128)(2,1)S(1)}, bf16[4,16,576]{2,1,0:T(8,128)(2,1)S(1)}, u32[]{:S(2)}, u32[]{:S(2)}) collective-permute-start(bf16[4,16,576]{2,1,0:T(8,128)(2,1)S(1)} %get-tuple-element.136), channel_id=1, source_target_pairs={{0,4},{1,5},{2,6},{3,7},{4,0},{5,1},{6,2},{7,3},{8,12},{9,13},{10,... | collective-permute-start | bytes 221192 | tf_op jit(solution)/shard_map/ppermute | solution.py:511
  125.2 12.9 %collective-permute-start.29 = (bf16[4,16,576]{2,1,0:T(8,128)(2,1)S(1)}, bf16[4,16,576]{2,1,0:T(8,128)(2,1)S(1)}, u32[]{:S(2)}, u32[]{:S(2)}) collective-permute-start(bf16[4,16,576]{2,1,0:T(8,128)(2,1)S(1)} %get-tuple-element.135), channel_id=1, source_target_pairs={{0,8},{1,9},{2,10},{3,11},{4,12},{5,13},{6,14},{7,15},{8,0},{9,1},... | collective-permute-start | bytes 221192 | tf_op jit(solution)/shard_map/ppermute | solution.py:511
  127.3 14.1 %collective-permute-start.30 = (bf16[4,16,576]{2,1,0:T(8,128)(2,1)S(1)}, bf16[4,16,576]{2,1,0:T(8,128)(2,1)S(1)}, u32[]{:S(2)}, u32[]{:S(2)}) collective-permute-start(bf16[4,16,576]{2,1,0:T(8,128)(2,1)S(1)} %get-tuple-element.134), channel_id=1, source_target_pairs={{0,12},{1,13},{2,14},{3,15},{4,8},{5,9},{6,10},{7,11},{8,4},{9,5},... | collective-permute-start | bytes 221192 | tf_op jit(solution)/shard_map/ppermute | solution.py:511
  137.8 4.8 %copy-start.12 = (bf16[128,3584]{1,0:T(8,128)(2,1)S(1)}, bf16[128,3584]{1,0:T(8,128)(2,1)}, u32[]{:S(2)}) copy-start(bf16[128,3584]{1,0:T(8,128)(2,1)} %copy-done.11) | copy-start | bytes 2752516
  141.5 1.1 copy-start.21
  142.6 42.2 %collective-permute-start.31 = (bf16[128,3584]{1,0:T(8,128)(2,1)S(1)}, bf16[128,3584]{1,0:T(8,128)(2,1)S(1)}, u32[]{:S(2)}, u32[]{:S(2)}) collective-permute-start(bf16[128,3584]{1,0:T(8,128)(2,1)S(1)} %copy-done.12), channel_id=1, source_target_pairs={{0,4},{1,5},{2,6},{3,7},{4,0},{5,1},{6,2},{7,3},{8,12},{9,13},{10,... | collective-permute-start | bytes 2752520 | tf_op jit(solution)/shard_map/ppermute | solution.py:511
  142.6 42.2 %collective-permute-start.32 = (bf16[128,3584]{1,0:T(8,128)(2,1)}, bf16[128,3584]{1,0:T(8,128)(2,1)}, u32[]{:S(2)}, u32[]{:S(2)}) collective-permute-start(bf16[128,3584]{1,0:T(8,128)(2,1)} %add_convert_fusion.1), channel_id=1, source_target_pairs={{0,12},{1,13},{2,14},{3,15},{4,8},{5,9},{6,10},{7,11},{8,4},{9,5},... | collective-permute-start | bytes 2752520 | tf_op jit(solution)/shard_map/ppermute | solution.py:511
  144.2 6.4 %collective-permute-start.33 = (bf16[4,2,16,576]{3,2,0,1:T(8,128)(2,1)S(1)}, bf16[4,2,16,576]{3,2,0,1:T(8,128)(2,1)S(1)}, u32[]{:S(2)}, u32[]{:S(2)}) collective-permute-start(bf16[4,2,16,576]{3,2,0,1:T(8,128)(2,1)S(1)} %get-tuple-element.132), channel_id=1, source_target_pairs={{0,2},{1,3},{2,0},{3,1},{4,6},{5,7},{6,4},{7,5},{8,10},{9,11},{10,... | collective-permute-start | bytes 442376 | tf_op jit(solution)/shard_map/ppermute | solution.py:511
  150.7 1.5 collective-permute-start.34

commit v4 on v3

--- a/solution.py
+++ b/solution.py
@@ -155,14 +155,13 @@
 
 
 def entry_kernel(
-    place_ref, tokens_ref, gain_ref, index_ref, route_ref, weight_ref,
-    rows0_ref, rows1_ref, half_ref, sem,
+    place_ref, tokens_ref, gain_ref, index_ref, route_ref, weight_ref, rows_ref, half_ref, sem
 ):
     rows = half_ref.shape[0]
     copy = pltpu.make_async_copy(weight_ref.at[pl.ds(place_ref[1] * rows, rows)], half_ref, sem)
     copy.start()
     tok_rows, features = tokens_ref.shape
-    some = rows0_ref.shape[0]
+    some = tok_rows // 2
     row = lax.broadcasted_iota(jnp.int32, (SCALE_COLUMNS, tok_rows), 0)
     expert, term = row // 3, row % 3
     left = jnp.zeros((SCALE_COLUMNS, tok_rows), jnp.float32)
@@ -175,7 +174,7 @@
         terms = jnp.where(term == number, rounded, terms)
         left = left - rounded
     terms = terms.T.astype(jnp.bfloat16)
-    for part, ref in enumerate((rows0_ref, rows1_ref)):
+    for part in range(2):
         mine = slice(part * some, (part + 1) * some)
         values = tokens_ref[mine].astype(jnp.float32)
         scale = lax.rsqrt(jnp.mean(values * values, axis=-1, keepdims=True) + eps)
@@ -183,26 +182,24 @@
         for piece in range(gain_ref.shape[0]):
             at_piece = slice(piece * lanes, (piece + 1) * lanes)
             values = tokens_ref[mine, at_piece].astype(jnp.float32)
-            ref[:, at_piece] = (values * scale * gain_ref[piece : piece + 1, :]).astype(jnp.bfloat16)
-        ref[:, features:] = terms[mine]
+            rows_ref[mine, at_piece] = (values * scale * gain_ref[piece : piece + 1, :]).astype(jnp.bfloat16)
+        rows_ref[mine, features:] = terms[mine]
     copy.wait()
 
 
 def entry(place, tokens, gain, expert_index, route_gate, weight):
-    some, features = tokens.shape[0] // 2, tokens.shape[1]
+    tok_rows, features = tokens.shape
     smem, vmem, hbm = (
         pl.BlockSpec(memory_space=space) for space in (pltpu.SMEM, pltpu.VMEM, pltpu.HBM)
     )
-    rows = pltpu.VMEM((some, features + SCALE_COLUMNS), jnp.bfloat16)
     return pl.pallas_call(
         entry_kernel,
         out_shape=[
-            rows,
-            rows,
+            pltpu.VMEM((tok_rows, features + SCALE_COLUMNS), jnp.bfloat16),
             pltpu.VMEM((weight.shape[0] // 2, weight.shape[1]), weight.dtype),
         ],
         in_specs=[smem, vmem, vmem, vmem, vmem, hbm],
-        out_specs=[vmem] * 3,
+        out_specs=[vmem] * 2,
         scratch_shapes=[pltpu.SemaphoreType.DMA],
         cost_estimate=BRIEF,
         name="entry",
@@ -312,13 +309,13 @@
 
 
 def hidden_kernel(place_ref, *refs):
-    row_refs, gate_refs, up_refs, refs = refs[:7], refs[7:13], refs[13:19], refs[19:]
+    row_refs, gate_refs, up_refs, refs = refs[:4], refs[4:10], refs[10:16], refs[16:]
     down_refs, (hidden_ref, scale_ref, part_ref), refs = refs[:2], refs[2:5], refs[5:]
     rows_buf, gate_buf, up_buf, down_buf = refs[:4]
     row_sems, gate_sems, up_sems, down_sems = refs[4:]
     place, rep, plane = place_ref[0], place_ref[1], place_ref[2]
     core = place & 1
-    some = row_refs[0].shape[0]
+    tok_rows = row_refs[0].shape[0]
     row_copies, first = [], 0
     for index, ref in enumerate(row_refs):
         target = rows_buf.at[pl.ds(first, ref.shape[0])]
@@ -360,7 +357,9 @@
         await_block(down_buf, down_sems, slot, core ^ slot)
         width = down_buf.shape[2]
         part_ref[:, slot * width : (slot + 1) * width] = weighed(
-            hidden_ref[4 * some : 6 * some], scale_ref[4 * some : 6 * some], down_buf[slot]
+            hidden_ref[2 * tok_rows : 3 * tok_rows],
+            scale_ref[2 * tok_rows : 3 * tok_rows],
+            down_buf[slot],
         )
 
 
@@ -370,13 +369,13 @@
 
 
 def hidden_units(place, rows, gates, ups, near):
-    some, extended = rows[0].shape
+    tok_rows, extended = rows[0].shape
     features, units = gates[0].shape
     columns = near[0].shape[1]
     hbm, vmem = pl.BlockSpec(memory_space=pltpu.HBM), pl.BlockSpec(memory_space=pltpu.VMEM)
     bf16, dma = jnp.bfloat16, pltpu.SemaphoreType.DMA
     operands = (*rows, *gates, *ups, *near)
-    late = [rows[4], ups[3], ups[4], ups[5], gates[5]]
+    late = [rows[2], ups[3], ups[4], ups[5], gates[5]]
     specs = [
         pl.BlockSpec(memory_space=pl.ANY if any(each is one for one in late) else pltpu.HBM)
         for each in operands
@@ -384,14 +383,14 @@
     return pl.pallas_call(
         hidden_kernel,
         out_shape=[
-            pltpu.VMEM((2 * LINE * some, GROUP * units), bf16),
-            pltpu.VMEM((2 * LINE * some, 1), jnp.float32),
+            pltpu.VMEM((LINE * tok_rows, GROUP * units), bf16),
+            pltpu.VMEM((LINE * tok_rows, 1), jnp.float32),
         ]
-        + [pltpu.VMEM((2 * some, 2 * columns), bf16)],
+        + [pltpu.VMEM((tok_rows, 2 * columns), bf16)],
         in_specs=[pl.BlockSpec(memory_space=pltpu.SMEM)] + specs,
         out_specs=[vmem] * 3,
         scratch_shapes=[
-            pltpu.VMEM((2 * LINE * some, extended), bf16),
+            pltpu.VMEM((LINE * tok_rows, extended), bf16),
             pltpu.VMEM((GROUP, features, units), bf16),
             pltpu.VMEM((GROUP, features, units), bf16),
             pltpu.VMEM((2, GROUP * units, columns), bf16),
@@ -528,40 +527,39 @@
     def wide(value):
         return value.astype(jnp.float32)
 
-    some = tokens.shape[0] // 2
     slots = cache_slots(owner, device_count, push_cap)
 
-    gate_core, up_core = other_core(gate_weight), other_core(up_weight)
     kv_core, kv_x = other_core(kv_weight), other_chip(kv_weight)
-    rows0, rows1, gate_half = entry(
+    gate_own, up_own, place_info = hold((gate_weight, up_weight, place_info))
+    gate_core, up_core = other_core(gate_own), other_core(up_own)
+    rows, gate_half = entry(
         place_info, tokens, norm_gain, expert_index, route_gate, gate_weight
     )
-    rows0, rows1, gate_half, gate_core, up_core, kv_core, kv_x, up_own, down_own = hold(
-        (rows0, rows1, gate_half, gate_core, up_core, kv_core, kv_x, up_weight, down_weight)
-    )
-
-    f0, a0 = across_line(rows0, 3), across_line(rows0, 1)
+    rows, gate_half, gate_core, up_core, kv_core, kv_x, up_own, down_own = hold(
+        (rows, gate_half, gate_core, up_core, kv_core, kv_x, up_weight, down_weight)
+    )
+
+    f = across_line(rows, 3)
     gate_x = other_chip(gate_half)
     down_core, kv_x_core = other_core(down_own), other_core(kv_x)
     up_half, down_half = halves_of(place_info, up_own, down_own)
-    f0, a0, gate_x, down_core, kv_x_core, up_half, down_half, later, slots = hold(
-        (f0, a0, gate_x, down_core, kv_x_core, up_half, down_half, rows1, slots)
+    rows, up_half = hold((rows, up_half))
+    a = across_line(rows, 1)
+    gate_x, down_core, kv_x_core, up_half, down_half, slots = hold(
+        (gate_x, down_core, kv_x_core, up_half, down_half, slots)
     )
     kv_parts = (kv_weight, kv_core, kv_x, kv_x_core)
 
-    f1, a1 = across_line(later, 3), across_line(later, 1)
     gate_y = other_rep(gate_x)
     up_x = other_chip(up_half)
     gate_x_core = other_core(gate_x)
-    f0, f1, a1, gate_y, up_x, gate_x_core, down_half = hold(
-        (f0, f1, a1, gate_y, up_x, gate_x_core, down_half)
-    )
-
-    c = across_line(jnp.concatenate([f0, f1]), 1)
+    gate_y, up_x, gate_x_core, down_half = hold((gate_y, up_x, gate_x_core, down_half))
+
+    c = across_line(f, 1)
     up_y = other_rep(up_x)
     down_x = other_chip(down_half)
     latent0, latent1, latent3 = latent_parts(
-        place_info, (rows0, later, a0, a1, f0, f1), kv_parts, 2 * some
+        place_info, (rows, a, f), kv_parts, tokens.shape[0]
     )
     gate_y_core, up_x_core = other_core(gate_y), other_core(up_x)
     c, up_y, down_x, gate_y_core, up_x_core, latent1, latent3 = hold(
@@ -570,11 +568,11 @@
 
     up_y_core = other_core(up_y)
     down_y, down_x_core = other_rep(down_x), other_core(down_x)
-    (latent2,) = latent_parts(place_info, (c,), kv_parts, 2 * some)
+    (latent2,) = latent_parts(place_info, (c,), kv_parts, tokens.shape[0])
     latents = [across_line(value, k) for k, value in ((1, latent1), (2, latent2), (3, latent3))]
     hidden, scale, near2 = hidden_units(
         place_info,
-        (rows0, later, a0, a1, c, f0, f1),
+        (rows, a, c, f),
         (gate_weight, gate_core, gate_x, gate_y, gate_x_core, gate_y_core),
         (up_weight, up_core, up_x, up_y, up_x_core, up_y_core),
         (down_weight, down_core),

time: 188 us -> 185 us (0.984)
  waiting for transfers between devices: 105 us -> 81.4 us
  starting transfers between devices: 31.5 us -> 47.8 us
  local copies, waits for them, and re-layouts: 4.8 us -> 7.34 us
    ppermute x32 -> x30, starting transfers between devices: 27.9 us -> 43.9 us  [exchange(): lax.ppermute(value, 'dev', [(i, i ^ distance) for i in range(device_count)])]
    ppermute x3, waiting for transfers between devices: 15.4 us -> 1.56 us  [other_rep(): return lax.ppermute(value, 'rep', [(0, 1), (1, 0)])]
    ppermute x32 -> x30, waiting for transfers between devices: 89.1 us -> 79.8 us  [exchange(): lax.ppermute(value, 'dev', [(i, i ^ distance) for i in range(device_count)])]
    unnamed x49 -> x53, local copies, waits for them, and re-layouts: 4.72 us -> 7.26 us
  transfers between devices with their start and end apart: 35 -> 33, of which waited for: 14 -> 13; matrix products, arithmetic and copies ran while one was open for 5% -> 5% of each run, Pallas kernels for 19% -> 19%
where the time goes in v4:
time: 185 us
  waiting for transfers between devices  81.4 us (44%)
  starting transfers between devices  47.8 us (26%)
  Pallas kernels  35.1 us (19%)
  other arithmetic  12.1 us (7%)
  local copies, waits for them, and re-layouts  7.34 us (4%)
    ppermute x30, waiting for transfers between devices, exchange(): lax.ppermute(value, 'dev', [(i, i ^ distance) for i in range(device_count)])  79.8 us
    ppermute x30, starting transfers between devices, exchange(): lax.ppermute(value, 'dev', [(i, i ^ distance) for i in range(device_count)])  43.9 us
    pallas_call x1, Pallas kernels, hidden_units(): pl.pallas_call(hidden_kernel, out_shape=[pltpu.VMEM((LINE * tok_rows, GRO...  14 us
    unnamed x53, local copies, waits for them, and re-layouts  7.26 us
    pallas_call x1, Pallas kernels, rest_products(): pl.pallas_call(rest_kernel, out_shape=[pltpu.VMEM((tok_rows, GROUP * widt...  6.67 us
    pallas_call x2, Pallas kernels, latent_parts(): pl.pallas_call(functools.partial(latent_kernel, len(rows)), out_shape=[pl...  5.44 us
    ppermute x3, starting transfers between devices, other_rep(): return lax.ppermute(value, 'rep', [(0, 1), (1, 0)])  3.86 us
    convert_element_type x2, other arithmetic, narrow(): return value.astype(jnp.bfloat16)  3.84 us
  transfers between devices with their start and end apart: 33, of which 13 were waited for; matrix products, arithmetic and copies ran while one was open for 5% of the time, Pallas kernels for 19%

profile of v4, /device:TPU:0, one launch (start us, length us, event | category | flops | bytes accessed | tf_op | source)
XLA Modules:
  0.0 184.7 jit_solution(1815850738366929094)
XLA Ops:
  0.7 0.7 pad_add_fusion.place_ref
  1.3 0.5 collective-permute-start
  1.8 0.5 collective-permute-start.2
  2.3 2.5 %collective-permute-start.3 = (bf16[224,576]{1,0:T(8,128)(2,1)}, bf16[224,576]{1,0:T(8,128)(2,1)}, u32[]{:S(2)}, u32[]{:S(2)}) collective-permute-start(bf16[224,576]{1,0:T(8,128)(2,1)} %refs_1_.2), channel_id=1, source_target_pairs={{0,2},{1,3},{2,0},{3,1},{4,6},{5,7},{6,4},{7,5},{8,10},{9,11},{10,... | collective-permute-start | bytes 774152 | tf_op jit(solution)/shard_map/ppermute | solution.py:510
  4.8 3.3 %entry.1 = (bf16[128,3712]{1,0:T(8,128)(2,1)S(1)}, bf16[1792,256]{1,0:T(8,128)(2,1)}) custom-call(s32[3]{0:T(128)} %pad_add_fusion.place_ref, bf16[128,3584]{1,0:T(8,128)(2,1)} %tokens_ref.1, f32[28,128]{1,0:T(8,128)} %bitcast.42, s32[2,128]{1,0:T(2,128)} %bitcast.45, f32[2,128]{1,0:T(2,128)} %bitcast.46, bf16[3584,256]{1,0:T(8,128)(2,1)} %refs_4_.1), custom_call_target="tpu_custom_call" | custom-call | flops 1048576 | bytes 1048576 | tf_op jit(solution)/shard_map/entry/pallas_call | solution.py:195
  8.1 4.5 %collective-permute-done.3.refs_5_.refs_3_ = bf16[224,576]{1,0:T(8,128)(2,1)} collective-permute-done((bf16[224,576]{1,0:T(8,128)(2,1)}, bf16[224,576]{1,0:T(8,128)(2,1)}, u32[]{:S(2)}, u32[]{:S(2)}) %collective-permute-start.3) | collective-permute-done | bytes 258080 | tf_op jit(solution)/shard_map/ppermute | solution.py:510
  12.6 1.8 collective-permute-start.7
  14.5 0.2 reduce_window_sum.11
  14.7 0.2 collective-permute-start.9
  14.9 0.2 select_reduce_fusion
  15.1 3.7 %collective-permute-start.5 = (bf16[128,3712]{1,0:T(8,128)(2,1)S(1)}, bf16[128,3712]{1,0:T(8,128)(2,1)}, u32[]{:S(2)}, u32[]{:S(2)}) collective-permute-start(bf16[128,3712]{1,0:T(8,128)(2,1)S(1)} %get-tuple-element.69.refs_0_), channel_id=1, source_target_pairs={{0,12},{1,13},{2,14},{3,15},{4,8},{5,9},{6,10},{7,11},{8,4},{9,5},... | collective-permute-start | bytes 2850824 | tf_op jit(solution)/shard_map/ppermute | solution.py:510
  18.8 3.1 %weight_halves.1 = (bf16[1792,256]{1,0:T(8,128)(2,1)}, bf16[512,896]{1,0:T(8,128)(2,1)S(1)}) custom-call(s32[3]{0:T(128)} %pad_add_fusion.place_ref, bf16[3584,256]{1,0:T(8,128)(2,1)} %refs_10_.1, bf16[1024,896]{1,0:T(8,128)(2,1)} %refs_0_.2), custom_call_target="tpu_custom_call" | custom-call | flops 1048576 | bytes 1048576 | tf_op jit(solution)/shard_map/weight_halves/pallas_call | solution.py:228
  21.9 0.9 copy-done.14
  22.8 0.5 multiply_add_fusion
  23.3 12.3 %collective-permute-done.7.refs_6_ = bf16[1792,256]{1,0:T(8,128)(2,1)} collective-permute-done((bf16[1792,256]{1,0:T(8,128)(2,1)}, bf16[1792,256]{1,0:T(8,128)(2,1)}, u32[]{:S(2)}, u32[]{:S(2)}) %collective-permute-start.7) | collective-permute-done | bytes 917536 | tf_op jit(solution)/shard_map/ppermute | solution.py:510
  35.7 1.8 collective-permute-start.10
  37.5 1.5 collective-permute-start.11
  38.9 2.1 %collective-permute-done.5.refs_2_.refs_3_ = bf16[128,3712]{1,0:T(8,128)(2,1)} collective-permute-done((bf16[128,3712]{1,0:T(8,128)(2,1)S(1)}, bf16[128,3712]{1,0:T(8,128)(2,1)}, u32[]{:S(2)}, u32[]{:S(2)}) %collective-permute-start.5) | collective-permute-done | bytes 950304 | tf_op jit(solution)/shard_map/ppermute | solution.py:510
  41.0 19.5 %collective-permute-start.6 = (bf16[128,3712]{1,0:T(8,128)(2,1)}, bf16[128,3712]{1,0:T(8,128)(2,1)S(1)}, u32[]{:S(2)}, u32[]{:S(2)}) collective-permute-start(bf16[128,3712]{1,0:T(8,128)(2,1)} %collective-permute-done.5.refs_2_.refs_3_), channel_id=1, source_target_pairs={{0,4},{1,5},{2,6},{3,7},{4,0},{5,1},{6,2},{7,3},{8,12},{9,13},{10,... | collective-permute-start | bytes 2850824 | tf_op jit(solution)/shard_map/ppermute | solution.py:510
  60.6 1.0 copy-done.17
  61.5 1.5 collective-permute-start.13
  63.0 0.5 collective-permute-start.14
  63.6 0.5 collective-permute-start.16
  64.1 3.3 %latent_parts.2 = (bf16[128,576]{1,0:T(8,128)(2,1)S(1)}, bf16[128,576]{1,0:T(8,128)(2,1)}, bf16[128,576]{1,0:T(8,128)(2,1)}) custom-call(s32[3]{0:T(128)S(1)} %copy-done.9, bf16[128,3712]{1,0:T(8,128)(2,1)S(1)} %get-tuple-element.69.refs_0_, bf16[128,3712]{1,0:T(8,128)(2,1)S(1)} %collective-permute-done.4.refs_1_, ...), custom_call_target="tpu_custom_call" | custom-call | flops 1048576 | bytes 1048576 | tf_op jit(solution)/shard_map/latent_parts/pallas_call | solution.py:293
  67.4 14.0 %collective-permute-done.6.refs_2_.refs_0_ = bf16[128,3712]{1,0:T(8,128)(2,1)S(1)} collective-permute-done((bf16[128,3712]{1,0:T(8,128)(2,1)}, bf16[128,3712]{1,0:T(8,128)(2,1)S(1)}, u32[]{:S(2)}, u32[]{:S(2)}) %collective-permute-start.6) | collective-permute-done | bytes 950304 | tf_op jit(solution)/shard_map/ppermute | solution.py:510
  81.5 1.6 collective-permute-done.13.refs_13_
  83.0 1.4 collective-permute-done.14.refs_2_
  84.6 0.6 collective-permute-start.21
  85.2 0.2 collective-permute-start.22
  85.3 2.1 %latent_parts.3 = bf16[128,576]{1,0:T(8,128)(2,1)S(1)} custom-call(s32[3]{0:T(128)S(1)} %copy-done.10, bf16[128,3712]{1,0:T(8,128)(2,1)S(1)} %collective-permute-done.6.refs_2_.refs_0_, bf16[224,576]{1,0:T(8,128)(2,1)S(1)} %copy-done.4, bf16[224,576]{1,0:T(8,128)(2,1)S(1)} %collective-permute-done.2.refs_4_.refs_2_, ...), custom_call_target="tpu_custom_call" | custom-call | flops 1048576 | bytes 1048576 | tf_op jit(solution)/shard_map/latent_parts/pallas_call | solution.py:293
  87.5 1.4 collective-permute-start.19
  88.9 1.7 collective-permute-start.18
  90.6 0.9 copy-done.21
  91.5 1.4 collective-permute-start.20
  92.9 0.7 copy-done.11
  93.6 14.0 %hidden_units.1 = (bf16[512,1024]{1,0:T(8,128)(2,1)S(1)}, f32[512,1]{1,0:T(8,128)S(1)}, bf16[128,1792]{1,0:T(8,128)(2,1)}) custom-call(s32[3]{0:T(128)S(1)} %copy-done.11, bf16[128,3712]{1,0:T(8,128)(2,1)} %copy-done.2, bf16[128,3712]{1,0:T(8,128)(2,1)} %copy-done.3, bf16[128,3712]{1,0:T(8,128)(2,1)} %copy-done.1, ...), custom_call_target="tpu_custom_call" | custom-call | flops 1048576 | bytes 1048576 | tf_op jit(solution)/shard_map/hidden_units/pallas_call | solution.py:383
  107.9 1.0 add_add_fusion
  108.9 0.1 multiply_reduce_fusion
  109.0 0.3 fusion.16
  109.3 0.9 collective-permute-done.23.refs_5_
  110.2 6.7 %rest_products.1 = (bf16[128,3584]{1,0:T(8,128)(2,1)S(1)}, bf16[128,3584]{1,0:T(8,128)(2,1)S(1)}, bf16[128,3584]{1,0:T(8,128)(2,1)S(1)}, bf16[128,1792]{1,0:T(8,128)(2,1)S(1)}) custom-call(s32[3]{0:T(128)S(1)} %copy-done.11, bf16[512,1024]{1,0:T(8,128)(2,1)S(1)} %get-tuple-element.97.hidden_ref, f32[512,1]{1,0:T(8,128)S(1)} %get-tuple-element.98.scale_ref, ...), custom_call_target="tpu_custom_call" | custom-call | flops 1048576 | bytes 1048576 | tf_op jit(solution)/shard_map/rest_products/pallas_call | solution.py:436
  116.9 0.9 copy-done.5
  117.8 1.0 copy-done.12
  118.8 1.1 collective-permute-start.24
  120.0 1.3 scatter_custom_fusion
  121.4 0.9 collective-permute-start.26
  122.3 2.2 %collective-permute-start.27 = (bf16[4,16,576]{2,1,0:T(8,128)(2,1)S(1)}, bf16[4,16,576]{2,1,0:T(8,128)(2,1)S(1)}, u32[]{:S(2)}, u32[]{:S(2)}) collective-permute-start(bf16[4,16,576]{2,1,0:T(8,128)(2,1)S(1)} %get-tuple-element.129), channel_id=1, source_target_pairs={{0,8},{1,9},{2,10},{3,11},{4,12},{5,13},{6,14},{7,15},{8,0},{9,1},... | collective-permute-start | bytes 221192 | tf_op jit(solution)/shard_map/ppermute | solution.py:510
  124.5 1.3 collective-permute-start.28
  125.8 7.7 %collective-permute-done.24 = bf16[128,1792]{1,0:T(8,128)(2,1)S(1)} collective-permute-done((bf16[128,1792]{1,0:T(8,128)(2,1)S(1)}, bf16[128,1792]{1,0:T(8,128)(2,1)S(1)}, u32[]{:S(2)}, u32[]{:S(2)}) %collective-permute-start.24) | collective-permute-done | bytes 458784 | tf_op jit(solution)/shard_map/ppermute | solution.py:510
  133.5 1.4 maximum_select_fusion
  134.9 0.4 collective-permute-done.26
  135.3 3.3 %collective-permute-done.28 = bf16[4,16,576]{2,1,0:T(8,128)(2,1)S(1)} collective-permute-done((bf16[4,16,576]{2,1,0:T(8,128)(2,1)S(1)}, bf16[4,16,576]{2,1,0:T(8,128)(2,1)S(1)}, u32[]{:S(2)}, u32[]{:S(2)}) %collective-permute-start.28) | collective-permute-done | bytes 73760 | tf_op jit(solution)/shard_map/ppermute | solution.py:510
  138.5 1.1 add_convert_fusion.1
  139.7 1.4 collective-permute-start.30
  141.1 0.9 pad_maximum_fusion
  142.1 0.8 collective-permute-start.31
  142.9 5.4 %collective-permute-done.31 = bf16[4,2,16,576]{3,2,0,1:T(8,128)(2,1)S(1)} collective-permute-done((bf16[4,2,16,576]{3,2,0,1:T(8,128)(2,1)S(1)}, bf16[4,2,16,576]{3,2,0,1:T(8,128)(2,1)S(1)}, u32[]{:S(2)}, u32[]{:S(2)}) %collective-permute-start.31) | collective-permute-done | bytes 147488 | tf_op jit(solution)/shard_map/ppermute | solution.py:510
  148.4 0.7 pad_add_fusion.1.place_ref
  149.1 0.7 collective-permute-done.32
  149.8 0.8 pad_maximum_fusion.1
  150.6 2.5 %in_source_order.1 = bf16[256,576]{1,0:T(8,128)(2,1)} custom-call(s32[3]{0:T(128)} %pad_add_fusion.1.place_ref, bf16[256,576]{1,0:T(8,128)(2,1)} %bitcast.35), custom_call_target="tpu_custom_call" | custom-call | flops 1048576 | bytes 1048576 | tf_op jit(solution)/shard_map/in_source_order/pallas_call | solution.py:476
  153.1 1.8 copy.14
  154.9 27.1 %collective-permute-done.29 = bf16[128,3584]{1,0:T(8,128)(2,1)} collective-permute-done((bf16[128,3584]{1,0:T(8,128)(2,1)S(1)}, bf16[128,3584]{1,0:T(8,128)(2,1)}, u32[]{:S(2)}, u32[]{:S(2)}) %collective-permute-start.29) | collective-permute-done | bytes 917536 | tf_op jit(solution)/shard_map/ppermute | solution.py:510
  182.0 2.7 %add_convert_fusion = bf16[128,3584]{1,0:T(8,128)(2,1)} fusion(bf16[128,3584]{1,0:T(8,128)(2,1)} %collective-permute-done.30, bf16[128,3584]{1,0:T(8,128)(2,1)} %collective-permute-done.29, bf16[128,3584]{1,0:T(8,128)(2,1)S(1)} %get-tuple-element.101), kind=kLoop, calls=%fused_computation.1 | loop fusion | flops 2752512 | bytes 3670016 | tf_op jit(solution)/shard_map/convert_element_type | solution.py:525
  (85 shorter events, 0.8 us)
Async XLA Ops:
  0.6 13.8 %copy-start.24 = (s32[128,1]{0,1:T(1,128)S(1)}, s32[128,1]{0,1:T(1,128)}, u32[]{:S(2)}) copy-start(s32[128,1]{0,1:T(1,128)} %param.19) | copy-start | bytes 1540
  1.3 11.3 %collective-permute-start = (bf16[3584,256]{1,0:T(8,128)(2,1)}, bf16[3584,256]{1,0:T(8,128)(2,1)}, u32[]{:S(2)}, u32[]{:S(2)}) collective-permute-start(bf16[3584,256]{1,0:T(8,128)(2,1)} %refs_4_.1), channel_id=1, source_target_pairs={{0,1},{1,0},{2,3},{3,2},{4,5},{5,4},{6,7},{7,6},{8,9},{9,8},{10,11... | collective-permute-start | bytes 5505032 | tf_op jit(solution)/shard_map/ppermute | solution.py:510
  1.8 10.8 %collective-permute-start.1 = (bf16[3584,256]{1,0:T(8,128)(2,1)}, bf16[3584,256]{1,0:T(8,128)(2,1)}, u32[]{:S(2)}, u32[]{:S(2)}) collective-permute-start(bf16[3584,256]{1,0:T(8,128)(2,1)} %refs_10_.1), channel_id=1, source_target_pairs={{0,1},{1,0},{2,3},{3,2},{4,5},{5,4},{6,7},{7,6},{8,9},{9,8},{10,11... | collective-permute-start | bytes 5505032 | tf_op jit(solution)/shard_map/ppermute | solution.py:510
  1.8 6.3 %collective-permute-start.2 = (bf16[224,576]{1,0:T(8,128)(2,1)}, bf16[224,576]{1,0:T(8,128)(2,1)S(1)}, u32[]{:S(2)}, u32[]{:S(2)}) collective-permute-start(bf16[224,576]{1,0:T(8,128)(2,1)} %refs_1_.2), channel_id=1, source_target_pairs={{0,1},{1,0},{2,3},{3,2},{4,5},{5,4},{6,7},{7,6},{8,9},{9,8},{10,11... | collective-permute-start | bytes 774152 | tf_op jit(solution)/shard_map/ppermute | solution.py:510
  2.3 10.3 %collective-permute-start.3 = (bf16[224,576]{1,0:T(8,128)(2,1)}, bf16[224,576]{1,0:T(8,128)(2,1)}, u32[]{:S(2)}, u32[]{:S(2)}) collective-permute-start(bf16[224,576]{1,0:T(8,128)(2,1)} %refs_1_.2), channel_id=1, source_target_pairs={{0,2},{1,3},{2,0},{3,1},{4,6},{5,7},{6,4},{7,5},{8,10},{9,11},{10,... | collective-permute-start | bytes 774152 | tf_op jit(solution)/shard_map/ppermute | solution.py:510
  8.1 56.0 %copy-start.2 = (bf16[128,3712]{1,0:T(8,128)(2,1)}, bf16[128,3712]{1,0:T(8,128)(2,1)S(1)}, u32[]{:S(2)}) copy-start(bf16[128,3712]{1,0:T(8,128)(2,1)S(1)} %get-tuple-element.69.refs_0_) | copy-start | bytes 2850820
  12.6 23.1 %collective-permute-start.8 = (bf16[1024,896]{1,0:T(8,128)(2,1)}, bf16[1024,896]{1,0:T(8,128)(2,1)}, u32[]{:S(2)}, u32[]{:S(2)}) collective-permute-start(bf16[1024,896]{1,0:T(8,128)(2,1)} %refs_0_.2), channel_id=1, source_target_pairs={{0,1},{1,0},{2,3},{3,2},{4,5},{5,4},{6,7},{7,6},{8,9},{9,8},{10,11... | collective-permute-start | bytes 5505032 | tf_op jit(solution)/shard_map/ppermute | solution.py:510
  12.6 23.1 %collective-permute-start.7 = (bf16[1792,256]{1,0:T(8,128)(2,1)}, bf16[1792,256]{1,0:T(8,128)(2,1)}, u32[]{:S(2)}, u32[]{:S(2)}) collective-permute-start(bf16[1792,256]{1,0:T(8,128)(2,1)} %get-tuple-element.70), channel_id=1, source_target_pairs={{0,2},{1,3},{2,0},{3,1},{4,6},{5,7},{6,4},{7,5},{8,10},{9,11},{10,... | collective-permute-start | bytes 2752520 | tf_op jit(solution)/shard_map/ppermute | solution.py:510
  14.7 8.7 %collective-permute-start.9 = (bf16[224,576]{1,0:T(8,128)(2,1)}, bf16[224,576]{1,0:T(8,128)(2,1)}, u32[]{:S(2)}, u32[]{:S(2)}) collective-permute-start(bf16[224,576]{1,0:T(8,128)(2,1)} %collective-permute-done.3.refs_5_.refs_3_), channel_id=1, source_target_pairs={{0,1},{1,0},{2,3},{3,2},{4,5},{5,4},{6,7},{7,6},{8,9},{9,8},{10,11... | collective-permute-start | bytes 774152 | tf_op jit(solution)/shard_map/ppermute | solution.py:510
  15.1 49.0 %copy-start.4 = (bf16[224,576]{1,0:T(8,128)(2,1)S(1)}, bf16[224,576]{1,0:T(8,128)(2,1)}, u32[]{:S(2)}) copy-start(bf16[224,576]{1,0:T(8,128)(2,1)} %refs_1_.2) | copy-start | bytes 774148
  15.1 49.0 %copy-start.9 = (s32[3]{0:T(128)S(1)}, s32[3]{0:T(128)}, u32[]{:S(2)}) copy-start(s32[3]{0:T(128)} %pad_add_fusion.place_ref) | copy-start | bytes 40
  15.1 25.9 %collective-permute-start.5 = (bf16[128,3712]{1,0:T(8,128)(2,1)S(1)}, bf16[128,3712]{1,0:T(8,128)(2,1)}, u32[]{:S(2)}, u32[]{:S(2)}) collective-permute-start(bf16[128,3712]{1,0:T(8,128)(2,1)S(1)} %get-tuple-element.69.refs_0_), channel_id=1, source_target_pairs={{0,12},{1,13},{2,14},{3,15},{4,8},{5,9},{6,10},{7,11},{8,4},{9,5},... | collective-permute-start | bytes 2850824 | tf_op jit(solution)/shard_map/ppermute | solution.py:510
  21.9 0.9 copy-start.14
  22.8 40.8 %collective-permute-start.4 = (bf16[128,3712]{1,0:T(8,128)(2,1)S(1)}, bf16[128,3712]{1,0:T(8,128)(2,1)S(1)}, u32[]{:S(2)}, u32[]{:S(2)}) collective-permute-start(bf16[128,3712]{1,0:T(8,128)(2,1)S(1)} %get-tuple-element.69.refs_0_), channel_id=1, source_target_pairs={{0,4},{1,5},{2,6},{3,7},{4,0},{5,1},{6,2},{7,3},{8,12},{9,13},{10,... | collective-permute-start | bytes 2850824 | tf_op jit(solution)/shard_map/ppermute | solution.py:510
  35.7 49.7 %copy-start.10 = (s32[3]{0:T(128)S(1)}, s32[3]{0:T(128)}, u32[]{:S(2)}) copy-start(s32[3]{0:T(128)} %pad_add_fusion.place_ref) | copy-start | bytes 40
  35.7 24.8 %collective-permute-start.10 = (bf16[1792,256]{1,0:T(8,128)(2,1)}, bf16[1792,256]{1,0:T(8,128)(2,1)S(1)}, u32[]{:S(2)}, u32[]{:S(2)}) collective-permute-start(bf16[1792,256]{1,0:T(8,128)(2,1)} %collective-permute-done.7.refs_6_), channel_id=1, source_target_pairs={{0,16},{16,0},{1,17},{17,1},{2,18},{18,2},{3,19},{19,3},{4,20},{20... | collective-permute-start | bytes 2752520 | tf_op jit(solution)/shard_map/ppermute | solution.py:522
  37.5 23.1 %collective-permute-start.11 = (bf16[1792,256]{1,0:T(8,128)(2,1)}, bf16[1792,256]{1,0:T(8,128)(2,1)S(1)}, u32[]{:S(2)}, u32[]{:S(2)}) collective-permute-start(bf16[1792,256]{1,0:T(8,128)(2,1)} %get-tuple-element.75), channel_id=1, source_target_pairs={{0,2},{1,3},{2,0},{3,1},{4,6},{5,7},{6,4},{7,5},{8,10},{9,11},{10,... | collective-permute-start | bytes 2752520 | tf_op jit(solution)/shard_map/ppermute | solution.py:510
  38.9 21.6 %collective-permute-start.12 = (bf16[1792,256]{1,0:T(8,128)(2,1)}, bf16[1792,256]{1,0:T(8,128)(2,1)S(1)}, u32[]{:S(2)}, u32[]{:S(2)}) collective-permute-start(bf16[1792,256]{1,0:T(8,128)(2,1)} %collective-permute-done.7.refs_6_), channel_id=1, source_target_pairs={{0,1},{1,0},{2,3},{3,2},{4,5},{5,4},{6,7},{7,6},{8,9},{9,8},{10,11... | collective-permute-start | bytes 2752520 | tf_op jit(solution)/shard_map/ppermute | solution.py:510
  41.0 40.5 %collective-permute-start.6 = (bf16[128,3712]{1,0:T(8,128)(2,1)}, bf16[128,3712]{1,0:T(8,128)(2,1)S(1)}, u32[]{:S(2)}, u32[]{:S(2)}) collective-permute-start(bf16[128,3712]{1,0:T(8,128)(2,1)} %collective-permute-done.5.refs_2_.refs_3_), channel_id=1, source_target_pairs={{0,4},{1,5},{2,6},{3,7},{4,0},{5,1},{6,2},{7,3},{8,12},{9,13},{10,... | collective-permute-start | bytes 2850824 | tf_op jit(solution)/shard_map/ppermute | solution.py:510
  60.5 6.9 %copy-start.15 = (bf16[1792,256]{1,0:T(8,128)(2,1)}, bf16[1792,256]{1,0:T(8,128)(2,1)S(1)}, u32[]{:S(2)}) copy-start(bf16[1792,256]{1,0:T(8,128)(2,1)S(1)} %collective-permute-done.10.refs_7_) | copy-start | bytes 2752516
  60.5 6.9 %copy-start.16 = (bf16[1792,256]{1,0:T(8,128)(2,1)}, bf16[1792,256]{1,0:T(8,128)(2,1)S(1)}, u32[]{:S(2)}) copy-start(bf16[1792,256]{1,0:T(8,128)(2,1)S(1)} %collective-permute-done.11.refs_12_) | copy-start | bytes 2752516
  60.5 1.0 copy-start.17
  61.5 21.5 %collective-permute-start.13 = (bf16[1792,256]{1,0:T(8,128)(2,1)S(1)}, bf16[1792,256]{1,0:T(8,128)(2,1)S(1)}, u32[]{:S(2)}, u32[]{:S(2)}) collective-permute-start(bf16[1792,256]{1,0:T(8,128)(2,1)S(1)} %collective-permute-done.11.refs_12_), channel_id=1, source_target_pairs={{0,16},{16,0},{1,17},{17,1},{2,18},{18,2},{3,19},{19,3},{4,20},{20... | collective-permute-start | bytes 2752520 | tf_op jit(solution)/shard_map/ppermute | solution.py:522
  63.0 21.5 %collective-permute-start.14 = (bf16[512,896]{1,0:T(8,128)(2,1)}, bf16[512,896]{1,0:T(8,128)(2,1)S(1)}, u32[]{:S(2)}, u32[]{:S(2)}) collective-permute-start(bf16[512,896]{1,0:T(8,128)(2,1)} %copy-done.14), channel_id=1, source_target_pairs={{0,2},{1,3},{2,0},{3,1},{4,6},{5,7},{6,4},{7,5},{8,10},{9,11},{10,... | collective-permute-start | bytes 2752520 | tf_op jit(solution)/shard_map/ppermute | solution.py:510
  63.6 20.9 %collective-permute-start.15 = (bf16[1792,256]{1,0:T(8,128)(2,1)S(1)}, bf16[1792,256]{1,0:T(8,128)(2,1)S(1)}, u32[]{:S(2)}, u32[]{:S(2)}) collective-permute-start(bf16[1792,256]{1,0:T(8,128)(2,1)S(1)} %collective-permute-done.10.refs_7_), channel_id=1, source_target_pairs={{0,1},{1,0},{2,3},{3,2},{4,5},{5,4},{6,7},{7,6},{8,9},{9,8},{10,11... | collective-permute-start | bytes 2752520 | tf_op jit(solution)/shard_map/ppermute | solution.py:510
  63.6 3.8 %copy-start.3 = (bf16[128,3712]{1,0:T(8,128)(2,1)}, bf16[128,3712]{1,0:T(8,128)(2,1)S(1)}, u32[]{:S(2)}) copy-start(bf16[128,3712]{1,0:T(8,128)(2,1)S(1)} %collective-permute-done.4.refs_1_) | copy-start | bytes 2850820
  63.6 20.9 %collective-permute-start.16 = (bf16[1792,256]{1,0:T(8,128)(2,1)S(1)}, bf16[1792,256]{1,0:T(8,128)(2,1)S(1)}, u32[]{:S(2)}, u32[]{:S(2)}) collective-permute-start(bf16[1792,256]{1,0:T(8,128)(2,1)S(1)} %collective-permute-done.11.refs_12_), channel_id=1, source_target_pairs={{0,1},{1,0},{2,3},{3,2},{4,5},{5,4},{6,7},{7,6},{8,9},{9,8},{10,11... | collective-permute-start | bytes 2752520 | tf_op jit(solution)/shard_map/ppermute | solution.py:510
  67.4 21.5 %copy-start.7 = (bf16[128,576]{1,0:T(8,128)(2,1)}, bf16[128,576]{1,0:T(8,128)(2,1)S(1)}, u32[]{:S(2)}) copy-start(bf16[128,576]{1,0:T(8,128)(2,1)S(1)} %get-tuple-element.106) | copy-start | bytes 442372
  81.5 11.4 %copy-start.1 = (bf16[128,3712]{1,0:T(8,128)(2,1)}, bf16[128,3712]{1,0:T(8,128)(2,1)S(1)}, u32[]{:S(2)}) copy-start(bf16[128,3712]{1,0:T(8,128)(2,1)S(1)} %collective-permute-done.6.refs_2_.refs_0_) | copy-start | bytes 2850820
  83.0 7.6 %copy-start.18 = (bf16[1792,256]{1,0:T(8,128)(2,1)}, bf16[1792,256]{1,0:T(8,128)(2,1)S(1)}, u32[]{:S(2)}) copy-start(bf16[1792,256]{1,0:T(8,128)(2,1)S(1)} %collective-permute-done.13.refs_13_) | copy-start | bytes 2752516
  84.5 6.1 %copy-start.19 = (bf16[1792,256]{1,0:T(8,128)(2,1)}, bf16[1792,256]{1,0:T(8,128)(2,1)S(1)}, u32[]{:S(2)}) copy-start(bf16[1792,256]{1,0:T(8,128)(2,1)S(1)} %collective-permute-done.15.refs_9_) | copy-start | bytes 2752516
  84.5 6.1 %copy-start.20 = (bf16[1792,256]{1,0:T(8,128)(2,1)}, bf16[1792,256]{1,0:T(8,128)(2,1)S(1)}, u32[]{:S(2)}) copy-start(bf16[1792,256]{1,0:T(8,128)(2,1)S(1)} %collective-permute-done.16.refs_14_) | copy-start | bytes 2752516
  84.5 6.1 %collective-permute-start.17 = (bf16[1792,256]{1,0:T(8,128)(2,1)S(1)}, bf16[1792,256]{1,0:T(8,128)(2,1)S(1)}, u32[]{:S(2)}, u32[]{:S(2)}) collective-permute-start(bf16[1792,256]{1,0:T(8,128)(2,1)S(1)} %collective-permute-done.13.refs_13_), channel_id=1, source_target_pairs={{0,1},{1,0},{2,3},{3,2},{4,5},{5,4},{6,7},{7,6},{8,9},{9,8},{10,11... | collective-permute-start | bytes 2752520 | tf_op jit(solution)/shard_map/ppermute | solution.py:510
  84.6 23.1 %collective-permute-start.21 = (bf16[512,896]{1,0:T(8,128)(2,1)S(1)}, bf16[512,896]{1,0:T(8,128)(2,1)S(1)}, u32[]{:S(2)}, u32[]{:S(2)}) collective-permute-start(bf16[512,896]{1,0:T(8,128)(2,1)S(1)} %collective-permute-done.14.refs_2_), channel_id=1, source_target_pairs={{0,16},{16,0},{1,17},{17,1},{2,18},{18,2},{3,19},{19,3},{4,20},{20... | collective-permute-start | bytes 2752520 | tf_op jit(solution)/shard_map/ppermute | solution.py:522
  85.2 22.5 %collective-permute-start.22 = (bf16[512,896]{1,0:T(8,128)(2,1)S(1)}, bf16[512,896]{1,0:T(8,128)(2,1)}, u32[]{:S(2)}, u32[]{:S(2)}) collective-permute-start(bf16[512,896]{1,0:T(8,128)(2,1)S(1)} %collective-permute-done.14.refs_2_), channel_id=1, source_target_pairs={{0,1},{1,0},{2,3},{3,2},{4,5},{5,4},{6,7},{7,6},{8,9},{9,8},{10,11... | collective-permute-start | bytes 2752520 | tf_op jit(solution)/shard_map/ppermute | solution.py:510
  87.5 20.1 %collective-permute-start.19 = (bf16[128,576]{1,0:T(8,128)(2,1)S(1)}, bf16[128,576]{1,0:T(8,128)(2,1)S(1)}, u32[]{:S(2)}, u32[]{:S(2)}) collective-permute-start(bf16[128,576]{1,0:T(8,128)(2,1)S(1)} %latent_parts.3), channel_id=1, source_target_pairs={{0,8},{1,9},{2,10},{3,11},{4,12},{5,13},{6,14},{7,15},{8,0},{9,1},... | collective-permute-start | bytes 442376 | tf_op jit(solution)/shard_map/ppermute | solution.py:510
  88.9 18.7 %collective-permute-start.18 = (bf16[128,576]{1,0:T(8,128)(2,1)}, bf16[128,576]{1,0:T(8,128)(2,1)S(1)}, u32[]{:S(2)}, u32[]{:S(2)}) collective-permute-start(bf16[128,576]{1,0:T(8,128)(2,1)} %get-tuple-element.94), channel_id=1, source_target_pairs={{0,4},{1,5},{2,6},{3,7},{4,0},{5,1},{6,2},{7,3},{8,12},{9,13},{10,... | collective-permute-start | bytes 442376 | tf_op jit(solution)/shard_map/ppermute | solution.py:510
  90.6 0.9 copy-start.21
  91.5 16.1 %collective-permute-start.20 = (bf16[128,576]{1,0:T(8,128)(2,1)}, bf16[128,576]{1,0:T(8,128)(2,1)}, u32[]{:S(2)}, u32[]{:S(2)}) collective-permute-start(bf16[128,576]{1,0:T(8,128)(2,1)} %get-tuple-element.95), channel_id=1, source_target_pairs={{0,12},{1,13},{2,14},{3,15},{4,8},{5,9},{6,10},{7,11},{8,4},{9,5},... | collective-permute-start | bytes 442376 | tf_op jit(solution)/shard_map/ppermute | solution.py:510
  92.9 0.7 copy-start.11
  93.6 14.2 %copy-start.25 = (s32[128]{0:T(128)S(1)}, s32[128]{0:T(128)}, u32[]{:S(2)}) copy-start(s32[128]{0:T(128)} %multiply_add_fusion) | copy-start | bytes 1540
  93.6 14.3 %copy-start.8 = (bf16[128,576]{1,0:T(8,128)(2,1)S(1)}, bf16[128,576]{1,0:T(8,128)(2,1)}, u32[]{:S(2)}) copy-start(bf16[128,576]{1,0:T(8,128)(2,1)} %copy-done.7) | copy-start | bytes 442372
  93.6 16.6 %copy-start = (bf16[1024,896]{1,0:T(8,128)(2,1)S(1)}, bf16[1024,896]{1,0:T(8,128)(2,1)}, u32[]{:S(2)}) copy-start(bf16[1024,896]{1,0:T(8,128)(2,1)} %refs_0_.2) | copy-start | bytes 5505028
  107.7 2.5 %collective-permute-start.23 = (bf16[512,896]{1,0:T(8,128)(2,1)S(1)}, bf16[512,896]{1,0:T(8,128)(2,1)S(1)}, u32[]{:S(2)}, u32[]{:S(2)}) collective-permute-start(bf16[512,896]{1,0:T(8,128)(2,1)S(1)} %collective-permute-done.21.refs_3_), channel_id=1, source_target_pairs={{0,1},{1,0},{2,3},{3,2},{4,5},{5,4},{6,7},{7,6},{8,9},{9,8},{10,11... | collective-permute-start | bytes 2752520 | tf_op jit(solution)/shard_map/ppermute | solution.py:510
  107.8 18.0 %collective-permute-start.25 = (bf16[128,1792]{1,0:T(8,128)(2,1)}, bf16[128,1792]{1,0:T(8,128)(2,1)}, u32[]{:S(2)}, u32[]{:S(2)}) collective-permute-start(bf16[128,1792]{1,0:T(8,128)(2,1)} %get-tuple-element.104), channel_id=1, source_target_pairs={{0,4},{1,5},{2,6},{3,7},{4,0},{5,1},{6,2},{7,3},{8,12},{9,13},{10,... | collective-permute-start | bytes 1376264 | tf_op jit(solution)/shard_map/ppermute | solution.py:510
  110.2 9.7 %copy-start.23 = (f32[512]{0:T(512)S(1)}, f32[512]{0:T(512)}, u32[]{:S(2)}) copy-start(f32[512]{0:T(512)} %param.13) | copy-start | bytes 6148
  116.9 0.9 copy-start.5
  117.8 1.0 copy-start.12
  118.8 19.8 %copy-start.6 = (bf16[128,3584]{1,0:T(8,128)(2,1)S(1)}, bf16[128,3584]{1,0:T(8,128)(2,1)}, u32[]{:S(2)}) copy-start(bf16[128,3584]{1,0:T(8,128)(2,1)} %copy-done.5) | copy-start | bytes 2752516
  118.8 14.7 %collective-permute-start.24 = (bf16[128,1792]{1,0:T(8,128)(2,1)S(1)}, bf16[128,1792]{1,0:T(8,128)(2,1)S(1)}, u32[]{:S(2)}, u32[]{:S(2)}) collective-permute-start(bf16[128,1792]{1,0:T(8,128)(2,1)S(1)} %get-tuple-element.103), channel_id=1, source_target_pairs={{0,4},{1,5},{2,6},{3,7},{4,0},{5,1},{6,2},{7,3},{8,12},{9,13},{10,... | collective-permute-start | bytes 1376264 | tf_op jit(solution)/shard_map/ppermute | solution.py:510
  121.4 13.9 %collective-permute-start.26 = (bf16[4,16,576]{2,1,0:T(8,128)(2,1)S(1)}, bf16[4,16,576]{2,1,0:T(8,128)(2,1)S(1)}, u32[]{:S(2)}, u32[]{:S(2)}) collective-permute-start(bf16[4,16,576]{2,1,0:T(8,128)(2,1)S(1)} %get-tuple-element.130), channel_id=1, source_target_pairs={{0,4},{1,5},{2,6},{3,7},{4,0},{5,1},{6,2},{7,3},{8,12},{9,13},{10,... | collective-permute-start | bytes 221192 | tf_op jit(solution)/shard_map/ppermute | solution.py:510
  122.3 12.9 %collective-permute-start.27 = (bf16[4,16,576]{2,1,0:T(8,128)(2,1)S(1)}, bf16[4,16,576]{2,1,0:T(8,128)(2,1)S(1)}, u32[]{:S(2)}, u32[]{:S(2)}) collective-permute-start(bf16[4,16,576]{2,1,0:T(8,128)(2,1)S(1)} %get-tuple-element.129), channel_id=1, source_target_pairs={{0,8},{1,9},{2,10},{3,11},{4,12},{5,13},{6,14},{7,15},{8,0},{9,1},... | collective-permute-start | bytes 221192 | tf_op jit(solution)/shard_map/ppermute | solution.py:510
  124.5 14.1 %collective-permute-start.28 = (bf16[4,16,576]{2,1,0:T(8,128)(2,1)S(1)}, bf16[4,16,576]{2,1,0:T(8,128)(2,1)S(1)}, u32[]{:S(2)}, u32[]{:S(2)}) collective-permute-start(bf16[4,16,576]{2,1,0:T(8,128)(2,1)S(1)} %get-tuple-element.128), channel_id=1, source_target_pairs={{0,12},{1,13},{2,14},{3,15},{4,8},{5,9},{6,10},{7,11},{8,4},{9,5},... | collective-permute-start | bytes 221192 | tf_op jit(solution)/shard_map/ppermute | solution.py:510
  134.9 4.8 %copy-start.13 = (bf16[128,3584]{1,0:T(8,128)(2,1)S(1)}, bf16[128,3584]{1,0:T(8,128)(2,1)}, u32[]{:S(2)}) copy-start(bf16[128,3584]{1,0:T(8,128)(2,1)} %copy-done.12) | copy-start | bytes 2752516
  138.5 1.1 copy-start.22
  139.7 42.3 %collective-permute-start.29 = (bf16[128,3584]{1,0:T(8,128)(2,1)S(1)}, bf16[128,3584]{1,0:T(8,128)(2,1)}, u32[]{:S(2)}, u32[]{:S(2)}) collective-permute-start(bf16[128,3584]{1,0:T(8,128)(2,1)S(1)} %copy-done.13), channel_id=1, source_target_pairs={{0,4},{1,5},{2,6},{3,7},{4,0},{5,1},{6,2},{7,3},{8,12},{9,13},{10,... | collective-permute-start | bytes 2752520 | tf_op jit(solution)/shard_map/ppermute | solution.py:510
  139.7 42.3 %collective-permute-start.30 = (bf16[128,3584]{1,0:T(8,128)(2,1)}, bf16[128,3584]{1,0:T(8,128)(2,1)}, u32[]{:S(2)}, u32[]{:S(2)}) collective-permute-start(bf16[128,3584]{1,0:T(8,128)(2,1)} %add_convert_fusion.1), channel_id=1, source_target_pairs={{0,12},{1,13},{2,14},{3,15},{4,8},{5,9},{6,10},{7,11},{8,4},{9,5},... | collective-permute-start | bytes 2752520 | tf_op jit(solution)/shard_map/ppermute | solution.py:510
  142.1 6.2 %collective-permute-start.31 = (bf16[4,2,16,576]{3,2,0,1:T(8,128)(2,1)S(1)}, bf16[4,2,16,576]{3,2,0,1:T(8,128)(2,1)S(1)}, u32[]{:S(2)}, u32[]{:S(2)}) collective-permute-start(bf16[4,2,16,576]{3,2,0,1:T(8,128)(2,1)S(1)} %get-tuple-element.126), channel_id=1, source_target_pairs={{0,2},{1,3},{2,0},{3,1},{4,6},{5,7},{6,4},{7,5},{8,10},{9,11},{10,... | collective-permute-start | bytes 442376 | tf_op jit(solution)/shard_map/ppermute | solution.py:510
  148.4 1.5 collective-permute-start.32

commit v5 on v4

--- a/solution.py
+++ b/solution.py
@@ -482,6 +482,7 @@
         ],
         out_specs=pl.BlockSpec(memory_space=pltpu.VMEM),
         scratch_shapes=[pltpu.SemaphoreType.DMA((blocks.shape[0] // rows,))],
+        compiler_params=pltpu.CompilerParams(vmem_limit_bytes=4 * MIB),
         cost_estimate=BRIEF,
         name="in_source_order",
     )(place, blocks)
@@ -535,8 +536,8 @@
     rows, gate_half = entry(
         place_info, tokens, norm_gain, expert_index, route_gate, gate_weight
     )
-    rows, gate_half, gate_core, up_core, kv_core, kv_x, up_own, down_own = hold(
-        (rows, gate_half, gate_core, up_core, kv_core, kv_x, up_weight, down_weight)
+    rows, gate_core, up_core, kv_core, kv_x, up_own, down_own = hold(
+        (rows, gate_core, up_core, kv_core, kv_x, up_weight, down_weight)
     )
 
     f = across_line(rows, 3)
@@ -577,10 +578,9 @@
         (up_weight, up_core, up_x, up_y, up_x_core, up_y_core),
         (down_weight, down_core),
     )
-    hidden, near2, latents, down_y, down_x_core = hold(
-        (hidden, near2, latents, down_y, down_x_core)
-    )
+    hidden, near2, latents, down_x_core = hold((hidden, near2, latents, down_x_core))
     near2_there = across_line(near2, 1)
+    hidden, down_y = hold((hidden, down_y))
     down_y_core = other_core(down_y)
     part0, part1, part3, far2 = rest_products(
         place_info,
@@ -606,9 +606,8 @@
         jnp.concatenate([far2_there, near2_there], axis=1),
         jnp.concatenate([near2_there, far2_there], axis=1),
     )
-    part2_there, there = hold((part2_there, there))
     part_sum = narrow(wide(part3) + wide(part2_there))
-    part_sum, part1 = hold((part_sum, part1))
+    part_sum, part1, there = hold((part_sum, part1, there))
     there3, there1 = across_line(part_sum, 3), across_line(part1, 1)
 
     chip, core = place >> 1, place & 1

time: 185 us -> 184 us (level)
  waiting for transfers between devices: 81.4 us -> 84.4 us
    ppermute x30, waiting for transfers between devices: 79.8 us -> 82.8 us  [exchange(): lax.ppermute(value, 'dev', [(i, i ^ distance) for i in range(device_count)])]
    unnamed x53 -> x51, local copies, waits for them, and re-layouts: 7.26 us -> 6.34 us
  transfers between devices with their start and end apart: 33 -> 33, of which waited for: 13 -> 12; matrix products, arithmetic and copies ran while one was open for 5% -> 5% of each run, Pallas kernels for 19% -> 18%
where the time goes in v5:
time: 184 us
  waiting for transfers between devices  84.4 us (46%)
  starting transfers between devices  47.4 us (26%)
  Pallas kernels  33.8 us (18%)
  other arithmetic  10.5 us (6%)
  local copies, waits for them, and re-layouts  6.42 us (3%)
    ppermute x30, waiting for transfers between devices, exchange(): lax.ppermute(value, 'dev', [(i, i ^ distance) for i in range(device_count)])  82.8 us
    ppermute x30, starting transfers between devices, exchange(): lax.ppermute(value, 'dev', [(i, i ^ distance) for i in range(device_count)])  43.6 us
    pallas_call x1, Pallas kernels, hidden_units(): pl.pallas_call(hidden_kernel, out_shape=[pltpu.VMEM((LINE * tok_rows, GRO...  14 us
    pallas_call x1, Pallas kernels, rest_products(): pl.pallas_call(rest_kernel, out_shape=[pltpu.VMEM((tok_rows, GROUP * widt...  6.67 us
    unnamed x51, local copies, waits for them, and re-layouts  6.34 us
    pallas_call x2, Pallas kernels, latent_parts(): pl.pallas_call(functools.partial(latent_kernel, len(rows)), out_shape=[pl...  5.46 us
    convert_element_type x2, other arithmetic, narrow(): return value.astype(jnp.bfloat16)  4.84 us
    ppermute x3, starting transfers between devices, other_rep(): return lax.ppermute(value, 'rep', [(0, 1), (1, 0)])  3.86 us
  transfers between devices with their start and end apart: 33, of which 12 were waited for; matrix products, arithmetic and copies ran while one was open for 5% of the time, Pallas kernels for 18%

profile of v5, /device:TPU:0, one launch (start us, length us, event | category | flops | bytes accessed | tf_op | source)
XLA Modules:
  0.0 183.6 jit_solution(13870863645645130043)
XLA Ops:
  0.7 0.7 pad_add_fusion.place_ref
  1.3 0.5 collective-permute-start
  1.8 0.5 collective-permute-start.2
  2.3 2.5 %collective-permute-start.3 = (bf16[224,576]{1,0:T(8,128)(2,1)}, bf16[224,576]{1,0:T(8,128)(2,1)}, u32[]{:S(2)}, u32[]{:S(2)}) collective-permute-start(bf16[224,576]{1,0:T(8,128)(2,1)} %refs_1_.2), channel_id=1, source_target_pairs={{0,2},{1,3},{2,0},{3,1},{4,6},{5,7},{6,4},{7,5},{8,10},{9,11},{10,... | collective-permute-start | bytes 774152 | tf_op jit(solution)/shard_map/ppermute | solution.py:511
  4.8 3.3 %entry.1 = (bf16[128,3712]{1,0:T(8,128)(2,1)S(1)}, bf16[1792,256]{1,0:T(8,128)(2,1)}) custom-call(s32[3]{0:T(128)} %pad_add_fusion.place_ref, bf16[128,3584]{1,0:T(8,128)(2,1)} %tokens_ref.1, f32[28,128]{1,0:T(8,128)} %bitcast.41, s32[2,128]{1,0:T(2,128)} %bitcast.44, f32[2,128]{1,0:T(2,128)} %bitcast.45, bf16[3584,256]{1,0:T(8,128)(2,1)} %refs_4_.1), custom_call_target="tpu_custom_call" | custom-call | flops 1048576 | bytes 1048576 | tf_op jit(solution)/shard_map/entry/pallas_call | solution.py:195
  8.1 4.5 %collective-permute-done.3.refs_5_.refs_3_ = bf16[224,576]{1,0:T(8,128)(2,1)} collective-permute-done((bf16[224,576]{1,0:T(8,128)(2,1)}, bf16[224,576]{1,0:T(8,128)(2,1)}, u32[]{:S(2)}, u32[]{:S(2)}) %collective-permute-start.3) | collective-permute-done | bytes 258080 | tf_op jit(solution)/shard_map/ppermute | solution.py:511
  12.6 1.8 collective-permute-start.7
  14.4 0.1 fusion.19
  14.5 0.2 reduce_window_sum.11
  14.7 0.2 collective-permute-start.9
  14.9 0.2 select_reduce_fusion
  15.1 3.7 %collective-permute-start.5 = (bf16[128,3712]{1,0:T(8,128)(2,1)S(1)}, bf16[128,3712]{1,0:T(8,128)(2,1)}, u32[]{:S(2)}, u32[]{:S(2)}) collective-permute-start(bf16[128,3712]{1,0:T(8,128)(2,1)S(1)} %get-tuple-element.67.refs_0_), channel_id=1, source_target_pairs={{0,12},{1,13},{2,14},{3,15},{4,8},{5,9},{6,10},{7,11},{8,4},{9,5},... | collective-permute-start | bytes 2850824 | tf_op jit(solution)/shard_map/ppermute | solution.py:511
  18.8 3.1 %weight_halves.1 = (bf16[1792,256]{1,0:T(8,128)(2,1)}, bf16[512,896]{1,0:T(8,128)(2,1)S(1)}) custom-call(s32[3]{0:T(128)} %pad_add_fusion.place_ref, bf16[3584,256]{1,0:T(8,128)(2,1)} %refs_10_.1, bf16[1024,896]{1,0:T(8,128)(2,1)} %refs_0_.2), custom_call_target="tpu_custom_call" | custom-call | flops 1048576 | bytes 1048576 | tf_op jit(solution)/shard_map/weight_halves/pallas_call | solution.py:228
  21.9 0.9 copy-done.14
  22.8 0.5 multiply_add_fusion
  23.3 12.3 %collective-permute-done.7.refs_6_ = bf16[1792,256]{1,0:T(8,128)(2,1)} collective-permute-done((bf16[1792,256]{1,0:T(8,128)(2,1)}, bf16[1792,256]{1,0:T(8,128)(2,1)}, u32[]{:S(2)}, u32[]{:S(2)}) %collective-permute-start.7) | collective-permute-done | bytes 917536 | tf_op jit(solution)/shard_map/ppermute | solution.py:511
  35.7 1.8 %collective-permute-start.10 = (bf16[1792,256]{1,0:T(8,128)(2,1)}, bf16[1792,256]{1,0:T(8,128)(2,1)S(1)}, u32[]{:S(2)}, u32[]{:S(2)}) collective-permute-start(bf16[1792,256]{1,0:T(8,128)(2,1)} %collective-permute-done.7.refs_6_), channel_id=1, source_target_pairs={{0,16},{16,0},{1,17},{17,1},{2,18},{18,2},{3,19},{19,3},{4,20},{20... | collective-permute-start | bytes 2752520 | tf_op jit(solution)/shard_map/ppermute | solution.py:523
  37.5 1.5 collective-permute-start.11
  39.0 2.0 %collective-permute-done.5.refs_2_.refs_3_ = bf16[128,3712]{1,0:T(8,128)(2,1)} collective-permute-done((bf16[128,3712]{1,0:T(8,128)(2,1)S(1)}, bf16[128,3712]{1,0:T(8,128)(2,1)}, u32[]{:S(2)}, u32[]{:S(2)}) %collective-permute-start.5) | collective-permute-done | bytes 950304 | tf_op jit(solution)/shard_map/ppermute | solution.py:511
  41.0 19.5 %collective-permute-start.6 = (bf16[128,3712]{1,0:T(8,128)(2,1)}, bf16[128,3712]{1,0:T(8,128)(2,1)S(1)}, u32[]{:S(2)}, u32[]{:S(2)}) collective-permute-start(bf16[128,3712]{1,0:T(8,128)(2,1)} %collective-permute-done.5.refs_2_.refs_3_), channel_id=1, source_target_pairs={{0,4},{1,5},{2,6},{3,7},{4,0},{5,1},{6,2},{7,3},{8,12},{9,13},{10,... | collective-permute-start | bytes 2850824 | tf_op jit(solution)/shard_map/ppermute | solution.py:511
  60.6 1.0 copy-done.17
  61.5 1.5 collective-permute-start.13
  63.0 0.5 collective-permute-start.14
  63.6 0.5 collective-permute-start.16
  64.1 3.3 %latent_parts.2 = (bf16[128,576]{1,0:T(8,128)(2,1)S(1)}, bf16[128,576]{1,0:T(8,128)(2,1)}, bf16[128,576]{1,0:T(8,128)(2,1)}) custom-call(s32[3]{0:T(128)S(1)} %copy-done.9, bf16[128,3712]{1,0:T(8,128)(2,1)S(1)} %get-tuple-element.67.refs_0_, bf16[128,3712]{1,0:T(8,128)(2,1)S(1)} %collective-permute-done.4.refs_1_, ...), custom_call_target="tpu_custom_call" | custom-call | flops 1048576 | bytes 1048576 | tf_op jit(solution)/shard_map/latent_parts/pallas_call | solution.py:293
  67.5 14.0 %collective-permute-done.6.refs_2_.refs_0_ = bf16[128,3712]{1,0:T(8,128)(2,1)S(1)} collective-permute-done((bf16[128,3712]{1,0:T(8,128)(2,1)}, bf16[128,3712]{1,0:T(8,128)(2,1)S(1)}, u32[]{:S(2)}, u32[]{:S(2)}) %collective-permute-start.6) | collective-permute-done | bytes 950304 | tf_op jit(solution)/shard_map/ppermute | solution.py:511
  81.5 1.6 collective-permute-done.13.refs_13_
  83.1 1.4 collective-permute-done.14.refs_2_
  84.6 0.5 collective-permute-start.21
  85.1 0.5 collective-permute-start.22
  85.6 2.1 %latent_parts.3 = bf16[128,576]{1,0:T(8,128)(2,1)S(1)} custom-call(s32[3]{0:T(128)S(1)} %copy-done.10, bf16[128,3712]{1,0:T(8,128)(2,1)S(1)} %collective-permute-done.6.refs_2_.refs_0_, bf16[224,576]{1,0:T(8,128)(2,1)S(1)} %copy-done.4, bf16[224,576]{1,0:T(8,128)(2,1)S(1)} %collective-permute-done.2.refs_4_.refs_2_, ...), custom_call_target="tpu_custom_call" | custom-call | flops 1048576 | bytes 1048576 | tf_op jit(solution)/shard_map/latent_parts/pallas_call | solution.py:293
  87.8 1.4 collective-permute-start.19
  89.2 1.7 collective-permute-start.18
  90.9 0.9 copy-done.21
  91.8 1.3 collective-permute-start.20
  93.2 0.7 copy-done.11
  93.9 14.0 %hidden_units.1 = (bf16[512,1024]{1,0:T(8,128)(2,1)S(1)}, f32[512,1]{1,0:T(8,128)S(1)}, bf16[128,1792]{1,0:T(8,128)(2,1)}) custom-call(s32[3]{0:T(128)S(1)} %copy-done.11, bf16[128,3712]{1,0:T(8,128)(2,1)} %copy-done.2, bf16[128,3712]{1,0:T(8,128)(2,1)} %copy-done.3, bf16[128,3712]{1,0:T(8,128)(2,1)} %copy-done.1, ...), custom_call_target="tpu_custom_call" | custom-call | flops 1048576 | bytes 1048576 | tf_op jit(solution)/shard_map/hidden_units/pallas_call | solution.py:383
  108.1 0.1 collective-permute-start.25
  108.2 1.0 add_add_fusion
  109.2 0.1 multiply_reduce_fusion
  109.3 0.3 fusion.16
  109.6 1.1 collective-permute-done.23.refs_5_
  110.7 6.7 %rest_products.1 = (bf16[128,3584]{1,0:T(8,128)(2,1)S(1)}, bf16[128,3584]{1,0:T(8,128)(2,1)S(1)}, bf16[128,3584]{1,0:T(8,128)(2,1)S(1)}, bf16[128,1792]{1,0:T(8,128)(2,1)S(1)}) custom-call(s32[3]{0:T(128)S(1)} %copy-done.11, bf16[512,1024]{1,0:T(8,128)(2,1)S(1)} %get-tuple-element.96.hidden_ref, f32[512,1]{1,0:T(8,128)S(1)} %get-tuple-element.97.scale_ref, ...), custom_call_target="tpu_custom_call" | custom-call | flops 1048576 | bytes 1048576 | tf_op jit(solution)/shard_map/rest_products/pallas_call | solution.py:436
  117.4 1.0 copy-done.5
  118.4 0.9 copy-done.12
  119.3 0.9 collective-permute-start.24
  120.2 0.1 multiply_convert_fusion
  120.3 1.3 scatter_custom_fusion
  121.7 1.2 collective-permute-start.26
  122.8 1.9 %collective-permute-start.27 = (bf16[4,16,576]{2,1,0:T(8,128)(2,1)S(1)}, bf16[4,16,576]{2,1,0:T(8,128)(2,1)S(1)}, u32[]{:S(2)}, u32[]{:S(2)}) collective-permute-start(bf16[4,16,576]{2,1,0:T(8,128)(2,1)S(1)} %get-tuple-element.127), channel_id=1, source_target_pairs={{0,8},{1,9},{2,10},{3,11},{4,12},{5,13},{6,14},{7,15},{8,0},{9,1},... | collective-permute-start | bytes 221192 | tf_op jit(solution)/shard_map/ppermute | solution.py:511
  124.8 1.3 collective-permute-start.28
  126.1 7.9 %collective-permute-done.24 = bf16[128,1792]{1,0:T(8,128)(2,1)S(1)} collective-permute-done((bf16[128,1792]{1,0:T(8,128)(2,1)S(1)}, bf16[128,1792]{1,0:T(8,128)(2,1)S(1)}, u32[]{:S(2)}, u32[]{:S(2)}) %collective-permute-start.24) | collective-permute-done | bytes 458784 | tf_op jit(solution)/shard_map/ppermute | solution.py:511
  134.0 2.4 %add_convert_fusion.1 = bf16[128,3584]{1,0:T(8,128)(2,1)} fusion(bf16[128,3584]{1,0:T(8,128)(2,1)S(1)} %get-tuple-element.101, bf16[128,1792]{1,0:T(8,128)(2,1)} %collective-permute-done.25, bf16[128,1792]{1,0:T(8,128)(2,1)S(1)} %collective-permute-done.24, pred[]{:T(512)S(6)} %eq.33), kind=kLoop, calls=%fused_computation.2 | loop fusion | flops 5963776 | bytes 2752513 | tf_op jit(solution)/shard_map/convert_element_type | solution.py:526
  136.4 2.5 %collective-permute-done.28 = bf16[4,16,576]{2,1,0:T(8,128)(2,1)} collective-permute-done((bf16[4,16,576]{2,1,0:T(8,128)(2,1)S(1)}, bf16[4,16,576]{2,1,0:T(8,128)(2,1)}, u32[]{:S(2)}, u32[]{:S(2)}) %collective-permute-start.28) | collective-permute-done | bytes 73760 | tf_op jit(solution)/shard_map/ppermute | solution.py:511
  138.9 1.3 collective-permute-start.30
  140.3 1.0 pad_maximum_fusion
  141.4 0.4 collective-permute-start.31
  141.8 5.8 %collective-permute-done.31 = bf16[4,2,16,576]{3,2,0,1:T(8,128)(2,1)S(1)} collective-permute-done((bf16[4,2,16,576]{3,2,0,1:T(8,128)(2,1)S(1)}, bf16[4,2,16,576]{3,2,0,1:T(8,128)(2,1)S(1)}, u32[]{:S(2)}, u32[]{:S(2)}) %collective-permute-start.31) | collective-permute-done | bytes 147488 | tf_op jit(solution)/shard_map/ppermute | solution.py:511
  147.7 0.1 pad_add_fusion.1.place_ref
  147.8 1.3 collective-permute-done.32
  149.2 1.2 in_source_order.1
  150.3 0.9 copy.14
  151.2 30.0 %collective-permute-done.29 = bf16[128,3584]{1,0:T(8,128)(2,1)S(1)} collective-permute-done((bf16[128,3584]{1,0:T(8,128)(2,1)S(1)}, bf16[128,3584]{1,0:T(8,128)(2,1)S(1)}, u32[]{:S(2)}, u32[]{:S(2)}) %collective-permute-start.29) | collective-permute-done | bytes 917536 | tf_op jit(solution)/shard_map/ppermute | solution.py:511
  181.2 2.4 %add_convert_fusion = bf16[128,3584]{1,0:T(8,128)(2,1)} fusion(bf16[128,3584]{1,0:T(8,128)(2,1)} %collective-permute-done.30, bf16[128,3584]{1,0:T(8,128)(2,1)S(1)} %collective-permute-done.29, bf16[128,3584]{1,0:T(8,128)(2,1)S(1)} %copy-done.6), kind=kLoop, calls=%fused_computation.1 | loop fusion | flops 2752512 | bytes 3670016 | tf_op jit(solution)/shard_map/convert_element_type | solution.py:526
  (82 shorter events, 0.6 us)
Async XLA Ops:
  0.6 13.8 %copy-start.23 = (s32[128,1]{0,1:T(1,128)S(1)}, s32[128,1]{0,1:T(1,128)}, u32[]{:S(2)}) copy-start(s32[128,1]{0,1:T(1,128)} %param.19) | copy-start | bytes 1540
  1.3 11.3 %collective-permute-start = (bf16[3584,256]{1,0:T(8,128)(2,1)}, bf16[3584,256]{1,0:T(8,128)(2,1)}, u32[]{:S(2)}, u32[]{:S(2)}) collective-permute-start(bf16[3584,256]{1,0:T(8,128)(2,1)} %refs_4_.1), channel_id=1, source_target_pairs={{0,1},{1,0},{2,3},{3,2},{4,5},{5,4},{6,7},{7,6},{8,9},{9,8},{10,11... | collective-permute-start | bytes 5505032 | tf_op jit(solution)/shard_map/ppermute | solution.py:511
  1.8 10.8 %collective-permute-start.1 = (bf16[3584,256]{1,0:T(8,128)(2,1)}, bf16[3584,256]{1,0:T(8,128)(2,1)}, u32[]{:S(2)}, u32[]{:S(2)}) collective-permute-start(bf16[3584,256]{1,0:T(8,128)(2,1)} %refs_10_.1), channel_id=1, source_target_pairs={{0,1},{1,0},{2,3},{3,2},{4,5},{5,4},{6,7},{7,6},{8,9},{9,8},{10,11... | collective-permute-start | bytes 5505032 | tf_op jit(solution)/shard_map/ppermute | solution.py:511
  1.8 6.3 %collective-permute-start.2 = (bf16[224,576]{1,0:T(8,128)(2,1)}, bf16[224,576]{1,0:T(8,128)(2,1)S(1)}, u32[]{:S(2)}, u32[]{:S(2)}) collective-permute-start(bf16[224,576]{1,0:T(8,128)(2,1)} %refs_1_.2), channel_id=1, source_target_pairs={{0,1},{1,0},{2,3},{3,2},{4,5},{5,4},{6,7},{7,6},{8,9},{9,8},{10,11... | collective-permute-start | bytes 774152 | tf_op jit(solution)/shard_map/ppermute | solution.py:511
  2.3 10.3 %collective-permute-start.3 = (bf16[224,576]{1,0:T(8,128)(2,1)}, bf16[224,576]{1,0:T(8,128)(2,1)}, u32[]{:S(2)}, u32[]{:S(2)}) collective-permute-start(bf16[224,576]{1,0:T(8,128)(2,1)} %refs_1_.2), channel_id=1, source_target_pairs={{0,2},{1,3},{2,0},{3,1},{4,6},{5,7},{6,4},{7,5},{8,10},{9,11},{10,... | collective-permute-start | bytes 774152 | tf_op jit(solution)/shard_map/ppermute | solution.py:511
  8.1 56.0 %copy-start.2 = (bf16[128,3712]{1,0:T(8,128)(2,1)}, bf16[128,3712]{1,0:T(8,128)(2,1)S(1)}, u32[]{:S(2)}) copy-start(bf16[128,3712]{1,0:T(8,128)(2,1)S(1)} %get-tuple-element.67.refs_0_) | copy-start | bytes 2850820
  12.6 23.1 %collective-permute-start.8 = (bf16[1024,896]{1,0:T(8,128)(2,1)}, bf16[1024,896]{1,0:T(8,128)(2,1)}, u32[]{:S(2)}, u32[]{:S(2)}) collective-permute-start(bf16[1024,896]{1,0:T(8,128)(2,1)} %refs_0_.2), channel_id=1, source_target_pairs={{0,1},{1,0},{2,3},{3,2},{4,5},{5,4},{6,7},{7,6},{8,9},{9,8},{10,11... | collective-permute-start | bytes 5505032 | tf_op jit(solution)/shard_map/ppermute | solution.py:511
  12.6 23.1 %collective-permute-start.7 = (bf16[1792,256]{1,0:T(8,128)(2,1)}, bf16[1792,256]{1,0:T(8,128)(2,1)}, u32[]{:S(2)}, u32[]{:S(2)}) collective-permute-start(bf16[1792,256]{1,0:T(8,128)(2,1)} %get-tuple-element.68), channel_id=1, source_target_pairs={{0,2},{1,3},{2,0},{3,1},{4,6},{5,7},{6,4},{7,5},{8,10},{9,11},{10,... | collective-permute-start | bytes 2752520 | tf_op jit(solution)/shard_map/ppermute | solution.py:511
  14.7 21.0 %collective-permute-start.9 = (bf16[224,576]{1,0:T(8,128)(2,1)}, bf16[224,576]{1,0:T(8,128)(2,1)}, u32[]{:S(2)}, u32[]{:S(2)}) collective-permute-start(bf16[224,576]{1,0:T(8,128)(2,1)} %collective-permute-done.3.refs_5_.refs_3_), channel_id=1, source_target_pairs={{0,1},{1,0},{2,3},{3,2},{4,5},{5,4},{6,7},{7,6},{8,9},{9,8},{10,11... | collective-permute-start | bytes 774152 | tf_op jit(solution)/shard_map/ppermute | solution.py:511
  15.1 49.0 %copy-start.4 = (bf16[224,576]{1,0:T(8,128)(2,1)S(1)}, bf16[224,576]{1,0:T(8,128)(2,1)}, u32[]{:S(2)}) copy-start(bf16[224,576]{1,0:T(8,128)(2,1)} %refs_1_.2) | copy-start | bytes 774148
  15.1 49.0 %copy-start.9 = (s32[3]{0:T(128)S(1)}, s32[3]{0:T(128)}, u32[]{:S(2)}) copy-start(s32[3]{0:T(128)} %pad_add_fusion.place_ref) | copy-start | bytes 40
  15.1 25.9 %collective-permute-start.5 = (bf16[128,3712]{1,0:T(8,128)(2,1)S(1)}, bf16[128,3712]{1,0:T(8,128)(2,1)}, u32[]{:S(2)}, u32[]{:S(2)}) collective-permute-start(bf16[128,3712]{1,0:T(8,128)(2,1)S(1)} %get-tuple-element.67.refs_0_), channel_id=1, source_target_pairs={{0,12},{1,13},{2,14},{3,15},{4,8},{5,9},{6,10},{7,11},{8,4},{9,5},... | collective-permute-start | bytes 2850824 | tf_op jit(solution)/shard_map/ppermute | solution.py:511
  21.9 0.9 copy-start.14
  22.8 40.8 %collective-permute-start.4 = (bf16[128,3712]{1,0:T(8,128)(2,1)S(1)}, bf16[128,3712]{1,0:T(8,128)(2,1)S(1)}, u32[]{:S(2)}, u32[]{:S(2)}) collective-permute-start(bf16[128,3712]{1,0:T(8,128)(2,1)S(1)} %get-tuple-element.67.refs_0_), channel_id=1, source_target_pairs={{0,4},{1,5},{2,6},{3,7},{4,0},{5,1},{6,2},{7,3},{8,12},{9,13},{10,... | collective-permute-start | bytes 2850824 | tf_op jit(solution)/shard_map/ppermute | solution.py:511
  35.7 49.9 %copy-start.10 = (s32[3]{0:T(128)S(1)}, s32[3]{0:T(128)}, u32[]{:S(2)}) copy-start(s32[3]{0:T(128)} %pad_add_fusion.place_ref) | copy-start | bytes 40
  35.7 24.8 %collective-permute-start.10 = (bf16[1792,256]{1,0:T(8,128)(2,1)}, bf16[1792,256]{1,0:T(8,128)(2,1)S(1)}, u32[]{:S(2)}, u32[]{:S(2)}) collective-permute-start(bf16[1792,256]{1,0:T(8,128)(2,1)} %collective-permute-done.7.refs_6_), channel_id=1, source_target_pairs={{0,16},{16,0},{1,17},{17,1},{2,18},{18,2},{3,19},{19,3},{4,20},{20... | collective-permute-start | bytes 2752520 | tf_op jit(solution)/shard_map/ppermute | solution.py:523
  37.5 23.0 %collective-permute-start.11 = (bf16[1792,256]{1,0:T(8,128)(2,1)}, bf16[1792,256]{1,0:T(8,128)(2,1)S(1)}, u32[]{:S(2)}, u32[]{:S(2)}) collective-permute-start(bf16[1792,256]{1,0:T(8,128)(2,1)} %get-tuple-element.73), channel_id=1, source_target_pairs={{0,2},{1,3},{2,0},{3,1},{4,6},{5,7},{6,4},{7,5},{8,10},{9,11},{10,... | collective-permute-start | bytes 2752520 | tf_op jit(solution)/shard_map/ppermute | solution.py:511
  39.0 21.5 %collective-permute-start.12 = (bf16[1792,256]{1,0:T(8,128)(2,1)}, bf16[1792,256]{1,0:T(8,128)(2,1)S(1)}, u32[]{:S(2)}, u32[]{:S(2)}) collective-permute-start(bf16[1792,256]{1,0:T(8,128)(2,1)} %collective-permute-done.7.refs_6_), channel_id=1, source_target_pairs={{0,1},{1,0},{2,3},{3,2},{4,5},{5,4},{6,7},{7,6},{8,9},{9,8},{10,11... | collective-permute-start | bytes 2752520 | tf_op jit(solution)/shard_map/ppermute | solution.py:511
  41.0 40.5 %collective-permute-start.6 = (bf16[128,3712]{1,0:T(8,128)(2,1)}, bf16[128,3712]{1,0:T(8,128)(2,1)S(1)}, u32[]{:S(2)}, u32[]{:S(2)}) collective-permute-start(bf16[128,3712]{1,0:T(8,128)(2,1)} %collective-permute-done.5.refs_2_.refs_3_), channel_id=1, source_target_pairs={{0,4},{1,5},{2,6},{3,7},{4,0},{5,1},{6,2},{7,3},{8,12},{9,13},{10,... | collective-permute-start | bytes 2850824 | tf_op jit(solution)/shard_map/ppermute | solution.py:511
  60.5 6.9 %copy-start.15 = (bf16[1792,256]{1,0:T(8,128)(2,1)}, bf16[1792,256]{1,0:T(8,128)(2,1)S(1)}, u32[]{:S(2)}) copy-start(bf16[1792,256]{1,0:T(8,128)(2,1)S(1)} %collective-permute-done.10.refs_7_) | copy-start | bytes 2752516
  60.5 6.9 %copy-start.16 = (bf16[1792,256]{1,0:T(8,128)(2,1)}, bf16[1792,256]{1,0:T(8,128)(2,1)S(1)}, u32[]{:S(2)}) copy-start(bf16[1792,256]{1,0:T(8,128)(2,1)S(1)} %collective-permute-done.11.refs_12_) | copy-start | bytes 2752516
  60.5 1.0 copy-start.17
  61.5 21.5 %collective-permute-start.13 = (bf16[1792,256]{1,0:T(8,128)(2,1)S(1)}, bf16[1792,256]{1,0:T(8,128)(2,1)S(1)}, u32[]{:S(2)}, u32[]{:S(2)}) collective-permute-start(bf16[1792,256]{1,0:T(8,128)(2,1)S(1)} %collective-permute-done.11.refs_12_), channel_id=1, source_target_pairs={{0,16},{16,0},{1,17},{17,1},{2,18},{18,2},{3,19},{19,3},{4,20},{20... | collective-permute-start | bytes 2752520 | tf_op jit(solution)/shard_map/ppermute | solution.py:523
  63.0 21.5 %collective-permute-start.14 = (bf16[512,896]{1,0:T(8,128)(2,1)}, bf16[512,896]{1,0:T(8,128)(2,1)S(1)}, u32[]{:S(2)}, u32[]{:S(2)}) collective-permute-start(bf16[512,896]{1,0:T(8,128)(2,1)} %copy-done.14), channel_id=1, source_target_pairs={{0,2},{1,3},{2,0},{3,1},{4,6},{5,7},{6,4},{7,5},{8,10},{9,11},{10,... | collective-permute-start | bytes 2752520 | tf_op jit(solution)/shard_map/ppermute | solution.py:511
  63.6 20.9 %collective-permute-start.15 = (bf16[1792,256]{1,0:T(8,128)(2,1)S(1)}, bf16[1792,256]{1,0:T(8,128)(2,1)S(1)}, u32[]{:S(2)}, u32[]{:S(2)}) collective-permute-start(bf16[1792,256]{1,0:T(8,128)(2,1)S(1)} %collective-permute-done.10.refs_7_), channel_id=1, source_target_pairs={{0,1},{1,0},{2,3},{3,2},{4,5},{5,4},{6,7},{7,6},{8,9},{9,8},{10,11... | collective-permute-start | bytes 2752520 | tf_op jit(solution)/shard_map/ppermute | solution.py:511
  63.6 3.9 %copy-start.3 = (bf16[128,3712]{1,0:T(8,128)(2,1)}, bf16[128,3712]{1,0:T(8,128)(2,1)S(1)}, u32[]{:S(2)}) copy-start(bf16[128,3712]{1,0:T(8,128)(2,1)S(1)} %collective-permute-done.4.refs_1_) | copy-start | bytes 2850820
  63.6 20.9 %collective-permute-start.16 = (bf16[1792,256]{1,0:T(8,128)(2,1)S(1)}, bf16[1792,256]{1,0:T(8,128)(2,1)S(1)}, u32[]{:S(2)}, u32[]{:S(2)}) collective-permute-start(bf16[1792,256]{1,0:T(8,128)(2,1)S(1)} %collective-permute-done.11.refs_12_), channel_id=1, source_target_pairs={{0,1},{1,0},{2,3},{3,2},{4,5},{5,4},{6,7},{7,6},{8,9},{9,8},{10,11... | collective-permute-start | bytes 2752520 | tf_op jit(solution)/shard_map/ppermute | solution.py:511
  67.5 21.7 %copy-start.7 = (bf16[128,576]{1,0:T(8,128)(2,1)}, bf16[128,576]{1,0:T(8,128)(2,1)S(1)}, u32[]{:S(2)}) copy-start(bf16[128,576]{1,0:T(8,128)(2,1)S(1)} %get-tuple-element.106) | copy-start | bytes 442372
  81.5 11.7 %copy-start.1 = (bf16[128,3712]{1,0:T(8,128)(2,1)}, bf16[128,3712]{1,0:T(8,128)(2,1)S(1)}, u32[]{:S(2)}) copy-start(bf16[128,3712]{1,0:T(8,128)(2,1)S(1)} %collective-permute-done.6.refs_2_.refs_0_) | copy-start | bytes 2850820
  83.1 7.8 %copy-start.18 = (bf16[1792,256]{1,0:T(8,128)(2,1)}, bf16[1792,256]{1,0:T(8,128)(2,1)S(1)}, u32[]{:S(2)}) copy-start(bf16[1792,256]{1,0:T(8,128)(2,1)S(1)} %collective-permute-done.13.refs_13_) | copy-start | bytes 2752516
  84.5 6.4 %copy-start.19 = (bf16[1792,256]{1,0:T(8,128)(2,1)}, bf16[1792,256]{1,0:T(8,128)(2,1)S(1)}, u32[]{:S(2)}) copy-start(bf16[1792,256]{1,0:T(8,128)(2,1)S(1)} %collective-permute-done.15.refs_9_) | copy-start | bytes 2752516
  84.5 6.4 %copy-start.20 = (bf16[1792,256]{1,0:T(8,128)(2,1)}, bf16[1792,256]{1,0:T(8,128)(2,1)S(1)}, u32[]{:S(2)}) copy-start(bf16[1792,256]{1,0:T(8,128)(2,1)S(1)} %collective-permute-done.16.refs_14_) | copy-start | bytes 2752516
  84.5 6.4 %collective-permute-start.17 = (bf16[1792,256]{1,0:T(8,128)(2,1)S(1)}, bf16[1792,256]{1,0:T(8,128)(2,1)S(1)}, u32[]{:S(2)}, u32[]{:S(2)}) collective-permute-start(bf16[1792,256]{1,0:T(8,128)(2,1)S(1)} %collective-permute-done.13.refs_13_), channel_id=1, source_target_pairs={{0,1},{1,0},{2,3},{3,2},{4,5},{5,4},{6,7},{7,6},{8,9},{9,8},{10,11... | collective-permute-start | bytes 2752520 | tf_op jit(solution)/shard_map/ppermute | solution.py:511
  84.6 23.3 %collective-permute-start.21 = (bf16[512,896]{1,0:T(8,128)(2,1)S(1)}, bf16[512,896]{1,0:T(8,128)(2,1)S(1)}, u32[]{:S(2)}, u32[]{:S(2)}) collective-permute-start(bf16[512,896]{1,0:T(8,128)(2,1)S(1)} %collective-permute-done.14.refs_2_), channel_id=1, source_target_pairs={{0,1},{1,0},{2,3},{3,2},{4,5},{5,4},{6,7},{7,6},{8,9},{9,8},{10,11... | collective-permute-start | bytes 2752520 | tf_op jit(solution)/shard_map/ppermute | solution.py:511
  85.1 22.8 %collective-permute-start.22 = (bf16[512,896]{1,0:T(8,128)(2,1)S(1)}, bf16[512,896]{1,0:T(8,128)(2,1)}, u32[]{:S(2)}, u32[]{:S(2)}) collective-permute-start(bf16[512,896]{1,0:T(8,128)(2,1)S(1)} %collective-permute-done.14.refs_2_), channel_id=1, source_target_pairs={{0,16},{16,0},{1,17},{17,1},{2,18},{18,2},{3,19},{19,3},{4,20},{20... | collective-permute-start | bytes 2752520 | tf_op jit(solution)/shard_map/ppermute | solution.py:523
  87.8 20.1 %collective-permute-start.19 = (bf16[128,576]{1,0:T(8,128)(2,1)S(1)}, bf16[128,576]{1,0:T(8,128)(2,1)S(1)}, u32[]{:S(2)}, u32[]{:S(2)}) collective-permute-start(bf16[128,576]{1,0:T(8,128)(2,1)S(1)} %latent_parts.3), channel_id=1, source_target_pairs={{0,8},{1,9},{2,10},{3,11},{4,12},{5,13},{6,14},{7,15},{8,0},{9,1},... | collective-permute-start | bytes 442376 | tf_op jit(solution)/shard_map/ppermute | solution.py:511
  89.2 18.8 %collective-permute-start.18 = (bf16[128,576]{1,0:T(8,128)(2,1)}, bf16[128,576]{1,0:T(8,128)(2,1)S(1)}, u32[]{:S(2)}, u32[]{:S(2)}) collective-permute-start(bf16[128,576]{1,0:T(8,128)(2,1)} %get-tuple-element.92), channel_id=1, source_target_pairs={{0,4},{1,5},{2,6},{3,7},{4,0},{5,1},{6,2},{7,3},{8,12},{9,13},{10,... | collective-permute-start | bytes 442376 | tf_op jit(solution)/shard_map/ppermute | solution.py:511
  90.9 0.9 copy-start.21
  91.8 16.1 %collective-permute-start.20 = (bf16[128,576]{1,0:T(8,128)(2,1)}, bf16[128,576]{1,0:T(8,128)(2,1)}, u32[]{:S(2)}, u32[]{:S(2)}) collective-permute-start(bf16[128,576]{1,0:T(8,128)(2,1)} %get-tuple-element.93), channel_id=1, source_target_pairs={{0,12},{1,13},{2,14},{3,15},{4,8},{5,9},{6,10},{7,11},{8,4},{9,5},... | collective-permute-start | bytes 442376 | tf_op jit(solution)/shard_map/ppermute | solution.py:511
  93.2 0.7 copy-start.11
  93.9 14.2 %copy-start.24 = (s32[128]{0:T(128)S(1)}, s32[128]{0:T(128)}, u32[]{:S(2)}) copy-start(s32[128]{0:T(128)} %multiply_add_fusion) | copy-start | bytes 1540
  93.9 14.3 %copy-start.8 = (bf16[128,576]{1,0:T(8,128)(2,1)S(1)}, bf16[128,576]{1,0:T(8,128)(2,1)}, u32[]{:S(2)}) copy-start(bf16[128,576]{1,0:T(8,128)(2,1)} %copy-done.7) | copy-start | bytes 442372
  93.9 16.8 %copy-start = (bf16[1024,896]{1,0:T(8,128)(2,1)S(1)}, bf16[1024,896]{1,0:T(8,128)(2,1)}, u32[]{:S(2)}) copy-start(bf16[1024,896]{1,0:T(8,128)(2,1)} %refs_0_.2) | copy-start | bytes 5505028
  108.0 2.7 %collective-permute-start.23 = (bf16[512,896]{1,0:T(8,128)(2,1)}, bf16[512,896]{1,0:T(8,128)(2,1)S(1)}, u32[]{:S(2)}, u32[]{:S(2)}) collective-permute-start(bf16[512,896]{1,0:T(8,128)(2,1)} %collective-permute-done.22.refs_3_), channel_id=1, source_target_pairs={{0,1},{1,0},{2,3},{3,2},{4,5},{5,4},{6,7},{7,6},{8,9},{9,8},{10,11... | collective-permute-start | bytes 2752520 | tf_op jit(solution)/shard_map/ppermute | solution.py:511
  108.1 18.1 %collective-permute-start.25 = (bf16[128,1792]{1,0:T(8,128)(2,1)}, bf16[128,1792]{1,0:T(8,128)(2,1)}, u32[]{:S(2)}, u32[]{:S(2)}) collective-permute-start(bf16[128,1792]{1,0:T(8,128)(2,1)} %get-tuple-element.103), channel_id=1, source_target_pairs={{0,4},{1,5},{2,6},{3,7},{4,0},{5,1},{6,2},{7,3},{8,12},{9,13},{10,... | collective-permute-start | bytes 1376264 | tf_op jit(solution)/shard_map/ppermute | solution.py:511
  110.7 9.5 %copy-start.22 = (f32[512]{0:T(512)S(1)}, f32[512]{0:T(512)}, u32[]{:S(2)}) copy-start(f32[512]{0:T(512)} %param.13) | copy-start | bytes 6148
  117.4 1.0 copy-start.5
  118.4 0.9 copy-start.12
  119.3 14.7 %collective-permute-start.24 = (bf16[128,1792]{1,0:T(8,128)(2,1)S(1)}, bf16[128,1792]{1,0:T(8,128)(2,1)S(1)}, u32[]{:S(2)}, u32[]{:S(2)}) collective-permute-start(bf16[128,1792]{1,0:T(8,128)(2,1)S(1)} %get-tuple-element.102), channel_id=1, source_target_pairs={{0,4},{1,5},{2,6},{3,7},{4,0},{5,1},{6,2},{7,3},{8,12},{9,13},{10,... | collective-permute-start | bytes 1376264 | tf_op jit(solution)/shard_map/ppermute | solution.py:511
  121.6 17.3 %copy-start.13 = (bf16[128,3584]{1,0:T(8,128)(2,1)S(1)}, bf16[128,3584]{1,0:T(8,128)(2,1)}, u32[]{:S(2)}) copy-start(bf16[128,3584]{1,0:T(8,128)(2,1)} %copy-done.12) | copy-start | bytes 2752516
  121.7 14.8 %collective-permute-start.26 = (bf16[4,16,576]{2,1,0:T(8,128)(2,1)S(1)}, bf16[4,16,576]{2,1,0:T(8,128)(2,1)S(1)}, u32[]{:S(2)}, u32[]{:S(2)}) collective-permute-start(bf16[4,16,576]{2,1,0:T(8,128)(2,1)S(1)} %get-tuple-element.128), channel_id=1, source_target_pairs={{0,4},{1,5},{2,6},{3,7},{4,0},{5,1},{6,2},{7,3},{8,12},{9,13},{10,... | collective-permute-start | bytes 221192 | tf_op jit(solution)/shard_map/ppermute | solution.py:511
  122.8 13.6 %collective-permute-start.27 = (bf16[4,16,576]{2,1,0:T(8,128)(2,1)S(1)}, bf16[4,16,576]{2,1,0:T(8,128)(2,1)S(1)}, u32[]{:S(2)}, u32[]{:S(2)}) collective-permute-start(bf16[4,16,576]{2,1,0:T(8,128)(2,1)S(1)} %get-tuple-element.127), channel_id=1, source_target_pairs={{0,8},{1,9},{2,10},{3,11},{4,12},{5,13},{6,14},{7,15},{8,0},{9,1},... | collective-permute-start | bytes 221192 | tf_op jit(solution)/shard_map/ppermute | solution.py:511
  124.8 14.1 %collective-permute-start.28 = (bf16[4,16,576]{2,1,0:T(8,128)(2,1)S(1)}, bf16[4,16,576]{2,1,0:T(8,128)(2,1)}, u32[]{:S(2)}, u32[]{:S(2)}) collective-permute-start(bf16[4,16,576]{2,1,0:T(8,128)(2,1)S(1)} %get-tuple-element.126), channel_id=1, source_target_pairs={{0,12},{1,13},{2,14},{3,15},{4,8},{5,9},{6,10},{7,11},{8,4},{9,5},... | collective-permute-start | bytes 221192 | tf_op jit(solution)/shard_map/ppermute | solution.py:511
  138.9 42.2 %collective-permute-start.29 = (bf16[128,3584]{1,0:T(8,128)(2,1)S(1)}, bf16[128,3584]{1,0:T(8,128)(2,1)S(1)}, u32[]{:S(2)}, u32[]{:S(2)}) collective-permute-start(bf16[128,3584]{1,0:T(8,128)(2,1)S(1)} %copy-done.13), channel_id=1, source_target_pairs={{0,4},{1,5},{2,6},{3,7},{4,0},{5,1},{6,2},{7,3},{8,12},{9,13},{10,... | collective-permute-start | bytes 2752520 | tf_op jit(solution)/shard_map/ppermute | solution.py:511
  138.9 42.2 %collective-permute-start.30 = (bf16[128,3584]{1,0:T(8,128)(2,1)}, bf16[128,3584]{1,0:T(8,128)(2,1)}, u32[]{:S(2)}, u32[]{:S(2)}) collective-permute-start(bf16[128,3584]{1,0:T(8,128)(2,1)} %add_convert_fusion.1), channel_id=1, source_target_pairs={{0,12},{1,13},{2,14},{3,15},{4,8},{5,9},{6,10},{7,11},{8,4},{9,5},... | collective-permute-start | bytes 2752520 | tf_op jit(solution)/shard_map/ppermute | solution.py:511
  140.3 40.9 %copy-start.6 = (bf16[128,3584]{1,0:T(8,128)(2,1)S(1)}, bf16[128,3584]{1,0:T(8,128)(2,1)}, u32[]{:S(2)}) copy-start(bf16[128,3584]{1,0:T(8,128)(2,1)} %copy-done.5) | copy-start | bytes 2752516
  141.4 6.2 %collective-permute-start.31 = (bf16[4,2,16,576]{3,2,0,1:T(8,128)(2,1)S(1)}, bf16[4,2,16,576]{3,2,0,1:T(8,128)(2,1)S(1)}, u32[]{:S(2)}, u32[]{:S(2)}) collective-permute-start(bf16[4,2,16,576]{3,2,0,1:T(8,128)(2,1)S(1)} %get-tuple-element.124), channel_id=1, source_target_pairs={{0,2},{1,3},{2,0},{3,1},{4,6},{5,7},{6,4},{7,5},{8,10},{9,11},{10,... | collective-permute-start | bytes 442376 | tf_op jit(solution)/shard_map/ppermute | solution.py:511
  147.6 1.5 collective-permute-start.32

commit v6 on v5

--- a/solution.py
+++ b/solution.py
@@ -531,8 +531,7 @@
     slots = cache_slots(owner, device_count, push_cap)
 
     kv_core, kv_x = other_core(kv_weight), other_chip(kv_weight)
-    gate_own, up_own, place_info = hold((gate_weight, up_weight, place_info))
-    gate_core, up_core = other_core(gate_own), other_core(up_own)
+    gate_core, up_core = other_core(gate_weight), other_core(up_weight)
     rows, gate_half = entry(
         place_info, tokens, norm_gain, expert_index, route_gate, gate_weight
     )

time: 184 us -> 183 us (level)
  no operation moved by 1% of the time
where the time goes in v6:
time: 183 us
  waiting for transfers between devices  83.6 us (46%)
  starting transfers between devices  47.6 us (26%)
  Pallas kernels  33.8 us (18%)
  other arithmetic  10.5 us (6%)
  local copies, waits for them, and re-layouts  6.42 us (4%)
    ppermute x30, waiting for transfers between devices, exchange(): lax.ppermute(value, 'dev', [(i, i ^ distance) for i in range(device_count)])  82.1 us
    ppermute x30, starting transfers between devices, exchange(): lax.ppermute(value, 'dev', [(i, i ^ distance) for i in range(device_count)])  43.7 us
    pallas_call x1, Pallas kernels, hidden_units(): pl.pallas_call(hidden_kernel, out_shape=[pltpu.VMEM((LINE * tok_rows, GRO...  14 us
    pallas_call x1, Pallas kernels, rest_products(): pl.pallas_call(rest_kernel, out_shape=[pltpu.VMEM((tok_rows, GROUP * widt...  6.67 us
    unnamed x51, local copies, waits for them, and re-layouts  6.34 us
    pallas_call x2, Pallas kernels, latent_parts(): pl.pallas_call(functools.partial(latent_kernel, len(rows)), out_shape=[pl...  5.46 us
    convert_element_type x2, other arithmetic, narrow(): return value.astype(jnp.bfloat16)  4.84 us
    ppermute x3, starting transfers between devices, other_rep(): return lax.ppermute(value, 'rep', [(0, 1), (1, 0)])  3.86 us
  transfers between devices with their start and end apart: 33, of which 12 were waited for; matrix products, arithmetic and copies ran while one was open for 5% of the time, Pallas kernels for 18%

profile of v6, /device:TPU:0, one launch (start us, length us, event | category | flops | bytes accessed | tf_op | source)
XLA Modules:
  0.0 183.0 jit_solution(4764129148136209513)
XLA Ops:
  0.6 0.5 collective-permute-start
  1.2 0.1 collective-permute-start.1
  1.2 0.4 collective-permute-start.2
  1.7 2.6 %collective-permute-start.3 = (bf16[224,576]{1,0:T(8,128)(2,1)}, bf16[224,576]{1,0:T(8,128)(2,1)}, u32[]{:S(2)}, u32[]{:S(2)}) collective-permute-start(bf16[224,576]{1,0:T(8,128)(2,1)} %refs_1_.2), channel_id=1, source_target_pairs={{0,2},{1,3},{2,0},{3,1},{4,6},{5,7},{6,4},{7,5},{8,10},{9,11},{10,... | collective-permute-start | bytes 774152 | tf_op jit(solution)/shard_map/ppermute | solution.py:511
  4.2 0.7 pad_add_fusion.place_ref
  4.9 3.3 %entry.1 = (bf16[128,3712]{1,0:T(8,128)(2,1)S(1)}, bf16[1792,256]{1,0:T(8,128)(2,1)}) custom-call(s32[3]{0:T(128)} %pad_add_fusion.place_ref, bf16[128,3584]{1,0:T(8,128)(2,1)} %tokens_ref.1, f32[28,128]{1,0:T(8,128)} %bitcast.41, s32[2,128]{1,0:T(2,128)} %bitcast.44, f32[2,128]{1,0:T(2,128)} %bitcast.45, bf16[3584,256]{1,0:T(8,128)(2,1)} %refs_4_.1), custom_call_target="tpu_custom_call" | custom-call | flops 1048576 | bytes 1048576 | tf_op jit(solution)/shard_map/entry/pallas_call | solution.py:195
  8.2 3.7 %collective-permute-done.3.refs_5_.refs_3_ = bf16[224,576]{1,0:T(8,128)(2,1)} collective-permute-done((bf16[224,576]{1,0:T(8,128)(2,1)}, bf16[224,576]{1,0:T(8,128)(2,1)}, u32[]{:S(2)}, u32[]{:S(2)}) %collective-permute-start.3) | collective-permute-done | bytes 258080 | tf_op jit(solution)/shard_map/ppermute | solution.py:511
  12.0 1.8 collective-permute-start.7
  13.8 0.1 fusion.19
  13.9 0.2 reduce_window_sum.11
  14.1 0.2 collective-permute-start.9
  14.3 0.2 select_reduce_fusion
  14.5 3.7 %collective-permute-start.5 = (bf16[128,3712]{1,0:T(8,128)(2,1)S(1)}, bf16[128,3712]{1,0:T(8,128)(2,1)}, u32[]{:S(2)}, u32[]{:S(2)}) collective-permute-start(bf16[128,3712]{1,0:T(8,128)(2,1)S(1)} %get-tuple-element.61.refs_0_), channel_id=1, source_target_pairs={{0,12},{1,13},{2,14},{3,15},{4,8},{5,9},{6,10},{7,11},{8,4},{9,5},... | collective-permute-start | bytes 2850824 | tf_op jit(solution)/shard_map/ppermute | solution.py:511
  18.2 3.1 %weight_halves.1 = (bf16[1792,256]{1,0:T(8,128)(2,1)}, bf16[512,896]{1,0:T(8,128)(2,1)S(1)}) custom-call(s32[3]{0:T(128)} %pad_add_fusion.place_ref, bf16[3584,256]{1,0:T(8,128)(2,1)} %refs_10_.1, bf16[1024,896]{1,0:T(8,128)(2,1)} %refs_0_.2), custom_call_target="tpu_custom_call" | custom-call | flops 1048576 | bytes 1048576 | tf_op jit(solution)/shard_map/weight_halves/pallas_call | solution.py:228
  21.3 0.9 copy-done.14
  22.2 0.5 multiply_add_fusion
  22.8 12.3 %collective-permute-done.7.refs_6_ = bf16[1792,256]{1,0:T(8,128)(2,1)} collective-permute-done((bf16[1792,256]{1,0:T(8,128)(2,1)}, bf16[1792,256]{1,0:T(8,128)(2,1)}, u32[]{:S(2)}, u32[]{:S(2)}) %collective-permute-start.7) | collective-permute-done | bytes 917536 | tf_op jit(solution)/shard_map/ppermute | solution.py:511
  35.1 1.8 %collective-permute-start.10 = (bf16[1792,256]{1,0:T(8,128)(2,1)}, bf16[1792,256]{1,0:T(8,128)(2,1)S(1)}, u32[]{:S(2)}, u32[]{:S(2)}) collective-permute-start(bf16[1792,256]{1,0:T(8,128)(2,1)} %collective-permute-done.7.refs_6_), channel_id=1, source_target_pairs={{0,16},{16,0},{1,17},{17,1},{2,18},{18,2},{3,19},{19,3},{4,20},{20... | collective-permute-start | bytes 2752520 | tf_op jit(solution)/shard_map/ppermute | solution.py:523
  36.9 1.5 collective-permute-start.11
  38.4 2.0 %collective-permute-done.5.refs_2_.refs_3_ = bf16[128,3712]{1,0:T(8,128)(2,1)} collective-permute-done((bf16[128,3712]{1,0:T(8,128)(2,1)S(1)}, bf16[128,3712]{1,0:T(8,128)(2,1)}, u32[]{:S(2)}, u32[]{:S(2)}) %collective-permute-start.5) | collective-permute-done | bytes 950304 | tf_op jit(solution)/shard_map/ppermute | solution.py:511
  40.4 19.5 %collective-permute-start.6 = (bf16[128,3712]{1,0:T(8,128)(2,1)}, bf16[128,3712]{1,0:T(8,128)(2,1)S(1)}, u32[]{:S(2)}, u32[]{:S(2)}) collective-permute-start(bf16[128,3712]{1,0:T(8,128)(2,1)} %collective-permute-done.5.refs_2_.refs_3_), channel_id=1, source_target_pairs={{0,4},{1,5},{2,6},{3,7},{4,0},{5,1},{6,2},{7,3},{8,12},{9,13},{10,... | collective-permute-start | bytes 2850824 | tf_op jit(solution)/shard_map/ppermute | solution.py:511
  60.0 1.0 copy-done.17
  60.9 1.5 collective-permute-start.13
  62.5 0.5 collective-permute-start.14
  63.0 0.5 collective-permute-start.16
  63.5 3.3 %latent_parts.2 = (bf16[128,576]{1,0:T(8,128)(2,1)S(1)}, bf16[128,576]{1,0:T(8,128)(2,1)}, bf16[128,576]{1,0:T(8,128)(2,1)}) custom-call(s32[3]{0:T(128)S(1)} %copy-done.9, bf16[128,3712]{1,0:T(8,128)(2,1)S(1)} %get-tuple-element.61.refs_0_, bf16[128,3712]{1,0:T(8,128)(2,1)S(1)} %collective-permute-done.4.refs_1_, ...), custom_call_target="tpu_custom_call" | custom-call | flops 1048576 | bytes 1048576 | tf_op jit(solution)/shard_map/latent_parts/pallas_call | solution.py:293
  66.9 14.0 %collective-permute-done.6.refs_2_.refs_0_ = bf16[128,3712]{1,0:T(8,128)(2,1)S(1)} collective-permute-done((bf16[128,3712]{1,0:T(8,128)(2,1)}, bf16[128,3712]{1,0:T(8,128)(2,1)S(1)}, u32[]{:S(2)}, u32[]{:S(2)}) %collective-permute-start.6) | collective-permute-done | bytes 950304 | tf_op jit(solution)/shard_map/ppermute | solution.py:511
  80.9 1.6 collective-permute-done.13.refs_13_
  82.5 1.4 collective-permute-done.14.refs_2_
  84.0 0.5 collective-permute-start.21
  84.5 0.5 collective-permute-start.22
  85.0 2.1 %latent_parts.3 = bf16[128,576]{1,0:T(8,128)(2,1)S(1)} custom-call(s32[3]{0:T(128)S(1)} %copy-done.10, bf16[128,3712]{1,0:T(8,128)(2,1)S(1)} %collective-permute-done.6.refs_2_.refs_0_, bf16[224,576]{1,0:T(8,128)(2,1)S(1)} %copy-done.4, bf16[224,576]{1,0:T(8,128)(2,1)S(1)} %collective-permute-done.2.refs_4_.refs_2_, ...), custom_call_target="tpu_custom_call" | custom-call | flops 1048576 | bytes 1048576 | tf_op jit(solution)/shard_map/latent_parts/pallas_call | solution.py:293
  87.2 1.4 collective-permute-start.19
  88.6 1.7 collective-permute-start.18
  90.3 0.9 copy-done.21
  91.2 1.4 collective-permute-start.20
  92.6 0.7 copy-done.11
  93.3 14.0 %hidden_units.1 = (bf16[512,1024]{1,0:T(8,128)(2,1)S(1)}, f32[512,1]{1,0:T(8,128)S(1)}, bf16[128,1792]{1,0:T(8,128)(2,1)}) custom-call(s32[3]{0:T(128)S(1)} %copy-done.11, bf16[128,3712]{1,0:T(8,128)(2,1)} %copy-done.2, bf16[128,3712]{1,0:T(8,128)(2,1)} %copy-done.3, bf16[128,3712]{1,0:T(8,128)(2,1)} %copy-done.1, ...), custom_call_target="tpu_custom_call" | custom-call | flops 1048576 | bytes 1048576 | tf_op jit(solution)/shard_map/hidden_units/pallas_call | solution.py:383
  107.6 1.0 add_add_fusion
  108.6 0.1 multiply_reduce_fusion
  108.7 0.3 fusion.16
  109.0 1.1 collective-permute-done.23.refs_5_
  110.1 6.7 %rest_products.1 = (bf16[128,3584]{1,0:T(8,128)(2,1)S(1)}, bf16[128,3584]{1,0:T(8,128)(2,1)S(1)}, bf16[128,3584]{1,0:T(8,128)(2,1)S(1)}, bf16[128,1792]{1,0:T(8,128)(2,1)S(1)}) custom-call(s32[3]{0:T(128)S(1)} %copy-done.11, bf16[512,1024]{1,0:T(8,128)(2,1)S(1)} %get-tuple-element.90.hidden_ref, f32[512,1]{1,0:T(8,128)S(1)} %get-tuple-element.91.scale_ref, ...), custom_call_target="tpu_custom_call" | custom-call | flops 1048576 | bytes 1048576 | tf_op jit(solution)/shard_map/rest_products/pallas_call | solution.py:436
  116.8 1.0 copy-done.5
  117.8 0.9 copy-done.12
  118.7 0.9 collective-permute-start.24
  119.6 0.1 multiply_convert_fusion
  119.7 1.3 scatter_custom_fusion
  121.1 1.2 collective-permute-start.26
  122.2 1.9 %collective-permute-start.27 = (bf16[4,16,576]{2,1,0:T(8,128)(2,1)S(1)}, bf16[4,16,576]{2,1,0:T(8,128)(2,1)S(1)}, u32[]{:S(2)}, u32[]{:S(2)}) collective-permute-start(bf16[4,16,576]{2,1,0:T(8,128)(2,1)S(1)} %get-tuple-element.121), channel_id=1, source_target_pairs={{0,8},{1,9},{2,10},{3,11},{4,12},{5,13},{6,14},{7,15},{8,0},{9,1},... | collective-permute-start | bytes 221192 | tf_op jit(solution)/shard_map/ppermute | solution.py:511
  124.2 1.4 collective-permute-start.28
  125.5 7.9 %collective-permute-done.24 = bf16[128,1792]{1,0:T(8,128)(2,1)S(1)} collective-permute-done((bf16[128,1792]{1,0:T(8,128)(2,1)S(1)}, bf16[128,1792]{1,0:T(8,128)(2,1)S(1)}, u32[]{:S(2)}, u32[]{:S(2)}) %collective-permute-start.24) | collective-permute-done | bytes 458784 | tf_op jit(solution)/shard_map/ppermute | solution.py:511
  133.4 2.4 %add_convert_fusion.1 = bf16[128,3584]{1,0:T(8,128)(2,1)} fusion(bf16[128,3584]{1,0:T(8,128)(2,1)S(1)} %get-tuple-element.95, bf16[128,1792]{1,0:T(8,128)(2,1)} %collective-permute-done.25, bf16[128,1792]{1,0:T(8,128)(2,1)S(1)} %collective-permute-done.24, pred[]{:T(512)S(6)} %eq.33), kind=kLoop, calls=%fused_computation.2 | loop fusion | flops 5963776 | bytes 2752513 | tf_op jit(solution)/shard_map/convert_element_type | solution.py:526
  135.8 2.5 %collective-permute-done.28 = bf16[4,16,576]{2,1,0:T(8,128)(2,1)} collective-permute-done((bf16[4,16,576]{2,1,0:T(8,128)(2,1)S(1)}, bf16[4,16,576]{2,1,0:T(8,128)(2,1)}, u32[]{:S(2)}, u32[]{:S(2)}) %collective-permute-start.28) | collective-permute-done | bytes 73760 | tf_op jit(solution)/shard_map/ppermute | solution.py:511
  138.3 1.4 collective-permute-start.30
  139.7 1.0 pad_maximum_fusion
  140.8 0.4 collective-permute-start.31
  141.2 5.8 %collective-permute-done.31 = bf16[4,2,16,576]{3,2,0,1:T(8,128)(2,1)S(1)} collective-permute-done((bf16[4,2,16,576]{3,2,0,1:T(8,128)(2,1)S(1)}, bf16[4,2,16,576]{3,2,0,1:T(8,128)(2,1)S(1)}, u32[]{:S(2)}, u32[]{:S(2)}) %collective-permute-start.31) | collective-permute-done | bytes 147488 | tf_op jit(solution)/shard_map/ppermute | solution.py:511
  147.1 0.1 pad_add_fusion.1.place_ref
  147.2 1.3 collective-permute-done.32
  148.6 1.2 in_source_order.1
  149.8 0.9 copy.14
  150.6 29.9 %collective-permute-done.29 = bf16[128,3584]{1,0:T(8,128)(2,1)S(1)} collective-permute-done((bf16[128,3584]{1,0:T(8,128)(2,1)S(1)}, bf16[128,3584]{1,0:T(8,128)(2,1)S(1)}, u32[]{:S(2)}, u32[]{:S(2)}) %collective-permute-start.29) | collective-permute-done | bytes 917536 | tf_op jit(solution)/shard_map/ppermute | solution.py:511
  180.6 2.4 %add_convert_fusion = bf16[128,3584]{1,0:T(8,128)(2,1)} fusion(bf16[128,3584]{1,0:T(8,128)(2,1)} %collective-permute-done.30, bf16[128,3584]{1,0:T(8,128)(2,1)S(1)} %collective-permute-done.29, bf16[128,3584]{1,0:T(8,128)(2,1)S(1)} %copy-done.6), kind=kLoop, calls=%fused_computation.1 | loop fusion | flops 2752512 | bytes 3670016 | tf_op jit(solution)/shard_map/convert_element_type | solution.py:526
  (82 shorter events, 0.6 us)
Async XLA Ops:
  0.6 13.2 %copy-start.23 = (s32[128,1]{0,1:T(1,128)S(1)}, s32[128,1]{0,1:T(1,128)}, u32[]{:S(2)}) copy-start(s32[128,1]{0,1:T(1,128)} %param.19) | copy-start | bytes 1540
  0.6 11.3 %collective-permute-start = (bf16[3584,256]{1,0:T(8,128)(2,1)}, bf16[3584,256]{1,0:T(8,128)(2,1)}, u32[]{:S(2)}, u32[]{:S(2)}) collective-permute-start(bf16[3584,256]{1,0:T(8,128)(2,1)} %refs_4_.1), channel_id=1, source_target_pairs={{0,1},{1,0},{2,3},{3,2},{4,5},{5,4},{6,7},{7,6},{8,9},{9,8},{10,11... | collective-permute-start | bytes 5505032 | tf_op jit(solution)/shard_map/ppermute | solution.py:511
  1.2 10.8 %collective-permute-start.1 = (bf16[3584,256]{1,0:T(8,128)(2,1)}, bf16[3584,256]{1,0:T(8,128)(2,1)}, u32[]{:S(2)}, u32[]{:S(2)}) collective-permute-start(bf16[3584,256]{1,0:T(8,128)(2,1)} %refs_10_.1), channel_id=1, source_target_pairs={{0,1},{1,0},{2,3},{3,2},{4,5},{5,4},{6,7},{7,6},{8,9},{9,8},{10,11... | collective-permute-start | bytes 5505032 | tf_op jit(solution)/shard_map/ppermute | solution.py:511
  1.2 7.0 %collective-permute-start.2 = (bf16[224,576]{1,0:T(8,128)(2,1)}, bf16[224,576]{1,0:T(8,128)(2,1)S(1)}, u32[]{:S(2)}, u32[]{:S(2)}) collective-permute-start(bf16[224,576]{1,0:T(8,128)(2,1)} %refs_1_.2), channel_id=1, source_target_pairs={{0,1},{1,0},{2,3},{3,2},{4,5},{5,4},{6,7},{7,6},{8,9},{9,8},{10,11... | collective-permute-start | bytes 774152 | tf_op jit(solution)/shard_map/ppermute | solution.py:511
  1.7 10.3 %collective-permute-start.3 = (bf16[224,576]{1,0:T(8,128)(2,1)}, bf16[224,576]{1,0:T(8,128)(2,1)}, u32[]{:S(2)}, u32[]{:S(2)}) collective-permute-start(bf16[224,576]{1,0:T(8,128)(2,1)} %refs_1_.2), channel_id=1, source_target_pairs={{0,2},{1,3},{2,0},{3,1},{4,6},{5,7},{6,4},{7,5},{8,10},{9,11},{10,... | collective-permute-start | bytes 774152 | tf_op jit(solution)/shard_map/ppermute | solution.py:511
  8.2 55.3 %copy-start.2 = (bf16[128,3712]{1,0:T(8,128)(2,1)}, bf16[128,3712]{1,0:T(8,128)(2,1)S(1)}, u32[]{:S(2)}) copy-start(bf16[128,3712]{1,0:T(8,128)(2,1)S(1)} %get-tuple-element.61.refs_0_) | copy-start | bytes 2850820
  12.0 23.1 %collective-permute-start.8 = (bf16[1024,896]{1,0:T(8,128)(2,1)}, bf16[1024,896]{1,0:T(8,128)(2,1)}, u32[]{:S(2)}, u32[]{:S(2)}) collective-permute-start(bf16[1024,896]{1,0:T(8,128)(2,1)} %refs_0_.2), channel_id=1, source_target_pairs={{0,1},{1,0},{2,3},{3,2},{4,5},{5,4},{6,7},{7,6},{8,9},{9,8},{10,11... | collective-permute-start | bytes 5505032 | tf_op jit(solution)/shard_map/ppermute | solution.py:511
  12.0 23.1 %collective-permute-start.7 = (bf16[1792,256]{1,0:T(8,128)(2,1)}, bf16[1792,256]{1,0:T(8,128)(2,1)}, u32[]{:S(2)}, u32[]{:S(2)}) collective-permute-start(bf16[1792,256]{1,0:T(8,128)(2,1)} %get-tuple-element.62), channel_id=1, source_target_pairs={{0,2},{1,3},{2,0},{3,1},{4,6},{5,7},{6,4},{7,5},{8,10},{9,11},{10,... | collective-permute-start | bytes 2752520 | tf_op jit(solution)/shard_map/ppermute | solution.py:511
  14.1 21.0 %collective-permute-start.9 = (bf16[224,576]{1,0:T(8,128)(2,1)}, bf16[224,576]{1,0:T(8,128)(2,1)}, u32[]{:S(2)}, u32[]{:S(2)}) collective-permute-start(bf16[224,576]{1,0:T(8,128)(2,1)} %collective-permute-done.3.refs_5_.refs_3_), channel_id=1, source_target_pairs={{0,1},{1,0},{2,3},{3,2},{4,5},{5,4},{6,7},{7,6},{8,9},{9,8},{10,11... | collective-permute-start | bytes 774152 | tf_op jit(solution)/shard_map/ppermute | solution.py:511
  14.5 49.0 %copy-start.4 = (bf16[224,576]{1,0:T(8,128)(2,1)S(1)}, bf16[224,576]{1,0:T(8,128)(2,1)}, u32[]{:S(2)}) copy-start(bf16[224,576]{1,0:T(8,128)(2,1)} %refs_1_.2) | copy-start | bytes 774148
  14.5 49.0 %copy-start.9 = (s32[3]{0:T(128)S(1)}, s32[3]{0:T(128)}, u32[]{:S(2)}) copy-start(s32[3]{0:T(128)} %pad_add_fusion.place_ref) | copy-start | bytes 40
  14.5 25.9 %collective-permute-start.5 = (bf16[128,3712]{1,0:T(8,128)(2,1)S(1)}, bf16[128,3712]{1,0:T(8,128)(2,1)}, u32[]{:S(2)}, u32[]{:S(2)}) collective-permute-start(bf16[128,3712]{1,0:T(8,128)(2,1)S(1)} %get-tuple-element.61.refs_0_), channel_id=1, source_target_pairs={{0,12},{1,13},{2,14},{3,15},{4,8},{5,9},{6,10},{7,11},{8,4},{9,5},... | collective-permute-start | bytes 2850824 | tf_op jit(solution)/shard_map/ppermute | solution.py:511
  21.3 0.9 copy-start.14
  22.2 40.8 %collective-permute-start.4 = (bf16[128,3712]{1,0:T(8,128)(2,1)S(1)}, bf16[128,3712]{1,0:T(8,128)(2,1)S(1)}, u32[]{:S(2)}, u32[]{:S(2)}) collective-permute-start(bf16[128,3712]{1,0:T(8,128)(2,1)S(1)} %get-tuple-element.61.refs_0_), channel_id=1, source_target_pairs={{0,4},{1,5},{2,6},{3,7},{4,0},{5,1},{6,2},{7,3},{8,12},{9,13},{10,... | collective-permute-start | bytes 2850824 | tf_op jit(solution)/shard_map/ppermute | solution.py:511
  35.1 49.9 %copy-start.10 = (s32[3]{0:T(128)S(1)}, s32[3]{0:T(128)}, u32[]{:S(2)}) copy-start(s32[3]{0:T(128)} %pad_add_fusion.place_ref) | copy-start | bytes 40
  35.1 24.8 %collective-permute-start.10 = (bf16[1792,256]{1,0:T(8,128)(2,1)}, bf16[1792,256]{1,0:T(8,128)(2,1)S(1)}, u32[]{:S(2)}, u32[]{:S(2)}) collective-permute-start(bf16[1792,256]{1,0:T(8,128)(2,1)} %collective-permute-done.7.refs_6_), channel_id=1, source_target_pairs={{0,16},{16,0},{1,17},{17,1},{2,18},{18,2},{3,19},{19,3},{4,20},{20... | collective-permute-start | bytes 2752520 | tf_op jit(solution)/shard_map/ppermute | solution.py:523
  36.9 23.0 %collective-permute-start.11 = (bf16[1792,256]{1,0:T(8,128)(2,1)}, bf16[1792,256]{1,0:T(8,128)(2,1)S(1)}, u32[]{:S(2)}, u32[]{:S(2)}) collective-permute-start(bf16[1792,256]{1,0:T(8,128)(2,1)} %get-tuple-element.67), channel_id=1, source_target_pairs={{0,2},{1,3},{2,0},{3,1},{4,6},{5,7},{6,4},{7,5},{8,10},{9,11},{10,... | collective-permute-start | bytes 2752520 | tf_op jit(solution)/shard_map/ppermute | solution.py:511
  38.4 21.5 %collective-permute-start.12 = (bf16[1792,256]{1,0:T(8,128)(2,1)}, bf16[1792,256]{1,0:T(8,128)(2,1)S(1)}, u32[]{:S(2)}, u32[]{:S(2)}) collective-permute-start(bf16[1792,256]{1,0:T(8,128)(2,1)} %collective-permute-done.7.refs_6_), channel_id=1, source_target_pairs={{0,1},{1,0},{2,3},{3,2},{4,5},{5,4},{6,7},{7,6},{8,9},{9,8},{10,11... | collective-permute-start | bytes 2752520 | tf_op jit(solution)/shard_map/ppermute | solution.py:511
  40.4 40.5 %collective-permute-start.6 = (bf16[128,3712]{1,0:T(8,128)(2,1)}, bf16[128,3712]{1,0:T(8,128)(2,1)S(1)}, u32[]{:S(2)}, u32[]{:S(2)}) collective-permute-start(bf16[128,3712]{1,0:T(8,128)(2,1)} %collective-permute-done.5.refs_2_.refs_3_), channel_id=1, source_target_pairs={{0,4},{1,5},{2,6},{3,7},{4,0},{5,1},{6,2},{7,3},{8,12},{9,13},{10,... | collective-permute-start | bytes 2850824 | tf_op jit(solution)/shard_map/ppermute | solution.py:511
  59.9 6.9 %copy-start.15 = (bf16[1792,256]{1,0:T(8,128)(2,1)}, bf16[1792,256]{1,0:T(8,128)(2,1)S(1)}, u32[]{:S(2)}) copy-start(bf16[1792,256]{1,0:T(8,128)(2,1)S(1)} %collective-permute-done.10.refs_7_) | copy-start | bytes 2752516
  59.9 6.9 %copy-start.16 = (bf16[1792,256]{1,0:T(8,128)(2,1)}, bf16[1792,256]{1,0:T(8,128)(2,1)S(1)}, u32[]{:S(2)}) copy-start(bf16[1792,256]{1,0:T(8,128)(2,1)S(1)} %collective-permute-done.11.refs_12_) | copy-start | bytes 2752516
  59.9 1.0 copy-start.17
  60.9 21.5 %collective-permute-start.13 = (bf16[1792,256]{1,0:T(8,128)(2,1)S(1)}, bf16[1792,256]{1,0:T(8,128)(2,1)S(1)}, u32[]{:S(2)}, u32[]{:S(2)}) collective-permute-start(bf16[1792,256]{1,0:T(8,128)(2,1)S(1)} %collective-permute-done.11.refs_12_), channel_id=1, source_target_pairs={{0,16},{16,0},{1,17},{17,1},{2,18},{18,2},{3,19},{19,3},{4,20},{20... | collective-permute-start | bytes 2752520 | tf_op jit(solution)/shard_map/ppermute | solution.py:523
  62.5 21.5 %collective-permute-start.14 = (bf16[512,896]{1,0:T(8,128)(2,1)}, bf16[512,896]{1,0:T(8,128)(2,1)S(1)}, u32[]{:S(2)}, u32[]{:S(2)}) collective-permute-start(bf16[512,896]{1,0:T(8,128)(2,1)} %copy-done.14), channel_id=1, source_target_pairs={{0,2},{1,3},{2,0},{3,1},{4,6},{5,7},{6,4},{7,5},{8,10},{9,11},{10,... | collective-permute-start | bytes 2752520 | tf_op jit(solution)/shard_map/ppermute | solution.py:511
  63.0 20.9 %collective-permute-start.15 = (bf16[1792,256]{1,0:T(8,128)(2,1)S(1)}, bf16[1792,256]{1,0:T(8,128)(2,1)S(1)}, u32[]{:S(2)}, u32[]{:S(2)}) collective-permute-start(bf16[1792,256]{1,0:T(8,128)(2,1)S(1)} %collective-permute-done.10.refs_7_), channel_id=1, source_target_pairs={{0,1},{1,0},{2,3},{3,2},{4,5},{5,4},{6,7},{7,6},{8,9},{9,8},{10,11... | collective-permute-start | bytes 2752520 | tf_op jit(solution)/shard_map/ppermute | solution.py:511
  63.0 3.9 %copy-start.3 = (bf16[128,3712]{1,0:T(8,128)(2,1)}, bf16[128,3712]{1,0:T(8,128)(2,1)S(1)}, u32[]{:S(2)}) copy-start(bf16[128,3712]{1,0:T(8,128)(2,1)S(1)} %collective-permute-done.4.refs_1_) | copy-start | bytes 2850820
  63.0 20.9 %collective-permute-start.16 = (bf16[1792,256]{1,0:T(8,128)(2,1)S(1)}, bf16[1792,256]{1,0:T(8,128)(2,1)S(1)}, u32[]{:S(2)}, u32[]{:S(2)}) collective-permute-start(bf16[1792,256]{1,0:T(8,128)(2,1)S(1)} %collective-permute-done.11.refs_12_), channel_id=1, source_target_pairs={{0,1},{1,0},{2,3},{3,2},{4,5},{5,4},{6,7},{7,6},{8,9},{9,8},{10,11... | collective-permute-start | bytes 2752520 | tf_op jit(solution)/shard_map/ppermute | solution.py:511
  66.9 21.7 %copy-start.7 = (bf16[128,576]{1,0:T(8,128)(2,1)}, bf16[128,576]{1,0:T(8,128)(2,1)S(1)}, u32[]{:S(2)}) copy-start(bf16[128,576]{1,0:T(8,128)(2,1)S(1)} %get-tuple-element.100) | copy-start | bytes 442372
  80.9 11.7 %copy-start.1 = (bf16[128,3712]{1,0:T(8,128)(2,1)}, bf16[128,3712]{1,0:T(8,128)(2,1)S(1)}, u32[]{:S(2)}) copy-start(bf16[128,3712]{1,0:T(8,128)(2,1)S(1)} %collective-permute-done.6.refs_2_.refs_0_) | copy-start | bytes 2850820
  82.5 7.8 %copy-start.18 = (bf16[1792,256]{1,0:T(8,128)(2,1)}, bf16[1792,256]{1,0:T(8,128)(2,1)S(1)}, u32[]{:S(2)}) copy-start(bf16[1792,256]{1,0:T(8,128)(2,1)S(1)} %collective-permute-done.13.refs_13_) | copy-start | bytes 2752516
  83.9 6.4 %copy-start.19 = (bf16[1792,256]{1,0:T(8,128)(2,1)}, bf16[1792,256]{1,0:T(8,128)(2,1)S(1)}, u32[]{:S(2)}) copy-start(bf16[1792,256]{1,0:T(8,128)(2,1)S(1)} %collective-permute-done.15.refs_9_) | copy-start | bytes 2752516
  83.9 6.4 %copy-start.20 = (bf16[1792,256]{1,0:T(8,128)(2,1)}, bf16[1792,256]{1,0:T(8,128)(2,1)S(1)}, u32[]{:S(2)}) copy-start(bf16[1792,256]{1,0:T(8,128)(2,1)S(1)} %collective-permute-done.16.refs_14_) | copy-start | bytes 2752516
  83.9 6.4 %collective-permute-start.17 = (bf16[1792,256]{1,0:T(8,128)(2,1)S(1)}, bf16[1792,256]{1,0:T(8,128)(2,1)S(1)}, u32[]{:S(2)}, u32[]{:S(2)}) collective-permute-start(bf16[1792,256]{1,0:T(8,128)(2,1)S(1)} %collective-permute-done.13.refs_13_), channel_id=1, source_target_pairs={{0,1},{1,0},{2,3},{3,2},{4,5},{5,4},{6,7},{7,6},{8,9},{9,8},{10,11... | collective-permute-start | bytes 2752520 | tf_op jit(solution)/shard_map/ppermute | solution.py:511
  84.0 23.3 %collective-permute-start.21 = (bf16[512,896]{1,0:T(8,128)(2,1)S(1)}, bf16[512,896]{1,0:T(8,128)(2,1)S(1)}, u32[]{:S(2)}, u32[]{:S(2)}) collective-permute-start(bf16[512,896]{1,0:T(8,128)(2,1)S(1)} %collective-permute-done.14.refs_2_), channel_id=1, source_target_pairs={{0,1},{1,0},{2,3},{3,2},{4,5},{5,4},{6,7},{7,6},{8,9},{9,8},{10,11... | collective-permute-start | bytes 2752520 | tf_op jit(solution)/shard_map/ppermute | solution.py:511
  84.5 22.9 %collective-permute-start.22 = (bf16[512,896]{1,0:T(8,128)(2,1)S(1)}, bf16[512,896]{1,0:T(8,128)(2,1)}, u32[]{:S(2)}, u32[]{:S(2)}) collective-permute-start(bf16[512,896]{1,0:T(8,128)(2,1)S(1)} %collective-permute-done.14.refs_2_), channel_id=1, source_target_pairs={{0,16},{16,0},{1,17},{17,1},{2,18},{18,2},{3,19},{19,3},{4,20},{20... | collective-permute-start | bytes 2752520 | tf_op jit(solution)/shard_map/ppermute | solution.py:523
  87.2 20.1 %collective-permute-start.19 = (bf16[128,576]{1,0:T(8,128)(2,1)S(1)}, bf16[128,576]{1,0:T(8,128)(2,1)S(1)}, u32[]{:S(2)}, u32[]{:S(2)}) collective-permute-start(bf16[128,576]{1,0:T(8,128)(2,1)S(1)} %latent_parts.3), channel_id=1, source_target_pairs={{0,8},{1,9},{2,10},{3,11},{4,12},{5,13},{6,14},{7,15},{8,0},{9,1},... | collective-permute-start | bytes 442376 | tf_op jit(solution)/shard_map/ppermute | solution.py:511
  88.6 18.8 %collective-permute-start.18 = (bf16[128,576]{1,0:T(8,128)(2,1)}, bf16[128,576]{1,0:T(8,128)(2,1)S(1)}, u32[]{:S(2)}, u32[]{:S(2)}) collective-permute-start(bf16[128,576]{1,0:T(8,128)(2,1)} %get-tuple-element.86), channel_id=1, source_target_pairs={{0,4},{1,5},{2,6},{3,7},{4,0},{5,1},{6,2},{7,3},{8,12},{9,13},{10,... | collective-permute-start | bytes 442376 | tf_op jit(solution)/shard_map/ppermute | solution.py:511
  90.3 0.9 copy-start.21
  91.2 16.1 %collective-permute-start.20 = (bf16[128,576]{1,0:T(8,128)(2,1)}, bf16[128,576]{1,0:T(8,128)(2,1)}, u32[]{:S(2)}, u32[]{:S(2)}) collective-permute-start(bf16[128,576]{1,0:T(8,128)(2,1)} %get-tuple-element.87), channel_id=1, source_target_pairs={{0,12},{1,13},{2,14},{3,15},{4,8},{5,9},{6,10},{7,11},{8,4},{9,5},... | collective-permute-start | bytes 442376 | tf_op jit(solution)/shard_map/ppermute | solution.py:511
  92.6 0.7 copy-start.11
  93.3 14.2 %copy-start.24 = (s32[128]{0:T(128)S(1)}, s32[128]{0:T(128)}, u32[]{:S(2)}) copy-start(s32[128]{0:T(128)} %multiply_add_fusion) | copy-start | bytes 1540
  93.3 14.3 %copy-start.8 = (bf16[128,576]{1,0:T(8,128)(2,1)S(1)}, bf16[128,576]{1,0:T(8,128)(2,1)}, u32[]{:S(2)}) copy-start(bf16[128,576]{1,0:T(8,128)(2,1)} %copy-done.7) | copy-start | bytes 442372
  93.3 16.9 %copy-start = (bf16[1024,896]{1,0:T(8,128)(2,1)S(1)}, bf16[1024,896]{1,0:T(8,128)(2,1)}, u32[]{:S(2)}) copy-start(bf16[1024,896]{1,0:T(8,128)(2,1)} %refs_0_.2) | copy-start | bytes 5505028
  107.4 2.7 %collective-permute-start.23 = (bf16[512,896]{1,0:T(8,128)(2,1)}, bf16[512,896]{1,0:T(8,128)(2,1)S(1)}, u32[]{:S(2)}, u32[]{:S(2)}) collective-permute-start(bf16[512,896]{1,0:T(8,128)(2,1)} %collective-permute-done.22.refs_3_), channel_id=1, source_target_pairs={{0,1},{1,0},{2,3},{3,2},{4,5},{5,4},{6,7},{7,6},{8,9},{9,8},{10,11... | collective-permute-start | bytes 2752520 | tf_op jit(solution)/shard_map/ppermute | solution.py:511
  107.5 18.1 %collective-permute-start.25 = (bf16[128,1792]{1,0:T(8,128)(2,1)}, bf16[128,1792]{1,0:T(8,128)(2,1)}, u32[]{:S(2)}, u32[]{:S(2)}) collective-permute-start(bf16[128,1792]{1,0:T(8,128)(2,1)} %get-tuple-element.97), channel_id=1, source_target_pairs={{0,4},{1,5},{2,6},{3,7},{4,0},{5,1},{6,2},{7,3},{8,12},{9,13},{10,... | collective-permute-start | bytes 1376264 | tf_op jit(solution)/shard_map/ppermute | solution.py:511
  110.1 9.5 %copy-start.22 = (f32[512]{0:T(512)S(1)}, f32[512]{0:T(512)}, u32[]{:S(2)}) copy-start(f32[512]{0:T(512)} %param.13) | copy-start | bytes 6148
  116.8 1.0 copy-start.5
  117.8 0.9 copy-start.12
  118.7 14.7 %collective-permute-start.24 = (bf16[128,1792]{1,0:T(8,128)(2,1)S(1)}, bf16[128,1792]{1,0:T(8,128)(2,1)S(1)}, u32[]{:S(2)}, u32[]{:S(2)}) collective-permute-start(bf16[128,1792]{1,0:T(8,128)(2,1)S(1)} %get-tuple-element.96), channel_id=1, source_target_pairs={{0,4},{1,5},{2,6},{3,7},{4,0},{5,1},{6,2},{7,3},{8,12},{9,13},{10,... | collective-permute-start | bytes 1376264 | tf_op jit(solution)/shard_map/ppermute | solution.py:511
  121.0 17.3 %copy-start.13 = (bf16[128,3584]{1,0:T(8,128)(2,1)S(1)}, bf16[128,3584]{1,0:T(8,128)(2,1)}, u32[]{:S(2)}) copy-start(bf16[128,3584]{1,0:T(8,128)(2,1)} %copy-done.12) | copy-start | bytes 2752516
  121.1 14.8 %collective-permute-start.26 = (bf16[4,16,576]{2,1,0:T(8,128)(2,1)S(1)}, bf16[4,16,576]{2,1,0:T(8,128)(2,1)S(1)}, u32[]{:S(2)}, u32[]{:S(2)}) collective-permute-start(bf16[4,16,576]{2,1,0:T(8,128)(2,1)S(1)} %get-tuple-element.122), channel_id=1, source_target_pairs={{0,4},{1,5},{2,6},{3,7},{4,0},{5,1},{6,2},{7,3},{8,12},{9,13},{10,... | collective-permute-start | bytes 221192 | tf_op jit(solution)/shard_map/ppermute | solution.py:511
  122.2 13.6 %collective-permute-start.27 = (bf16[4,16,576]{2,1,0:T(8,128)(2,1)S(1)}, bf16[4,16,576]{2,1,0:T(8,128)(2,1)S(1)}, u32[]{:S(2)}, u32[]{:S(2)}) collective-permute-start(bf16[4,16,576]{2,1,0:T(8,128)(2,1)S(1)} %get-tuple-element.121), channel_id=1, source_target_pairs={{0,8},{1,9},{2,10},{3,11},{4,12},{5,13},{6,14},{7,15},{8,0},{9,1},... | collective-permute-start | bytes 221192 | tf_op jit(solution)/shard_map/ppermute | solution.py:511
  124.2 14.1 %collective-permute-start.28 = (bf16[4,16,576]{2,1,0:T(8,128)(2,1)S(1)}, bf16[4,16,576]{2,1,0:T(8,128)(2,1)}, u32[]{:S(2)}, u32[]{:S(2)}) collective-permute-start(bf16[4,16,576]{2,1,0:T(8,128)(2,1)S(1)} %get-tuple-element.120), channel_id=1, source_target_pairs={{0,12},{1,13},{2,14},{3,15},{4,8},{5,9},{6,10},{7,11},{8,4},{9,5},... | collective-permute-start | bytes 221192 | tf_op jit(solution)/shard_map/ppermute | solution.py:511
  138.3 42.2 %collective-permute-start.29 = (bf16[128,3584]{1,0:T(8,128)(2,1)S(1)}, bf16[128,3584]{1,0:T(8,128)(2,1)S(1)}, u32[]{:S(2)}, u32[]{:S(2)}) collective-permute-start(bf16[128,3584]{1,0:T(8,128)(2,1)S(1)} %copy-done.13), channel_id=1, source_target_pairs={{0,4},{1,5},{2,6},{3,7},{4,0},{5,1},{6,2},{7,3},{8,12},{9,13},{10,... | collective-permute-start | bytes 2752520 | tf_op jit(solution)/shard_map/ppermute | solution.py:511
  138.3 42.2 %collective-permute-start.30 = (bf16[128,3584]{1,0:T(8,128)(2,1)}, bf16[128,3584]{1,0:T(8,128)(2,1)}, u32[]{:S(2)}, u32[]{:S(2)}) collective-permute-start(bf16[128,3584]{1,0:T(8,128)(2,1)} %add_convert_fusion.1), channel_id=1, source_target_pairs={{0,12},{1,13},{2,14},{3,15},{4,8},{5,9},{6,10},{7,11},{8,4},{9,5},... | collective-permute-start | bytes 2752520 | tf_op jit(solution)/shard_map/ppermute | solution.py:511
  139.7 40.9 %copy-start.6 = (bf16[128,3584]{1,0:T(8,128)(2,1)S(1)}, bf16[128,3584]{1,0:T(8,128)(2,1)}, u32[]{:S(2)}) copy-start(bf16[128,3584]{1,0:T(8,128)(2,1)} %copy-done.5) | copy-start | bytes 2752516
  140.8 6.2 %collective-permute-start.31 = (bf16[4,2,16,576]{3,2,0,1:T(8,128)(2,1)S(1)}, bf16[4,2,16,576]{3,2,0,1:T(8,128)(2,1)S(1)}, u32[]{:S(2)}, u32[]{:S(2)}) collective-permute-start(bf16[4,2,16,576]{3,2,0,1:T(8,128)(2,1)S(1)} %get-tuple-element.118), channel_id=1, source_target_pairs={{0,2},{1,3},{2,0},{3,1},{4,6},{5,7},{6,4},{7,5},{8,10},{9,11},{10,... | collective-permute-start | bytes 442376 | tf_op jit(solution)/shard_map/ppermute | solution.py:511
  147.1 1.5 collective-permute-start.32
